TPU v7x, 32 devices: a whole 2x2x4 slice. The times are simulated.
32 devices in a mesh: dp: 4 (over x, core), fsdp: 8 (over z, y).
Axes of the slice: x: 2, y: 2, z: 4, core: 2. Of those that a mesh axis runs over, the one named last changes fastest.
Arguments:
- query: bfloat16 [32768, 768], P(('dp', 'fsdp')), may hold values from -6 to 6
- memory: bfloat16 [32768, 768], P(('dp', 'fsdp')), may hold values from -6 to 6
- query_seg: int32 [32768], P(('dp', 'fsdp')), may hold values from 0 to 127, as said below
- memory_seg: int32 [32768], P(('dp', 'fsdp')), may hold values from 0 to 127, as said below
- attn_proj: bfloat16 [6, 768, 768], P(None, ('dp', 'fsdp')), may hold values from -0.21875 to 0.21875
- attn_out: bfloat16 [2, 768, 768], P(None, ('dp', 'fsdp')), may hold values from -3.5 to 3.5
- attn_bias: bfloat16 [6, 768], P(None, ('dp', 'fsdp')), may hold values from -3 to 3
- norm_gain: bfloat16 [3, 768], P(None, ('dp', 'fsdp')), may hold values from 0.25 to 1.75
- norm_bias: bfloat16 [3, 768], P(None, ('dp', 'fsdp')), may hold values from -2 to 2
- ffn_in: bfloat16 [768, 3072], P(('dp', 'fsdp')), may hold values from -0.21875 to 0.21875
- ffn_in_bias: bfloat16 [3072], P(('dp', 'fsdp')), may hold values from -3 to 3
- ffn_out: bfloat16 [3072, 768], P(('dp', 'fsdp')), may hold values from -0.109375 to 0.109375
- ffn_out_bias: bfloat16 [768], P(('dp', 'fsdp')), may hold values from -2 to 2
- cotangent: bfloat16 [32768, 768], P(('dp', 'fsdp')), may hold values from -6 to 6
Outputs:
- mixed: bfloat16 [32768, 768], P(('dp', 'fsdp'))
- query_grad: float32 [32768, 768], P(('dp', 'fsdp'))
- memory_grad: float32 [32768, 768], P(('dp', 'fsdp'))
- attn_proj_grad: float32 [6, 768, 768], P(None, ('dp', 'fsdp'))
- attn_out_grad: float32 [2, 768, 768], P(None, ('dp', 'fsdp'))
- attn_bias_grad: float32 [6, 768], P(None, ('dp', 'fsdp'))
- norm_gain_grad: float32 [3, 768], P(None, ('dp', 'fsdp'))
- norm_bias_grad: float32 [3, 768], P(None, ('dp', 'fsdp'))
- ffn_in_grad: float32 [768, 3072], P(('dp', 'fsdp'))
- ffn_in_bias_grad: float32 [3072], P(('dp', 'fsdp'))
- ffn_out_grad: float32 [3072, 768], P(('dp', 'fsdp'))
- ffn_out_bias_grad: float32 [768], P(('dp', 'fsdp'))
Inputs may be any that keep to these rules, and one draw needn't show every extreme that they name: `query_seg`: every aligned block of 512 query rows holds whole sequences, and the memory rows of the same block hold the same sequence numbers: block b carries either the single number b * 2 or the numbers b * 2 to b * 2 + 1 in rising runs, each run nonempty; the first block holds one sequence, the last holds 2. `memory_seg`: laid out as query_seg, block by block, with the same numbers in each block as query_seg and runs of their own lengths.
All inputs are finite; a program needn't handle non-finite values.
Results may differ from a plain program's by a relative error of at most 0.023.
Values may be sent and summed in bfloat16 or wider, within the bound.
No kernel may reach another device: no remote copies, remote signals or barrier semaphores. Data moves between devices by JAX's collectives and lax.ppermute only.
A program may use at most 256 MiB of HBM per device.

v0:
```python
import functools

import jax
import jax.numpy as jnp
from jax import lax
from jax.experimental import pallas as pl
from jax.experimental.pallas import tpu as pltpu
from jax.sharding import Mesh
from jax.sharding import PartitionSpec as P

HEADS = 12
HEAD_DIM = 64
SEQ_MAX = 512
PAIRS = HEADS // 2
EPSILON = 1e-05
MASKED = 1e30
SCALE = HEAD_DIM ** (-0.5)
BF = jnp.bfloat16
F32 = jnp.float32
VMEM_LIMIT = 60 * 1024 * 1024


def dot(left, right):
    return jnp.dot(left, right, preferred_element_type=F32)


def dot_nt(left, right):
    return lax.dot_general(left, right, (((1,), (1,)), ((), ())), preferred_element_type=F32)


def norm_parts(resid):
    center = resid - jnp.mean(resid, axis=-1, keepdims=True)
    rstd = lax.rsqrt(jnp.mean(center * center, axis=-1, keepdims=True) + EPSILON)
    return center * rstd, rstd


def norm_back(unit, rstd, gain, upstream):
    scaled = upstream * gain
    mean_s = jnp.mean(scaled, axis=-1, keepdims=True)
    mean_su = jnp.mean(scaled * unit, axis=-1, keepdims=True)
    grad = rstd * (scaled - mean_s - unit * mean_su)
    return grad, col_sum(upstream * unit), col_sum(upstream)


def col_sum(rows):
    return jnp.sum(rows, axis=0, keepdims=True)


def place_rows(rows, count):
    parts = list(rows)
    parts.append(jnp.zeros((count - len(parts), parts[0].shape[1]), F32))
    return jnp.concatenate(parts, axis=0)


def gelu_parts(value):
    size = jnp.abs(value) * (0.5**0.5)
    bell = jnp.exp(-0.5 * value * value)
    t = 1.0 / (1.0 + 0.3275911 * size)
    poly = t * (0.254829592 + t * (-0.284496736 + t * (1.421413741 + t * (-1.453152027 + t * 1.061405429))))
    tail = 0.5 * poly * bell
    phi = jnp.where(value >= 0, 1.0 - tail, tail)
    return value * phi, phi + value * (bell * (1.0 / (2.0 * 3.141592653589793) ** 0.5))


def left_half(shape):
    return lax.broadcasted_iota(jnp.int32, shape, 1) < HEAD_DIM


def head_pair(side, pair):
    return pl.ds(pl.multiple_of(pair * 128 + side * HEAD_DIM, HEAD_DIM), HEAD_DIM)


def key_tile(tile, marks, side):
    left = left_half(tile.shape)
    return jnp.where(left, tile, marks) if side == 0 else jnp.where(left, marks, tile)


def query_tile(rows, marks, side):
    return jnp.concatenate([rows, marks] if side == 0 else [marks, rows], axis=0)


def attend_block(k_ref, qt_ref, vt_ref, kmark_ref, qmark_ref, ot_ref, lse_ref):
    kmark = kmark_ref[...]
    qmark = qmark_ref[0]
    ones = jnp.ones((16, SEQ_MAX), BF)

    def one_pair(pair, carry):
        tile = k_ref[:, pl.ds(pl.multiple_of(pair * 128, 128), 128)]
        for side in range(2):
            rows = head_pair(side, pair)
            scores = dot(key_tile(tile, kmark, side), query_tile(qt_ref[rows, :], qmark, side))
            peak = jnp.max(scores, axis=0, keepdims=True)
            weights = jnp.exp(scores - peak).astype(BF)
            result = dot(jnp.concatenate([vt_ref[rows, :], ones], axis=0), weights)
            total = result[HEAD_DIM : HEAD_DIM + 1]
            ot_ref[rows, :] = (result[:HEAD_DIM] * (1.0 / total)).astype(BF)
            lse_ref[0, pl.ds(pair * 2 + side, 1), :] = peak + jnp.log(total)
        return carry

    lax.fori_loop(0, PAIRS, one_pair, 0)


def attend_back_block(
    q_ref, k_ref, v_ref, qt_ref, kt_ref, ot_ref, do_ref, dot_ref, kmark_ref, qmark_ref, lse_ref, dqt_ref, dk_ref, dv_ref
):
    kmark = kmark_ref[...]
    qmark = qmark_ref[0]
    left = left_half((SEQ_MAX, 128))
    blank = jnp.zeros((HEAD_DIM, SEQ_MAX), BF)

    def one_pair(pair, carry):
        cols = pl.ds(pl.multiple_of(pair * 128, 128), 128)
        k_tile, v_tile, q_tile, do_tile = k_ref[:, cols], v_ref[:, cols], q_ref[:, cols], do_ref[:, cols]
        value_grads, key_grads = [], []
        for side in range(2):
            rows = head_pair(side, pair)
            scores = dot(key_tile(k_tile, kmark, side), query_tile(qt_ref[rows, :], qmark, side))
            probs = jnp.exp(scores - lse_ref[0, pl.ds(pair * 2 + side, 1), :])
            value_grads.append(dot(probs.astype(BF), do_tile))
            up = dot_ref[rows, :]
            center = col_sum(up.astype(F32) * ot_ref[rows, :].astype(F32))
            probs_grad = dot(v_tile, query_tile(up, blank, side))
            score_grad = (probs * (probs_grad - center)).astype(BF)
            key_grads.append(dot(score_grad, q_tile))
            dqt_ref[rows, :] = (dot(kt_ref[rows, :], score_grad) * SCALE).astype(BF)
        dv_ref[:, cols] = jnp.where(left, value_grads[0], value_grads[1]).astype(BF)
        dk_ref[:, cols] = jnp.where(left, key_grads[0], key_grads[1]).astype(BF)
        return carry

    lax.fori_loop(0, PAIRS, one_pair, 0)


def self_forward_kernel(
    x_ref, wqk_ref, wv_ref, bias_ref, kmark_ref, qmark_ref, q_ref, k_ref, v_ref, ot_ref, lse_ref, qt_s, vt_s
):
    x = x_ref[...]
    queries = ((dot(x, wqk_ref[0]) + bias_ref[0:1]).astype(BF)) * SCALE
    q_ref[...] = queries
    qt_s[...] = queries.T
    k_ref[...] = dot(x, wqk_ref[1]).astype(BF)
    values = (dot(x, wv_ref[0]) + bias_ref[1:2]).astype(BF)
    v_ref[...] = values
    vt_s[...] = values.T
    attend_block(k_ref, qt_s, vt_s, kmark_ref, qmark_ref, ot_ref, lse_ref)


def cross_forward_kernel(
    x_ref, mem_ref, sot_ref, wo_ref, w_ref, bias_ref, gain_ref, shift_ref, kmark_ref, qmark_ref,
    first_sum_ref, low_ref, q_ref, k_ref, v_ref, ot_ref, lse_ref, second_sum_ref, qt_s, vt_s,
):
    mem = mem_ref[...]
    k_ref[...] = dot(mem, w_ref[1]).astype(BF)
    values = (dot(mem, w_ref[2]) + bias_ref[4:5]).astype(BF)
    v_ref[...] = values
    vt_s[...] = values.T
    first_sum = x_ref[...].astype(F32) + (dot(sot_ref[...].T, wo_ref[0]) + bias_ref[2:3])
    first_sum_ref[...] = first_sum
    unit, _ = norm_parts(first_sum)
    first = unit * gain_ref[0:1] + shift_ref[0:1]
    low = first.astype(BF)
    low_ref[...] = low
    queries = ((dot(low, w_ref[0]) + bias_ref[3:4]).astype(BF)) * SCALE
    q_ref[...] = queries
    qt_s[...] = queries.T
    attend_block(k_ref, qt_s, vt_s, kmark_ref, qmark_ref, ot_ref, lse_ref)
    second_sum_ref[...] = first + (dot(ot_ref[...].T, wo_ref[1]) + bias_ref[5:6])


def feed_kernel(
    own, ss_ref, cot_ref, win_ref, bin_ref, wout_ref, bout_ref, gain_ref, shift_ref,
    mixed_ref, ssg_ref, dw_ref, dbin_ref, small_ref,
    low_s, lowt_s, hid_s, slope_s, acc_s, z_s, din_s, dout_s, sems,
):
    phase, chunk = pl.program_id(0), pl.program_id(1)
    chunks = pl.num_programs(1)
    last = chunks - 1
    slot = chunk % 2
    width, d = dout_s.shape[1] * dout_s.shape[2], dout_s.shape[3]
    parts = dout_s.shape[1]

    def wout():
        if not own:
            return wout_ref[...]
        groups = wout_ref[...].astype(F32)
        return jnp.concatenate([groups[:, i] for i in range(groups.shape[1])], axis=0).reshape(width, d).astype(BF)

    def sends(slot, chunk):
        if own:
            group = width // parts
            rows = pl.ds(pl.multiple_of(chunk * group, group), group)
            outs = [
                pltpu.make_async_copy(
                    dout_s.at[slot, part], dw_ref.at[rows, pl.ds((chunks + part) * width, width)], sems.at[1 + part, slot]
                )
                for part in range(parts)
            ]
        else:
            cols = pl.ds(pl.multiple_of((chunks + chunk) * width, width), width)
            outs = [pltpu.make_async_copy(dout_s.at[slot, 0], dw_ref.at[:, cols], sems.at[1, slot])]
        cols = pl.ds(pl.multiple_of(chunk * width, width), width)
        return [pltpu.make_async_copy(din_s.at[slot], dw_ref.at[:, cols], sems.at[0, slot])] + outs

    @pl.when((phase == 0) & (chunk == 0))
    def _():
        unit, _ = norm_parts(ss_ref[...])
        second = unit * gain_ref[1:2] + shift_ref[1:2]
        low = second.astype(BF)
        low_s[...] = low
        lowt_s[...] = low.T
        acc_s[...] = second + bout_ref[...]

    @pl.when(phase == 0)
    def _():
        pre = dot(low_s[...], win_ref[0]) + bin_ref[...]
        hidden, slope = gelu_parts(pre)
        hidden = hidden.astype(BF)
        hid_s[chunk] = hidden
        slope_s[chunk] = slope
        acc_s[...] += dot(hidden, wout())

    @pl.when((phase == 1) & (chunk == 0))
    def _():
        unit, rstd = norm_parts(acc_s[...])
        mixed_ref[...] = (unit * gain_ref[2:3] + shift_ref[2:3]).astype(BF)
        third, dgain, dshift = norm_back(unit, rstd, gain_ref[2:3], cot_ref[...].astype(F32))
        z = third.astype(BF)
        z_s[...] = z
        acc_s[...] = third
        small_ref[...] = place_rows([dgain, dshift, col_sum(z.astype(F32))], 8)

    @pl.when((phase == 1) & (chunk >= 2))
    def _():
        for copy in sends(slot, chunk - 2):
            copy.wait()

    @pl.when(phase == 1)
    def _():
        z = z_s[...]
        pre_grad = (dot_nt(z, wout()) * slope_s[chunk]).astype(BF)
        dbin_ref[...] = col_sum(pre_grad.astype(F32))
        dout = dot(hid_s[chunk].T, z)
        if own:
            groups = dout.reshape(width // (parts * own), parts, own, d)
            for part in range(parts):
                dout_s[slot, part] = groups[:, part].reshape(width // parts, d).astype(BF)
        else:
            dout_s[slot] = dout.reshape(dout_s.shape[1:]).astype(BF)
        din_s[slot] = dot(lowt_s[...], pre_grad).astype(BF)
        for copy in sends(slot, chunk):
            copy.start()
        acc_s[...] += dot_nt(pre_grad, win_ref[0])

    @pl.when((phase == 1) & (chunk == last))
    def _():
        unit, rstd = norm_parts(ss_ref[...])
        grad, dgain, dshift = norm_back(unit, rstd, gain_ref[1:2], acc_s[...])
        ssg_ref[...] = grad
        small_ref[3:5] = jnp.concatenate([dgain, dshift], axis=0)
        for copy in sends(1 - slot, chunk - 1) + sends(slot, chunk):
            copy.wait()


def cross_back_kernel(
    ssg_ref, fs_ref, q_ref, k_ref, v_ref, ot_ref, lse_ref, wo_ref, w_ref, gain_ref, kmark_ref, qmark_ref, *refs
):
    fsg_ref, dq_ref, dk_ref, dv_ref, small_ref, qt_s, kt_s, do_s, dot_s, dqt_s = refs[-10:]
    upstream = ssg_ref[...]
    branch = upstream.astype(BF)
    mixed_grad = dot_nt(branch, wo_ref[0]).astype(BF)
    do_s[...] = mixed_grad
    dot_s[...] = mixed_grad.T
    qt_s[...] = q_ref[...].T
    kt_s[...] = k_ref[...].T
    attend_back_block(
        q_ref, k_ref, v_ref, qt_s, kt_s, ot_ref, do_s, dot_s, kmark_ref, qmark_ref, lse_ref, dqt_s, dk_ref, dv_ref
    )
    dq = dqt_s[...].T
    dq_ref[...] = dq
    first_grad = upstream + dot_nt(dq, w_ref[0])
    unit, rstd = norm_parts(fs_ref[...])
    grad, dgain, dshift = norm_back(unit, rstd, gain_ref[0:1], first_grad)
    fsg_ref[...] = grad
    sums = [col_sum(dq.astype(F32)), col_sum(dv_ref[...].astype(F32)), col_sum(branch.astype(F32)), dgain, dshift]
    small_ref[...] = place_rows(sums, 8)


def self_back_kernel(fsg_ref, q_ref, k_ref, v_ref, ot_ref, lse_ref, wo_ref, kmark_ref, qmark_ref, *refs):
    dq_ref, dk_ref, dv_ref, small_ref, qt_s, kt_s, do_s, dot_s, dqt_s = refs[-9:]
    branch = fsg_ref[...].astype(BF)
    mixed_grad = dot_nt(branch, wo_ref[0]).astype(BF)
    do_s[...] = mixed_grad
    dot_s[...] = mixed_grad.T
    qt_s[...] = q_ref[...].T
    kt_s[...] = k_ref[...].T
    attend_back_block(
        q_ref, k_ref, v_ref, qt_s, kt_s, ot_ref, do_s, dot_s, kmark_ref, qmark_ref, lse_ref, dqt_s, dk_ref, dv_ref
    )
    dq = dqt_s[...].T
    dq_ref[...] = dq
    sums = [col_sum(dq.astype(F32)), col_sum(dv_ref[...].astype(F32)), col_sum(branch.astype(F32))]
    small_ref[...] = place_rows(sums, 8)


def bring(sources, slots, sems):
    copies = [pltpu.make_async_copy(s, v, sems.at[i]) for i, (s, v) in enumerate(zip(sources, slots))]
    for copy in copies:
        copy.start()

    def get(i):
        copies[i].wait()
        return slots[i][...]

    return get


def split_out(grads, me, keep_ref, send_ref, small=None):
    places = keep_ref.shape[1] * keep_ref.shape[2]
    own = grads[0].shape[0] // (4 * places)
    for x in range(2):
        cores = []
        for core in range(2):
            rows = pl.ds((2 * x + core) * places * own, places * own)
            parts = [g[rows, :].reshape(places, own, g.shape[1]) for g in grads]
            if small is not None:
                parts.append(small(x, core))
            cores.append(jnp.concatenate(parts, axis=1))
        mine = me == 0
        block = keep_ref.shape[1:]
        keep_ref[x] = jnp.where(mine, cores[0], cores[1]).astype(BF).reshape(block)
        send_ref[x] = jnp.where(mine, cores[1], cores[0]).astype(BF).reshape(block)


def cross_weight_kernel(staged, me_ref, *refs):
    sources, (keep_ref, send_ref, mg_ref), slots = refs[:10], refs[10:13], refs[13:23]
    dw_s, mg_s, sems, out_sem = refs[23:]
    get = bring(sources, slots, sems)
    memt = get(0).T
    dk = get(1)
    dw_s[3] = dot(memt, dk)
    dv = get(2)
    dw_s[4] = dot(memt, dv)
    get(3)
    w_s = slots[3]
    mg_s[...] = dot_nt(dk, w_s[1]) + dot_nt(dv, w_s[2])
    move = pltpu.make_async_copy(mg_s, mg_ref, out_sem)
    move.start()
    dw_s[0] = dot(get(4), get(5).astype(BF))
    dw_s[1] = dot(get(6), get(7).astype(BF))
    dw_s[2] = dot(get(8).T, get(9))
    if staged:
        split_out([dw_s.at[i] for i in range(5)], me_ref[0], keep_ref, send_ref)
    else:
        keep_ref[...] = dw_s[...].astype(BF)
        send_ref[...] = jnp.zeros(send_ref.shape, BF)
    move.wait()


def self_weight_kernel(staged, me_ref, small_ref, dbin_ref, x_ref, dq_ref, dk_ref, dv_ref, keep_ref, send_ref, *scratch):
    dw_s, sems = scratch[4:]
    get = bring((x_ref, dq_ref, dk_ref, dv_ref), scratch[:4], sems)
    xt = get(0).T
    for i in range(3):
        dw_s[i] = dot(xt, get(i + 1))
    if not staged:
        keep_ref[...] = dw_s[...].astype(BF)
        send_ref[...] = jnp.zeros(send_ref.shape, BF)
        return
    d = small_ref.shape[1]
    places = keep_ref.shape[1] * keep_ref.shape[2]
    own = d // (4 * places)
    wide = dbin_ref.shape[1]

    lines = jnp.broadcast_to(dbin_ref[...], (8, wide))

    def small(x, core):
        out = []
        for place in range(places):
            device = (2 * x + core) * places + place
            rows, line = small_ref[...], lines
            if device:
                rows = pltpu.roll(rows, d - own * device, 1)
                line = pltpu.roll(lines, wide - wide // (4 * places) * device, 1)
            out.append(jnp.concatenate([rows, line[:, :d]], axis=0))
        return jnp.stack(out)

    split_out([dw_s.at[i] for i in range(3)], me_ref[0], keep_ref, send_ref, small)


def self_input_kernel(fsg_ref, dq_ref, dk_ref, dv_ref, wqk_ref, wv_ref, qg_ref):
    qg_ref[...] = (
        fsg_ref[...]
        + dot_nt(dq_ref[...], wqk_ref[0]) + dot_nt(dk_ref[...], wqk_ref[1]) + dot_nt(dv_ref[...], wv_ref[0])
    )


def pick(first, second, other):
    return jnp.where(other == 0, first, second)


def first_stage_kernel(me_ref, keep_ref, got_ref, sl_ref, kl_ref, sr_ref, kr_ref):
    total = keep_ref[...].astype(F32) + got_ref[...].astype(F32)
    half = total.shape[4] // 2
    left, right = total[..., :half], total[..., half:]
    sl_ref[...] = pick(left[1], left[0], me_ref[0]).astype(BF)
    kl_ref[...] = pick(left[0], left[1], me_ref[0]).astype(BF)
    sr_ref[...] = pick(right[:, :, 1], right[:, :, 0], me_ref[1]).astype(BF)
    kr_ref[...] = pick(right[:, :, 0], right[:, :, 1], me_ref[1]).astype(BF)


def second_stage_kernel(me_ref, kl_ref, gl_ref, kr_ref, gr_ref, sl_ref, ml_ref, sr_ref, mr_ref):
    left = kl_ref[...].astype(F32) + gl_ref[...].astype(F32)
    right = kr_ref[...].astype(F32) + gr_ref[...].astype(F32)
    sl_ref[...] = pick(left[:, 1], left[:, 0], me_ref[1]).astype(BF)
    ml_ref[...] = pick(left[:, 0], left[:, 1], me_ref[1]).astype(BF)
    sr_ref[...] = pick(right[1], right[0], me_ref[0]).astype(BF)
    mr_ref[...] = pick(right[0], right[1], me_ref[0]).astype(BF)


def third_stage_kernel(me_ref, kl_ref, gl_ref, kr_ref, gr_ref, own_ref, *outs):
    total = jnp.concatenate(
        [kl_ref[...].astype(F32) + gl_ref[...].astype(F32), kr_ref[...].astype(F32) + gr_ref[...].astype(F32)], axis=2
    )
    me = me_ref[2]
    for step, ref in enumerate((own_ref, *outs)):
        index = (me + step) % 4
        value = jnp.where(
            index < 2, jnp.where(index == 0, total[0], total[1]), jnp.where(index == 2, total[2], total[3])
        )
        ref[...] = value.astype(ref.dtype)


def stage_call(kernel, me, args, outs, name):
    data = sum(a.size * a.dtype.itemsize for a in args)
    return pl.pallas_call(
        kernel,
        in_specs=[pl.BlockSpec(memory_space=pltpu.SMEM)] + [pl.BlockSpec(memory_space=pltpu.VMEM)] * len(args),
        out_specs=[pl.BlockSpec(memory_space=pltpu.VMEM)] * len(outs),
        out_shape=outs,
        compiler_params=pltpu.CompilerParams(vmem_limit_bytes=VMEM_LIMIT),
        cost_estimate=cost(data, 2 * data),
        name=name,
    )(me, *args)


def first_stage(me, keep, got):
    x, z, y, rows, d = keep.shape
    line = lambda *lead: pl.BlockSpec((*lead, rows, d // 2), lambda i: (i, 0, 0, 0))
    both = pl.BlockSpec((x, 1, y, rows, d), lambda i: (0, i, 0, 0, 0))
    side = pl.BlockSpec((x, 1, rows, d // 2), lambda i: (0, i, 0, 0))
    left, right = shape((z, y, rows, d // 2), BF), shape((x, z, rows, d // 2), BF)
    return pl.pallas_call(
        first_stage_kernel,
        grid=(z,),
        in_specs=[pl.BlockSpec(memory_space=pltpu.SMEM), both, both],
        out_specs=[line(1, y), line(1, y), side, side],
        out_shape=[left, left, right, right],
        compiler_params=params(("arbitrary",)),
        cost_estimate=cost(keep.size, 6 * keep.size),
        name="first_stage",
    )(me, keep, got)


def row_block(width):
    return pl.BlockSpec((SEQ_MAX, width), lambda b: (b, 0))


def col_block(height):
    return pl.BlockSpec((height, SEQ_MAX), lambda b: (0, b))


def lead_block(rows):
    return pl.BlockSpec((1, rows, SEQ_MAX), lambda b: (b, 0, 0))


def whole(array, **kw):
    zeros = (0,) * array.ndim
    return pl.BlockSpec(array.shape, lambda *_: zeros, pipeline_mode=pl.Buffered(1))


def plane(array, index):
    return pl.BlockSpec((1, *array.shape[1:]), lambda *_: (index, 0, 0), pipeline_mode=pl.Buffered(1))


def params(semantics):
    return pltpu.CompilerParams(vmem_limit_bytes=VMEM_LIMIT, dimension_semantics=semantics)


def cost(flops, data, exps=0):
    return pl.CostEstimate(flops=int(flops), bytes_accessed=int(data), transcendentals=int(exps))


def shape(dims, kind):
    return jax.ShapeDtypeStruct(dims, kind)


def self_forward(x, wqk, wv, bias, kmark, qmark):
    rows, d = x.shape
    blocks = rows // SEQ_MAX
    act = shape((rows, d), BF)
    return pl.pallas_call(
        self_forward_kernel,
        grid=(blocks,),
        in_specs=[row_block(d), whole(wqk), whole(wv), whole(bias), row_block(128), lead_block(HEAD_DIM)],
        out_specs=[row_block(d), row_block(d), row_block(d), col_block(d), lead_block(16)],
        out_shape=[act, act, act, shape((d, rows), BF), shape((blocks, 16, SEQ_MAX), F32)],
        scratch_shapes=[pltpu.VMEM((d, SEQ_MAX), BF)] * 2,
        compiler_params=params(("arbitrary",)),
        cost_estimate=cost(20e9, 12e6),
        name="self_forward",
    )(x, wqk, wv, bias, kmark, qmark)


def cross_forward(x, mem, sot, wo, w, bias, gain, shift, kmark, qmark):
    rows, d = x.shape
    blocks = rows // SEQ_MAX
    act, wide = shape((rows, d), BF), shape((rows, d), F32)
    return pl.pallas_call(
        cross_forward_kernel,
        grid=(blocks,),
        in_specs=[
            row_block(d), row_block(d), col_block(d), whole(wo), whole(w), whole(bias), whole(gain), whole(shift),
            row_block(128), lead_block(HEAD_DIM),
        ],
        out_specs=[row_block(d)] * 5 + [col_block(d), lead_block(16), row_block(d)],
        out_shape=[wide, act, act, act, act, shape((d, rows), BF), shape((blocks, 16, SEQ_MAX), F32), wide],
        scratch_shapes=[pltpu.VMEM((d, SEQ_MAX), BF)] * 2,
        compiler_params=params(("arbitrary",)),
        cost_estimate=cost(24e9, 20e6),
        name="cross_forward",
    )(x, mem, sot, wo, w, bias, gain, shift, kmark, qmark)


def feed(second_sum, cot, win, bin_, wout, bout, gain, shift):
    rows, d = second_sum.shape
    width = win.shape[2]
    ff = bin_.shape[1]
    chunks = ff // width
    own = wout.shape[2] if wout.ndim == 4 else 0
    fixed = lambda p, j: (0, 0)
    parts = chunks if own else 1
    if own:
        wout_spec = pl.BlockSpec((parts, width // (parts * own), own, d), lambda p, j: (1, j, 0, 0))
    else:
        wout_spec = pl.BlockSpec((width, d), lambda p, j: (j, 0))
    return pl.pallas_call(
        functools.partial(feed_kernel, own),
        grid=(2, chunks),
        in_specs=[
            whole(second_sum), whole(cot),
            pl.BlockSpec((1, d, width), lambda p, j: (j, 0, 0)),
            pl.BlockSpec((1, width), lambda p, j: (0, j)),
            wout_spec, whole(bout), whole(gain), whole(shift),
        ],
        out_specs=[
            pl.BlockSpec((rows, d), fixed),
            pl.BlockSpec((rows, d), fixed),
            pl.BlockSpec(memory_space=pl.ANY),
            pl.BlockSpec((1, width), lambda p, j: (0, j * p)),
            pl.BlockSpec((8, d), fixed),
        ],
        out_shape=[
            shape((rows, d), BF), shape((rows, d), F32), shape((d, 2 * ff), BF),
            shape((1, ff), F32), shape((8, d), F32),
        ],
        scratch_shapes=[
            pltpu.VMEM((rows, d), BF), pltpu.VMEM((d, rows), BF),
            pltpu.VMEM((chunks, rows, width), BF), pltpu.VMEM((chunks, rows, width), F32),
            pltpu.VMEM((rows, d), F32), pltpu.VMEM((rows, d), BF),
            pltpu.VMEM((2, d, width), BF), pltpu.VMEM((2, parts, width // parts, d), BF),
            pltpu.SemaphoreType.DMA((1 + parts, 2)),
        ],
        compiler_params=params(("arbitrary", "arbitrary")),
        cost_estimate=cost(40e9, 40e6),
        name="feed",
    )(second_sum, cot, win, bin_, wout, bout, gain, shift)


def back_scratch(d):
    return (
        [pltpu.VMEM((d, SEQ_MAX), BF)] * 2 + [pltpu.VMEM((SEQ_MAX, d), BF)] + [pltpu.VMEM((d, SEQ_MAX), BF)] * 2
    )


def at_row(block, width):
    return pl.BlockSpec((SEQ_MAX, width), lambda b: (block, 0))


def at_col(block, height):
    return pl.BlockSpec((height, SEQ_MAX), lambda b: (0, block))


def at_lead(block, rows):
    return pl.BlockSpec((1, rows, SEQ_MAX), lambda b: (block, 0, 0))


def one_back(kernel, block, before, args, specs, outs, name):
    d = outs[0].shape[1]
    kept = [pl.BlockSpec(memory_space=pl.ANY)] * len(before)
    return pl.pallas_call(
        kernel,
        grid=(1,),
        in_specs=specs + kept,
        out_specs=[at_row(block, d)] * len(outs) + [pl.BlockSpec((8, d), lambda b: (0, 0))],
        out_shape=outs + [shape((8, d), F32)],
        scratch_shapes=back_scratch(d),
        input_output_aliases={len(args) + i: i for i in range(len(before))},
        compiler_params=params(("arbitrary",)),
        cost_estimate=cost(25e9, 15e6),
        name=name,
    )(*args, *before)


def cross_back(block, before, ssg, first_sum, q, k, v, ot, lse, wo, w, gain, kmark, qmark):
    rows, d = first_sum.shape
    act = shape((rows, d), BF)
    specs = [at_row(block, d)] * 5 + [
        at_col(block, d), at_lead(block, 16), plane(wo, 1), plane(w, 0), whole(gain), at_row(block, 128), at_lead(block, HEAD_DIM),
    ]
    args = (ssg, first_sum, q, k, v, ot, lse, wo, w, gain, kmark, qmark)
    return one_back(
        cross_back_kernel, block, before, args, specs, [shape((rows, d), F32), act, act, act], f"cross_back_{block}"
    )


def self_back(block, before, fsg, q, k, v, ot, lse, wo, kmark, qmark):
    rows, d = fsg.shape
    act = shape((rows, d), BF)
    specs = [at_row(block, d)] * 4 + [
        at_col(block, d), at_lead(block, 16), plane(wo, 0), at_row(block, 128), at_lead(block, HEAD_DIM),
    ]
    args = (fsg, q, k, v, ot, lse, wo, kmark, qmark)
    return one_back(self_back_kernel, block, before, args, specs, [act, act, act], f"self_back_{block}")


def weight_outs(staged, count, extra, devices, d):
    if not staged:
        return [shape((count, d, d), BF), shape((8, 128), BF)]
    half = shape((2, 4, 2, count * d // devices + extra, d), BF)
    return [half, half]


def cross_weight(staged, me, devices, dq, dk, dv, low, mem, ot, ssg, sot, fsg, w):
    rows, d = dq.shape
    args = (mem, dk, dv, w, ot, ssg, sot, fsg, low, dq)
    anywhere, here = pl.BlockSpec(memory_space=pl.ANY), pl.BlockSpec(memory_space=pltpu.VMEM)
    return pl.pallas_call(
        functools.partial(cross_weight_kernel, staged),
        in_specs=[pl.BlockSpec(memory_space=pltpu.SMEM)] + [anywhere] * 10,
        out_specs=[here, here, anywhere],
        out_shape=weight_outs(staged, 5, 0, devices, d) + [shape((rows, d), F32)],
        scratch_shapes=[pltpu.VMEM(a.shape, a.dtype) for a in args] + [
            pltpu.VMEM((5, d, d), F32), pltpu.VMEM((rows, d), F32), pltpu.SemaphoreType.DMA((10,)),
            pltpu.SemaphoreType.DMA,
        ],
        compiler_params=pltpu.CompilerParams(vmem_limit_bytes=VMEM_LIMIT),
        cost_estimate=cost(9e9, 20e6),
        name="cross_weight",
    )(me, *args)


def self_weight(staged, me, devices, small, dbin, dq, dk, dv, x):
    rows, d = dq.shape
    args = (x, dq, dk, dv)
    anywhere, here = pl.BlockSpec(memory_space=pl.ANY), pl.BlockSpec(memory_space=pltpu.VMEM)
    return pl.pallas_call(
        functools.partial(self_weight_kernel, staged),
        in_specs=[pl.BlockSpec(memory_space=pltpu.SMEM), here, here] + [anywhere] * 4,
        out_specs=[here, here],
        out_shape=weight_outs(staged, 3, 32, devices, d),
        scratch_shapes=[pltpu.VMEM(a.shape, a.dtype) for a in args] + [
            pltpu.VMEM((3, d, d), F32), pltpu.SemaphoreType.DMA((4,)),
        ],
        compiler_params=pltpu.CompilerParams(vmem_limit_bytes=VMEM_LIMIT),
        cost_estimate=cost(4e9, 10e6),
        name="self_weight",
    )(me, small, dbin, *args)


def self_input(fsg, dq, dk, dv, wqk, wv):
    rows, d = fsg.shape
    return pl.pallas_call(
        self_input_kernel,
        grid=(rows // SEQ_MAX,),
        in_specs=[row_block(d)] * 4 + [whole(wqk), whole(wv)],
        out_specs=row_block(d),
        out_shape=shape((rows, d), F32),
        compiler_params=params(("arbitrary",)),
        cost_estimate=cost(4e9, 14e6),
        name="self_input",
    )(fsg, dq, dk, dv, wqk, wv)


def key_marks(seg):
    odd = (seg & 1)[:, None]
    lane = lax.broadcasted_iota(jnp.int32, (seg.shape[0], 128), 1) % HEAD_DIM
    return jnp.where(lane == 0, 1 - odd, jnp.where(lane == 1, odd, 0)).astype(BF)


def query_marks(seg):
    odd = (seg & 1).reshape(-1, 1, SEQ_MAX)
    row = lax.broadcasted_iota(jnp.int32, (odd.shape[0], HEAD_DIM, SEQ_MAX), 1)
    return jnp.where(row == 0, odd, jnp.where(row == 1, 1 - odd, 0)).astype(BF) * (-MASKED)


def swap(value, name):
    return lax.ppermute(value, name, [(0, 1), (1, 0)])


class Halving:
    def __init__(self, me, keep, send):
        self.me, self.keep, self.out = me, [keep], [send]

    def core(self):
        got = swap(self.out[0], "c")
        sl, kl, sr, kr = first_stage(self.me, self.keep[0], got)
        self.keep, self.out = [kl, kr], [sl, sr]

    def first(self):
        (kl, kr), (sl, sr) = self.keep, self.out
        gl, gr = swap(sl, "x"), swap(sr, "y")
        z, _, rows, half = kl.shape
        piece = shape((z, rows, half), BF)
        sl, ml, sr, mr = stage_call(second_stage_kernel, self.me, (kl, gl, kr, gr), [piece] * 4, "second_stage")
        self.keep, self.out = [ml, mr], [sl, sr]

    def second(self):
        (kl, kr), (sl, sr) = self.keep, self.out
        gl, gr = swap(sl, "y"), swap(sr, "x")
        _, rows, half = kl.shape
        piece = (rows, 2 * half)
        outs = [shape(piece, F32)] + [shape(piece, BF)] * 3
        own, *self.out = stage_call(third_stage_kernel, self.me, (kl, gl, kr, gr), outs, "third_stage")
        self.keep = [own]

    def last(self):
        total = self.keep[0]
        for step, out in zip(range(1, 4), self.out):
            total = total + lax.ppermute(out, "z", [(i, (i + step) % 4) for i in range(4)]).astype(F32)
        return total

    @staticmethod
    def feed(grads, own):
        sums = lax.psum_scatter(grads, ("x", "c", "z", "y"), scatter_dimension=0, tiled=True).astype(F32)
        half = sums.shape[1] // 2
        d = grads.shape[0]
        return sums[:, :half], sums[:, half:].reshape(own, -1, d).swapaxes(0, 1).reshape(-1, d)


class Whole:
    def __init__(self, me, grads, _):
        self.grads, self.out = grads, ()

    def core(self):
        pass

    first = second = core

    def last(self):
        sums = lax.psum_scatter(self.grads, ("dp", "fsdp"), scatter_dimension=1, tiled=True).astype(F32)
        return sums.reshape(-1, sums.shape[2])

    @staticmethod
    def feed(grads, own):
        sum_up = functools.partial(lax.psum_scatter, axis_name=("dp", "fsdp"), scatter_dimension=0, tiled=True)
        half, d = grads.shape[1] // 2, grads.shape[0]
        dwin = sum_up(grads[:, :half]).astype(F32)
        return dwin, sum_up(grads[:, half:].reshape(d, -1, d).swapaxes(0, 1).reshape(-1, d)).astype(F32)


def after(value, *sums):
    value, outs = lax.optimization_barrier((value, [s.out for s in sums]))
    for s, s.out in zip(sums, outs):
        pass
    return value


def take_turns(value):
    me = lax.axis_index("z")
    parts = [value]
    for step in range(3, 0, -1):
        parts.append(lax.ppermute(value, "z", [(i, (i + step) % 4) for i in range(4)]))
    return jnp.stack([lax.select_n((j - me) % 4, *parts) for j in range(4)], axis=1)


def take_pair(value, name, axis):
    me = lax.axis_index(name)
    got = lax.ppermute(value, name, [(0, 1), (1, 0)])
    return jnp.stack([jnp.where(me == 0, value, got), jnp.where(me == 0, got, value)], axis=axis)


class Doubling:
    def __init__(self, left, right):
        self.cut, self.rows = left.shape[0], left.shape[1]
        self.flat = left.shape[1:] != right.shape[1:]
        if self.flat:
            left, right = (a.reshape(1, -1, a.shape[2]) for a in (left, right))
            self.out = [jnp.concatenate([left, right], axis=1)]
            self.split = left.shape[1]
        else:
            self.out = [jnp.concatenate([left, right])]

    def line(self):
        both = take_turns(self.out[0])
        if self.flat:
            d = both.shape[3]
            left = both[0, :, : self.split].reshape(4, self.cut, self.rows, d).swapaxes(0, 1)
            self.out = [left, both[:, :, self.split :]]
        else:
            self.out = [both[: self.cut], both[self.cut :]]

    def first(self):
        self.out = [take_pair(self.out[0], "y", 2), take_pair(self.out[1], "x", 1)]

    def second(self):
        self.out = [take_pair(self.out[0], "x", 1), take_pair(self.out[1], "y", 3)]

    def core(self):
        self.out = [take_pair(self.out[0], "c", 2), take_pair(self.out[1], "c", 2)]
        return self.out


def local_small(bias, gain, shift, bin_, bout):
    return jnp.concatenate([a.reshape(-1) for a in (bias, gain, shift, bout, bin_)])


def spread_small(parts, own):
    parts = parts.astype(F32)
    devices = parts.shape[0]
    rows = parts[:, : 13 * own].reshape(devices, 13, own).swapaxes(0, 1).reshape(13, -1)
    bin_ = parts[:, 13 * own :].reshape(1, -1)
    return {"bias": rows[0:6], "gain": rows[6:9], "shift": rows[9:12], "bout": rows[12:13], "bin": bin_}


def behind(later, earlier):
    later.out = lax.optimization_barrier((later.out, earlier.out))[0]


class Stages:
    def __init__(self, proj, out, small, win, wout):
        _, own, d = proj.shape
        self.chunks = win.shape[1] // d
        feed_local = jnp.concatenate([win.reshape(own, self.chunks, d).swapaxes(0, 1), wout.reshape(self.chunks, own, d)])
        self.feed_all = lax.all_gather(feed_local, ("x", "c", "z", "y"), axis=1)
        extra = jnp.pad(small[None, None], ((0, 0), (0, 7), (0, d - small.shape[0])))
        self.one = Doubling(proj[:2], jnp.concatenate([proj[2:3], extra], axis=1))
        self.two = Doubling(proj[3:6], out)
        self.own, self.cut, self.d = own, small.shape[0], d

    def begin(self, value):
        one, two, own, d = self.one, self.two, self.own, self.d
        one.line()
        behind(two, one)
        one.first()
        two.line()
        one.second()
        behind(two, one)
        two.first()
        left, right = one.core()
        full = {"qk": left.reshape(2, -1, d), "v": right[..., :own, :].reshape(1, -1, d)}
        full.update(spread_small(right[..., own, : self.cut].reshape(-1, self.cut), own))
        value = after(value, two)
        two.second()
        return full, value

    def finish(self, value):
        two, d = self.two, self.d
        value = after(value, two)
        left, right = two.core()
        shape_f = (2 * self.chunks, -1, d)
        return {
            "cross_proj": left.reshape(3, -1, d), "out": right.reshape(2, -1, d),
            "win": self.feed_all.reshape(shape_f), "wout": self.feed_all,
        }, value


class Plain:
    def __init__(self, proj, out, small, win, wout):
        take = functools.partial(lax.all_gather, axis_name=("dp", "fsdp"), tiled=True)
        _, own, d = proj.shape
        proj = take(proj, axis=1)
        self.full = {"qk": proj[:2], "v": proj[2:3]}
        self.full.update(spread_small(take(small[None], axis=0), own))
        win = take(win, axis=0).reshape(d, -1, d).swapaxes(0, 1)
        self.rest = {"cross_proj": proj[3:], "out": take(out, axis=1), "win": win, "wout": take(wout, axis=0)}

    def begin(self, value):
        return self.full, value

    def finish(self, value):
        return self.rest, value


def body(
    gather, scatter, devices, query, memory, query_seg, memory_seg, attn_proj, attn_out, attn_bias, norm_gain, norm_bias,
    ffn_in, ffn_in_bias, ffn_out, ffn_out_bias, cotangent,
):
    blocks = range(query.shape[0] // SEQ_MAX)
    own = attn_proj.shape[1]
    d = query.shape[1]
    staged = scatter is Halving
    me, pair = jnp.zeros((3,), jnp.int32), jnp.zeros((1,), jnp.int32)
    if staged:
        me = jnp.stack([lax.axis_index(name) for name in ("x", "y", "z")])
        pair = lax.axis_index("c").reshape(1)
    small = local_small(attn_bias, norm_gain, norm_bias, ffn_in_bias, ffn_out_bias)
    weights = gather(attn_proj, attn_out, small, ffn_in, ffn_out)
    full, rows_in = weights.begin(query)
    bias, gain, shift = full["bias"], full["gain"], full["shift"]
    qmark = query_marks(query_seg)
    smark, cmark = key_marks(query_seg), key_marks(memory_seg)
    sq, sk, sv, sot, slse = self_forward(rows_in, full["qk"], full["v"], bias, smark, qmark)
    rest, sot = weights.finish(sot)
    out, cross_proj = rest["out"], rest["cross_proj"]
    first_sum, low, cq, ck, cv, cot_, clse, second_sum = cross_forward(
        query, memory, sot, out, cross_proj, bias, gain, shift, cmark, qmark
    )
    mixed, ssg, fdw, dbin, small3 = feed(
        second_sum, cotangent, rest["win"], full["bin"], rest["wout"], full["bout"], gain, shift
    )
    dwin, dwout = scatter.feed(fdw, own)
    grads, small2 = [], 0
    for block in blocks:
        *grads, part = cross_back(
            block, grads, ssg, first_sum, cq, ck, cv, cot_, clse, out, cross_proj, gain, cmark, qmark
        )
        small2 = small2 + part
    fsg, dq, dk, dv = grads
    keep, send, memory_grad = cross_weight(
        staged, pair, devices, dq, dk, dv, low, memory, cot_, ssg, sot, fsg, cross_proj
    )
    cross_sum = scatter(me, keep, send)
    upstream = after(fsg, cross_sum)
    grads, small1 = [], 0
    for block in blocks:
        *grads, part = self_back(block, grads, upstream, sq, sk, sv, sot, slse, out, smark, qmark)
        small1 = small1 + part
        if block == 0:
            cross_sum.core()
            upstream = after(upstream, cross_sum)
    dq, dk, dv = grads
    cross_sum.first()
    dq = after(dq, cross_sum)
    sums = jnp.concatenate([small1, small2, small3])
    keep, send = self_weight(staged, pair, devices, sums, dbin, dq, dk, dv, query)
    self_sum = scatter(me, keep, send)
    cross_sum.second()
    self_sum.core()
    upstream = after(fsg, self_sum, cross_sum)
    query_grad = self_input(upstream, dq, dk, dv, full["qk"], full["v"])
    self_sum.first()
    cross = cross_sum.last()
    self_sum.second()
    rows = self_sum.last()
    cross = cross.reshape(5, own, d)
    proj_grad = jnp.concatenate([rows[: 3 * own].reshape(3, own, d), cross[2:]])
    if staged:
        sums = rows[3 * own : 3 * own + 24, :own]
        dbin = rows[3 * own + 24, : dbin.shape[1] // devices]
    else:
        sum_up = functools.partial(lax.psum_scatter, axis_name=("dp", "fsdp"), scatter_dimension=1, tiled=True)
        sums, dbin = sum_up(sums), sum_up(dbin)[0]
    bias_g = jnp.concatenate([sums[0:3], sums[8:11]])
    gain_g = jnp.stack([sums[11], sums[19], sums[16]])
    shift_g = jnp.stack([sums[12], sums[20], sums[17]])
    return (
        mixed, query_grad, memory_grad, proj_grad, cross[1::-1], bias_g, gain_g, shift_g, dwin, dbin, dwout, sums[18],
    )


def solution(mesh):
    devices = mesh.size
    if dict(mesh.shape) == {"dp": 4, "fsdp": 8}:
        axes = ("x", "c", "z", "y")
        mesh = Mesh(mesh.devices.reshape(2, 2, 4, 2), axes)
        gather, scatter = Stages, Halving
    else:
        axes = ("dp", "fsdp")
        gather, scatter = Plain, Whole
    rows, mid, flat, row1 = P(axes, None), P(None, axes, None), P(None, axes), P(axes)
    return jax.shard_map(
        functools.partial(body, gather, scatter, devices),
        mesh=mesh,
        in_specs=(rows, rows, row1, row1, mid, mid, flat, flat, flat, rows, row1, rows, row1, rows),
        out_specs=(rows, rows, rows, mid, mid, flat, flat, flat, rows, row1, rows, row1),
        check_vma=False,
    )
```

profile of v0, /device:TPU:0, one launch (start us, length us, event | category | flops | bytes accessed | tf_op | source)
XLA Modules:
  0.0 445.0 jit_solution(11533148850607922596)
XLA Ops:
  23.5 8.0 %collective-permute-done.1 = bf16[1,80,768]{2,1,0:T(8,128)(2,1)S(1)} collective-permute-done((bf16[1,80,768]{2,1,0:T(8,128)(2,1)S(1)}, bf16[1,80,768]{2,1,0:T(8,128)(2,1)S(1)}, u32[]{:S(2)}, u32[]{:S(2)}) %collective-permute-start.1) | collective-permute-done | bytes 122912 | tf_op jit(solution)/shard_map/ppermute | solution.py:781
  50.5 8.6 %collective-permute-done.4 = bf16[5,24,768]{2,1,0:T(8,128)(2,1)S(1)} collective-permute-done((bf16[5,24,768]{2,1,0:T(8,128)(2,1)S(1)}, bf16[5,24,768]{2,1,0:T(8,128)(2,1)S(1)}, u32[]{:S(2)}, u32[]{:S(2)}) %collective-permute-start.4) | collective-permute-done | bytes 184352 | tf_op jit(solution)/shard_map/ppermute | solution.py:781
  66.5 4.7 %collective-permute-done.9 = bf16[1,2,4,32,768]{4,2,3,1,0:T(4,128)(2,1)S(1)} collective-permute-done((bf16[1,2,4,32,768]{4,2,3,1,0:T(4,128)(2,1)S(1)}, bf16[1,2,4,32,768]{4,2,3,1,0:T(4,128)(2,1)S(1)}, u32[]{:S(2)}, u32[]{:S(2)}) %collective-permute-start.9) | collective-permute-done | bytes 393248 | tf_op jit(solution)/shard_map/ppermute | solution.py:787
  72.3 4.9 %collective-permute-done.7 = bf16[2,4,2,24,768]{4,3,0,1,2:T(8,128)(2,1)S(1)} collective-permute-done((bf16[2,4,2,24,768]{4,3,0,1,2:T(8,128)(2,1)S(1)}, bf16[2,4,2,24,768]{4,3,0,1,2:T(8,128)(2,1)S(1)}, u32[]{:S(2)}, u32[]{:S(2)}) %collective-permute-start.7) | collective-permute-done | bytes 589856 | tf_op jit(solution)/shard_map/ppermute | solution.py:787
  80.9 10.6 %collective-permute-done.11 = bf16[2,4,24,768]{3,2,0,1:T(8,128)(2,1)S(1)} collective-permute-done((bf16[2,4,24,768]{3,2,0,1:T(8,128)(2,1)S(1)}, bf16[2,4,24,768]{3,2,0,1:T(8,128)(2,1)S(1)}, u32[]{:S(2)}, u32[]{:S(2)}) %collective-permute-start.11) | collective-permute-done | bytes 294944 | tf_op jit(solution)/shard_map/ppermute | solution.py:787
  91.6 9.6 %collective-permute-done.10 = bf16[3,4,24,768]{3,2,0,1:T(8,128)(2,1)S(1)} collective-permute-done((bf16[3,4,24,768]{3,2,0,1:T(8,128)(2,1)S(1)}, bf16[3,4,24,768]{3,2,0,1:T(8,128)(2,1)S(1)}, u32[]{:S(2)}, u32[]{:S(2)}) %collective-permute-start.10) | collective-permute-done | bytes 442400 | tf_op jit(solution)/shard_map/ppermute | solution.py:787
  108.6 9.3 %collective-permute-done.15 = bf16[2,2,4,24,768]{4,3,0,2,1:T(8,128)(2,1)} collective-permute-done((bf16[2,2,4,24,768]{4,3,0,2,1:T(8,128)(2,1)S(1)}, bf16[2,2,4,24,768]{4,3,0,2,1:T(8,128)(2,1)}, u32[]{:S(2)}, u32[]{:S(2)}) %collective-permute-start.15) | collective-permute-done | bytes 589856 | tf_op jit(solution)/shard_map/ppermute | solution.py:787
  122.4 21.3 %self_forward.1 = (bf16[1024,768]{1,0:T(8,128)(2,1)}, bf16[1024,768]{1,0:T(8,128)(2,1)}, bf16[1024,768]{1,0:T(8,128)(2,1)}, bf16[768,1024]{1,0:T(8,128)(2,1)}, f32[2,16,512]{2,1,0:T(8,128)}) custom-call(bf16[1024,768]{1,0:T(8,128)(2,1)} %x_ref.4, bf16[2,768,768]{2,1,0:T(8,128)(2,1)} %bitcast.116, bf16[1,768,768]{2,1,0:T(8,128)(2,1)} %bitcast.123, ...), custom_call_target="tpu_custom_call" | custom-call | flops 20000000000 | bytes 12000000 | tf_op jit(solution)/shard_map/self_forward/pallas_call | solution.py:500
  158.5 27.7 %cross_forward.1 = (f32[1024,768]{1,0:T(8,128)}, bf16[1024,768]{1,0:T(8,128)(2,1)}, bf16[1024,768]{1,0:T(8,128)(2,1)}, bf16[1024,768]{1,0:T(8,128)(2,1)}, bf16[1...) custom-call(bf16[1024,768]{1,0:T(8,128)(2,1)} %x_ref.4, ...), custom_call_target="tpu_custom_call" | custom-call | flops 24000000000 | bytes 20000000 | tf_op jit(solution)/shard_map/cross_forward/pallas_call | solution.py:517
  186.2 52.6 %feed.1 = (bf16[1024,768]{1,0:T(8,128)(2,1)}, f32[1024,768]{1,0:T(8,128)}, bf16[768,6144]{1,0:T(8,128)(2,1)}, f32[1,3072]{1,0:T(1,128)}, f32[8,768]{1,0:T(8,128)}) custom-call(f32[1024,768]{1,0:T(8,128)} %get-tuple-element.110.ss_ref, bf16[1024,768]{1,0:T(8,128)(2,1)} %cot_ref.1, bf16[8,768,768]{2,1,0:T(8,128)(2,1)} %all-gather.3.cloned.1.call-done.win_ref, ...), custom_call_target="tpu_custom_call" | custom-call | flops 40000000000 | bytes 40000000 | tf_op jit(solution)/shard_map/feed/pallas_call | solution.py:545
  238.8 15.9 %cross_back_0.1 = (f32[1024,768]{1,0:T(8,128)}, bf16[1024,768]{1,0:T(8,128)(2,1)}, bf16[1024,768]{1,0:T(8,128)(2,1)}, bf16[1024,768]{1,0:T(8,128)(2,1)}, f32[8,768]{1,0:T(8,128)}) custom-call(f32[1024,768]{1,0:T(8,128)} %get-tuple-element.112.ssg_ref.refs_5_, f32[1024,768]{1,0:T(8,128)} %get-tuple-element.113.fs_ref, ...), custom_call_target="tpu_custom_call" | custom-call | flops 24999999488 | bytes 15000000 | tf_op jit(solution)/shard_map/cross_back_0/pallas_call | solution.py:599
  254.7 16.3 %cross_back_1.1 = (f32[1024,768]{1,0:T(8,128)}, bf16[1024,768]{1,0:T(8,128)(2,1)}, bf16[1024,768]{1,0:T(8,128)(2,1)}, bf16[1024,768]{1,0:T(8,128)(2,1)}, f32[8,768]{1,0:T(8,128)}) custom-call(f32[1024,768]{1,0:T(8,128)} %get-tuple-element.112.ssg_ref.refs_5_, ...), custom_call_target="tpu_custom_call", output_to_operand_aliasing={{0}: (12, {}), {1}: (13, {}), {2}: (14, {}), {3}: (15, {})} | custom-call | flops 24999999488 | bytes 15000000 | tf_op jit(solution)/shard_map/cross_back_1/pallas_call | solution.py:599
  271.0 18.0 %cross_weight.1 = (bf16[2,4,2,120,768]{4,3,2,1,0:T(8,128)(2,1)}, bf16[2,4,2,120,768]{4,3,2,1,0:T(8,128)(2,1)}, f32[1024,768]{1,0:T(8,128)}) custom-call(s32[1]{0:T(128)} %bitcast.50.me_ref, bf16[1024,768]{1,0:T(8,128)(2,1)} %refs_0_.1, bf16[1024,768]{1,0:T(8,128)(2,1)} %get-tuple-element.124.refs_1_, bf16[1024,768]{1,0:T(8,128)(2,1)} %get-tuple-element.125.refs_2_, ...), custom_call_target="tpu_custom_call" | custom-call | flops 8999999488 | bytes 20000000 | tf_op jit(solution)/shard_map/cross_weight/pallas_call | solution.py:646
  289.9 13.9 %self_back_0.1 = (bf16[1024,768]{1,0:T(8,128)(2,1)}, bf16[1024,768]{1,0:T(8,128)(2,1)}, bf16[1024,768]{1,0:T(8,128)(2,1)}, f32[8,768]{1,0:T(8,128)}) custom-call(f32[1024,768]{1,0:T(8,128)} %get-tuple-element.169.refs_7_.fsg_ref, bf16[1024,768]{1,0:T(8,128)(2,1)} %get-tuple-element.130.q_ref, bf16[1024,768]{1,0:T(8,128)(2,1)} %get-tuple-element.131.k_ref, ...), custom_call_target="tpu_custom_call" | custom-call | flops 24999999488 | bytes 15000000 | tf_op jit(solution)/shard_map/self_back_0/pallas_call | solution.py:599
  305.3 4.9 %first_stage.2 = (bf16[4,2,120,384]{3,2,1,0:T(8,128)(2,1)}, bf16[4,2,120,384]{3,2,1,0:T(8,128)(2,1)}, bf16[2,4,120,384]{3,2,1,0:T(8,128)(2,1)}, bf16[2,4,120,384]{3,2,1,0:T(8,128)(2,1)}) custom-call(s32[3]{0:T(128)} %pad_add_fusion.me_ref, bf16[2,4,2,120,768]{4,3,2,1,0:T(8,128)(2,1)} %get-tuple-element.135.keep_ref, bf16[2,4,2,120,768]{4,3,2,1,0:T(8,128)(2,1)} %copy-done), custom_call_target="tpu_custom_call" | custom-call | flops 1474560 | bytes 8847360 | tf_op jit(solution)/shard_map/first_stage/pallas_call | solution.py:451
  310.9 13.9 %self_back_1.1 = (bf16[1024,768]{1,0:T(8,128)(2,1)}, bf16[1024,768]{1,0:T(8,128)(2,1)}, bf16[1024,768]{1,0:T(8,128)(2,1)}, f32[8,768]{1,0:T(8,128)}) custom-call(f32[1024,768]{1,0:T(8,128)} %get-tuple-element.169.refs_7_.fsg_ref, bf16[1024,768]{1,0:T(8,128)(2,1)} %get-tuple-element.130.q_ref, ...), custom_call_target="tpu_custom_call", output_to_operand_aliasing={{0}: (9, {}), {1}: (10, {}), {2}: (11, {})} | custom-call | flops 24999999488 | bytes 15000000 | tf_op jit(solution)/shard_map/self_back_1/pallas_call | solution.py:599
  326.2 10.0 %collective-permute-done.19.gl_ref = bf16[4,2,120,384]{3,2,1,0:T(8,128)(2,1)S(1)} collective-permute-done((bf16[4,2,120,384]{3,2,1,0:T(8,128)(2,1)}, bf16[4,2,120,384]{3,2,1,0:T(8,128)(2,1)S(1)}, u32[]{:S(2)}, u32[]{:S(2)}) %collective-permute-start.19) | collective-permute-done | bytes 737312 | tf_op jit(solution)/shard_map/ppermute | solution.py:706
  340.9 10.3 %self_weight.1 = (bf16[2,4,2,104,768]{4,3,2,1,0:T(8,128)(2,1)}, bf16[2,4,2,104,768]{4,3,2,1,0:T(8,128)(2,1)}) custom-call(s32[1]{0:T(128)} %bitcast.50.me_ref, f32[24,768]{1,0:T(8,128)} %pad_maximum_fusion.18.small_ref, f32[1,3072]{1,0:T(1,128)} %get-tuple-element.147.dbin_ref, bf16[1024,768]{1,0:T(8,128)(2,1)} %x_ref.4, ...), custom_call_target="tpu_custom_call" | custom-call | flops 4000000000 | bytes 10000000 | tf_op jit(solution)/shard_map/self_weight/pallas_call | solution.py:665
  353.1 16.1 %collective-permute-done.22.gl_ref = bf16[4,120,384]{2,1,0:T(8,128)(2,1)S(1)} collective-permute-done((bf16[4,120,384]{2,1,0:T(8,128)(2,1)S(1)}, bf16[4,120,384]{2,1,0:T(8,128)(2,1)S(1)}, u32[]{:S(2)}, u32[]{:S(2)}) %collective-permute-start.22) | collective-permute-done | bytes 368672 | tf_op jit(solution)/shard_map/ppermute | solution.py:706
  374.1 4.7 %first_stage.3 = (bf16[4,2,104,384]{3,2,1,0:T(8,128)(2,1)}, bf16[4,2,104,384]{3,2,1,0:T(8,128)(2,1)}, bf16[2,4,104,384]{3,2,1,0:T(8,128)(2,1)}, bf16[2,4,104,384]{3,2,1,0:T(8,128)(2,1)}) custom-call(s32[3]{0:T(128)} %pad_add_fusion.me_ref, bf16[2,4,2,104,768]{4,3,2,1,0:T(8,128)(2,1)} %get-tuple-element.158.keep_ref, bf16[2,4,2,104,768]{4,3,2,1,0:T(8,128)(2,1)} %copy-done.1), custom_call_target="tpu_custom_call" | custom-call | flops 1277952 | bytes 7667712 | tf_op jit(solution)/shard_map/first_stage/pallas_call | solution.py:451
  383.1 4.8 %collective-permute-start.32 = (bf16[120,768]{1,0:T(8,128)(2,1)S(1)}, bf16[120,768]{1,0:T(8,128)(2,1)S(1)}, u32[]{:S(2)}, u32[]{:S(2)}) collective-permute-start(bf16[120,768]{1,0:T(8,128)(2,1)S(1)} %copy-done.22), channel_id=1, source_target_pairs={{0,4},{2,6},{4,0},{6,2},{1,5},{3,7},{5,1},{7,3},{8,12},{10,14},{12... | collective-permute-start | bytes 552968 | tf_op jit(solution)/shard_map/ppermute | solution.py:738
  387.9 9.3 %collective-permute-done.24.gl_ref = bf16[4,2,104,384]{3,2,1,0:T(8,128)(2,1)S(1)} collective-permute-done((bf16[4,2,104,384]{3,2,1,0:T(8,128)(2,1)}, bf16[4,2,104,384]{3,2,1,0:T(8,128)(2,1)S(1)}, u32[]{:S(2)}, u32[]{:S(2)}) %collective-permute-start.24) | collective-permute-done | bytes 639008 | tf_op jit(solution)/shard_map/ppermute | solution.py:706
  403.3 8.9 %self_input.1 = f32[1024,768]{1,0:T(8,128)} custom-call(f32[1024,768]{1,0:T(8,128)} %get-tuple-element.169.refs_7_.fsg_ref, bf16[1024,768]{1,0:T(8,128)(2,1)} %get-tuple-element.155.dq_ref, bf16[1024,768]{1,0:T(8,128)(2,1)} %get-tuple-element.156.dk_ref, bf16[1024,768]{1,0:T(8,128)(2,1)} %get-tuple-element.157.dv_ref, bf16[2,768,768]{2,1,0:T(8,128)(2,1)} %bitcast.117, ...), custom_call_target="tpu_custom_call" | custom-call | flops 4000000000 | bytes 14000000 | tf_op jit(solution)/shard_map/self_input/pallas_call | solution.py:681
  426.2 5.1 %collective-permute-done.29 = bf16[104,768]{1,0:T(8,128)(2,1)S(1)} collective-permute-done((bf16[104,768]{1,0:T(8,128)(2,1)}, bf16[104,768]{1,0:T(8,128)(2,1)S(1)}, u32[]{:S(2)}, u32[]{:S(2)}) %collective-permute-start.29) | collective-permute-done | bytes 159776 | tf_op jit(solution)/shard_map/ppermute | solution.py:738
  (215 shorter events, 120.4 us)
Async XLA Ops:
  7.2 179.0 %all-gather.3.cloned.1.call-start = ((), (), s32[]{:S(2)}) async-start(), calls=%async_computation.2 | async-start | bytes 9732096 | tf_op jit(solution)/shard_map/all_gather | solution.py:843
  9.9 425.2 %reduce-scatter.2.cloned.1.call-start = ((), (), s32[]{:S(2)}) async-start(), calls=%async_computation.1 | async-start | bytes 9732096 | tf_op jit(solution)/shard_map/reduce_scatter | solution.py:743
  15.4 16.1 %collective-permute-start.1 = (bf16[1,80,768]{2,1,0:T(8,128)(2,1)S(1)}, bf16[1,80,768]{2,1,0:T(8,128)(2,1)S(1)}, u32[]{:S(2)}, u32[]{:S(2)}) collective-permute-start(bf16[1,80,768]{2,1,0:T(8,128)(2,1)S(1)} %fusion.9), channel_id=1, source_target_pairs={{0,4},{2,6},{4,0},{6,2},{1,5},{3,7},{5,1},{7,3},{8,12},{10,14},{12... | collective-permute-start | bytes 368648 | tf_op jit(solution)/shard_map/ppermute | solution.py:781
  40.4 18.7 %collective-permute-start.4 = (bf16[5,24,768]{2,1,0:T(8,128)(2,1)S(1)}, bf16[5,24,768]{2,1,0:T(8,128)(2,1)S(1)}, u32[]{:S(2)}, u32[]{:S(2)}) collective-permute-start(bf16[5,24,768]{2,1,0:T(8,128)(2,1)S(1)} %pad_maximum_fusion.17), channel_id=1, source_target_pairs={{0,4},{2,6},{4,0},{6,2},{1,5},{3,7},{5,1},{7,3},{8,12},{10,14},{12... | collective-permute-start | bytes 552968 | tf_op jit(solution)/shard_map/ppermute | solution.py:781
  42.4 19.5 %collective-permute-start.3 = (bf16[5,24,768]{2,1,0:T(8,128)(2,1)S(1)}, bf16[5,24,768]{2,1,0:T(8,128)(2,1)S(1)}, u32[]{:S(2)}, u32[]{:S(2)}) collective-permute-start(bf16[5,24,768]{2,1,0:T(8,128)(2,1)S(1)} %pad_maximum_fusion.17), channel_id=1, source_target_pairs={{0,6},{2,0},{4,2},{6,4},{1,7},{3,1},{5,3},{7,5},{8,14},{10,8},{12,... | collective-permute-start | bytes 552968 | tf_op jit(solution)/shard_map/ppermute | solution.py:781
  47.4 14.6 %collective-permute-start.8 = (bf16[1,4,32,768]{3,1,2,0:T(4,128)(2,1)S(1)}, bf16[1,4,32,768]{3,1,2,0:T(4,128)(2,1)S(1)}, u32[]{:S(2)}, u32[]{:S(2)}) collective-permute-start(bf16[1,4,32,768]{3,1,2,0:T(4,128)(2,1)S(1)} %pad_maximum_fusion.16), channel_id=1, source_target_pairs={{0,16},{16,0},{1,17},{17,1},{2,18},{18,2},{3,19},{19,3},{4,20},{20... | collective-permute-start | bytes 589832 | tf_op jit(solution)/shard_map/ppermute | solution.py:787
  49.0 15.7 %collective-permute-start.6 = (bf16[2,4,24,768]{3,2,0,1:T(8,128)(2,1)S(1)}, bf16[2,4,24,768]{3,2,0,1:T(8,128)(2,1)S(1)}, u32[]{:S(2)}, u32[]{:S(2)}) collective-permute-start(bf16[2,4,24,768]{3,2,0,1:T(8,128)(2,1)S(1)} %bitcast.136), channel_id=1, source_target_pairs={{0,1},{1,0},{2,3},{3,2},{4,5},{5,4},{6,7},{7,6},{8,9},{9,8},{10,11... | collective-permute-start | bytes 884744 | tf_op jit(solution)/shard_map/ppermute | solution.py:787
  80.1 21.2 %collective-permute-start.10 = (bf16[3,4,24,768]{3,2,0,1:T(8,128)(2,1)S(1)}, bf16[3,4,24,768]{3,2,0,1:T(8,128)(2,1)S(1)}, u32[]{:S(2)}, u32[]{:S(2)}) collective-permute-start(bf16[3,4,24,768]{3,2,0,1:T(8,128)(2,1)S(1)} %slice.155), channel_id=1, source_target_pairs={{0,1},{1,0},{2,3},{3,2},{4,5},{5,4},{6,7},{7,6},{8,9},{9,8},{10,11... | collective-permute-start | bytes 1327112 | tf_op jit(solution)/shard_map/ppermute | solution.py:787
  80.4 23.1 %collective-permute-start.13 = (bf16[1,2,4,2,32,768]{5,2,4,3,1,0:T(4,128)(2,1)S(1)}, bf16[1,2,4,2,32,768]{5,2,4,3,1,0:T(4,128)(2,1)}, u32[]{:S(2)}, u32[]{:S(2)}) collective-permute-start(bf16[1,2,4,2,32,768]{5,2,4,3,1,0:T(4,128)(2,1)S(1)} %pad_maximum_fusion.7), channel_id=1, source_target_pairs={{0,8},{8,0},{1,9},{9,1},{2,10},{10,2},{3,11},{11,3},{4,12},{12,4},... | collective-permute-start | bytes 2359304 | tf_op jit(solution)/shard_map/ppermute | solution.py:787
  80.4 38.7 %collective-permute-start.12 = (bf16[2,2,4,2,24,768]{5,4,0,2,1,3:T(8,128)(2,1)}, bf16[2,2,4,2,24,768]{5,4,0,2,1,3:T(8,128)(2,1)}, u32[]{:S(2)}, u32[]{:S(2)}) collective-permute-start(bf16[2,2,4,2,24,768]{5,4,0,2,1,3:T(8,128)(2,1)} %pad_maximum_fusion.4), channel_id=1, source_target_pairs={{0,8},{8,0},{1,9},{9,1},{2,10},{10,2},{3,11},{11,3},{4,12},{12,4},... | collective-permute-start | bytes 3538952 | tf_op jit(solution)/shard_map/ppermute | solution.py:787
  102.4 15.5 %collective-permute-start.15 = (bf16[2,2,4,24,768]{4,3,0,2,1:T(8,128)(2,1)S(1)}, bf16[2,2,4,24,768]{4,3,0,2,1:T(8,128)(2,1)}, u32[]{:S(2)}, u32[]{:S(2)}) collective-permute-start(bf16[2,2,4,24,768]{4,3,0,2,1:T(8,128)(2,1)S(1)} %pad_maximum_fusion.10), channel_id=1, source_target_pairs={{0,1},{1,0},{2,3},{3,2},{4,5},{5,4},{6,7},{7,6},{8,9},{9,8},{10,11... | collective-permute-start | bytes 1769480 | tf_op jit(solution)/shard_map/ppermute | solution.py:787
  103.4 40.3 %collective-permute-start.14 = (bf16[3,4,2,24,768]{4,3,0,1,2:T(8,128)(2,1)}, bf16[3,4,2,24,768]{4,3,0,1,2:T(8,128)(2,1)}, u32[]{:S(2)}, u32[]{:S(2)}) collective-permute-start(bf16[3,4,2,24,768]{4,3,0,1,2:T(8,128)(2,1)} %pad_maximum_fusion.6), channel_id=1, source_target_pairs={{0,16},{16,0},{1,17},{17,1},{2,18},{18,2},{3,19},{19,3},{4,20},{20... | collective-permute-start | bytes 2654216 | tf_op jit(solution)/shard_map/ppermute | solution.py:787
  289.1 14.7 %collective-permute-start.18 = (bf16[2,4,2,120,768]{4,3,2,1,0:T(8,128)(2,1)}, bf16[2,4,2,120,768]{4,3,2,1,0:T(8,128)(2,1)S(1)}, u32[]{:S(2)}, u32[]{:S(2)}) collective-permute-start(bf16[2,4,2,120,768]{4,3,2,1,0:T(8,128)(2,1)} %get-tuple-element.136), channel_id=1, source_target_pairs={{0,8},{8,0},{1,9},{9,1},{2,10},{10,2},{3,11},{11,3},{4,12},{12,4},... | collective-permute-start | bytes 8847368 | tf_op jit(solution)/shard_map/ppermute | solution.py:706
  310.2 26.0 %collective-permute-start.19 = (bf16[4,2,120,384]{3,2,1,0:T(8,128)(2,1)}, bf16[4,2,120,384]{3,2,1,0:T(8,128)(2,1)S(1)}, u32[]{:S(2)}, u32[]{:S(2)}) collective-permute-start(bf16[4,2,120,384]{3,2,1,0:T(8,128)(2,1)} %get-tuple-element.150), channel_id=1, source_target_pairs={{0,16},{16,0},{1,17},{17,1},{2,18},{18,2},{3,19},{19,3},{4,20},{20... | collective-permute-start | bytes 2211848 | tf_op jit(solution)/shard_map/ppermute | solution.py:706
  310.7 26.2 %collective-permute-start.20 = (bf16[2,4,120,384]{3,2,1,0:T(8,128)(2,1)}, bf16[2,4,120,384]{3,2,1,0:T(8,128)(2,1)S(1)}, u32[]{:S(2)}, u32[]{:S(2)}) collective-permute-start(bf16[2,4,120,384]{3,2,1,0:T(8,128)(2,1)} %get-tuple-element.152), channel_id=1, source_target_pairs={{0,1},{1,0},{2,3},{3,2},{4,5},{5,4},{6,7},{7,6},{8,9},{9,8},{10,11... | collective-permute-start | bytes 2211848 | tf_op jit(solution)/shard_map/ppermute | solution.py:706
  351.2 21.4 %collective-permute-start.21 = (bf16[2,4,2,104,768]{4,3,2,1,0:T(8,128)(2,1)}, bf16[2,4,2,104,768]{4,3,2,1,0:T(8,128)(2,1)S(1)}, u32[]{:S(2)}, u32[]{:S(2)}) collective-permute-start(bf16[2,4,2,104,768]{4,3,2,1,0:T(8,128)(2,1)} %get-tuple-element.159), channel_id=1, source_target_pairs={{0,8},{8,0},{1,9},{9,1},{2,10},{10,2},{3,11},{11,3},{4,12},{12,4},... | collective-permute-start | bytes 7667720 | tf_op jit(solution)/shard_map/ppermute | solution.py:706
  351.3 18.0 %collective-permute-start.22 = (bf16[4,120,384]{2,1,0:T(8,128)(2,1)S(1)}, bf16[4,120,384]{2,1,0:T(8,128)(2,1)S(1)}, u32[]{:S(2)}, u32[]{:S(2)}) collective-permute-start(bf16[4,120,384]{2,1,0:T(8,128)(2,1)S(1)} %copy-done.20), channel_id=1, source_target_pairs={{0,1},{1,0},{2,3},{3,2},{4,5},{5,4},{6,7},{7,6},{8,9},{9,8},{10,11... | collective-permute-start | bytes 1105928 | tf_op jit(solution)/shard_map/ppermute | solution.py:706
  351.4 17.9 %collective-permute-start.23 = (bf16[4,120,384]{2,1,0:T(8,128)(2,1)S(1)}, bf16[4,120,384]{2,1,0:T(8,128)(2,1)S(1)}, u32[]{:S(2)}, u32[]{:S(2)}) collective-permute-start(bf16[4,120,384]{2,1,0:T(8,128)(2,1)S(1)} %copy-done.19), channel_id=1, source_target_pairs={{0,16},{16,0},{1,17},{17,1},{2,18},{18,2},{3,19},{19,3},{4,20},{20... | collective-permute-start | bytes 1105928 | tf_op jit(solution)/shard_map/ppermute | solution.py:706
  378.8 18.5 %collective-permute-start.24 = (bf16[4,2,104,384]{3,2,1,0:T(8,128)(2,1)}, bf16[4,2,104,384]{3,2,1,0:T(8,128)(2,1)S(1)}, u32[]{:S(2)}, u32[]{:S(2)}) collective-permute-start(bf16[4,2,104,384]{3,2,1,0:T(8,128)(2,1)} %get-tuple-element.172), channel_id=1, source_target_pairs={{0,16},{16,0},{1,17},{17,1},{2,18},{18,2},{3,19},{19,3},{4,20},{20... | collective-permute-start | bytes 1916936 | tf_op jit(solution)/shard_map/ppermute | solution.py:706
  380.2 18.2 %collective-permute-start.25 = (bf16[2,4,104,384]{3,2,1,0:T(8,128)(2,1)}, bf16[2,4,104,384]{3,2,1,0:T(8,128)(2,1)S(1)}, u32[]{:S(2)}, u32[]{:S(2)}) collective-permute-start(bf16[2,4,104,384]{3,2,1,0:T(8,128)(2,1)} %get-tuple-element.174), channel_id=1, source_target_pairs={{0,1},{1,0},{2,3},{3,2},{4,5},{5,4},{6,7},{7,6},{8,9},{9,8},{10,11... | collective-permute-start | bytes 1916936 | tf_op jit(solution)/shard_map/ppermute | solution.py:706
  380.8 40.7 %collective-permute-start.31 = (bf16[120,768]{1,0:T(8,128)(2,1)S(1)}, bf16[120,768]{1,0:T(8,128)(2,1)S(1)}, u32[]{:S(2)}, u32[]{:S(2)}) collective-permute-start(bf16[120,768]{1,0:T(8,128)(2,1)S(1)} %copy-done.23), channel_id=1, source_target_pairs={{0,2},{2,4},{4,6},{6,0},{1,3},{3,5},{5,7},{7,1},{8,10},{10,12},{12... | collective-permute-start | bytes 552968 | tf_op jit(solution)/shard_map/ppermute | solution.py:738
  383.1 38.3 %collective-permute-start.32 = (bf16[120,768]{1,0:T(8,128)(2,1)S(1)}, bf16[120,768]{1,0:T(8,128)(2,1)S(1)}, u32[]{:S(2)}, u32[]{:S(2)}) collective-permute-start(bf16[120,768]{1,0:T(8,128)(2,1)S(1)} %copy-done.22), channel_id=1, source_target_pairs={{0,4},{2,6},{4,0},{6,2},{1,5},{3,7},{5,1},{7,3},{8,12},{10,14},{12... | collective-permute-start | bytes 552968 | tf_op jit(solution)/shard_map/ppermute | solution.py:738
  387.9 33.6 %collective-permute-start.33 = (bf16[120,768]{1,0:T(8,128)(2,1)S(1)}, bf16[120,768]{1,0:T(8,128)(2,1)S(1)}, u32[]{:S(2)}, u32[]{:S(2)}) collective-permute-start(bf16[120,768]{1,0:T(8,128)(2,1)S(1)} %copy-done.21), channel_id=1, source_target_pairs={{0,6},{2,0},{4,2},{6,4},{1,7},{3,1},{5,3},{7,5},{8,14},{10,8},{12,... | collective-permute-start | bytes 552968 | tf_op jit(solution)/shard_map/ppermute | solution.py:738
  417.1 14.3 %collective-permute-start.29 = (bf16[104,768]{1,0:T(8,128)(2,1)}, bf16[104,768]{1,0:T(8,128)(2,1)S(1)}, u32[]{:S(2)}, u32[]{:S(2)}) collective-permute-start(bf16[104,768]{1,0:T(8,128)(2,1)} %get-tuple-element.181), channel_id=1, source_target_pairs={{0,4},{2,6},{4,0},{6,2},{1,5},{3,7},{5,1},{7,3},{8,12},{10,14},{12... | collective-permute-start | bytes 479240 | tf_op jit(solution)/shard_map/ppermute | solution.py:738
  (37 other events, 353.1 us)
Sparse Core Ops, SparseCore 0:
  11.5 107.6 all-gather.2
  239.0 164.0 reduce-scatter.1
where the time goes:
time: 450 us; the launch traced here: 445 us
  Pallas kernels  219 us (49%)
  waiting for transfers between devices  109 us (24%)
  starting transfers between devices  45.8 us (10%)
  local copies, waits for them, and re-layouts  28.7 us (6%)
  other arithmetic  26.7 us (6%)
  between operations  15.2 us (3%)
    pallas_call x4, Pallas kernels, one_back(): pl.pallas_call(kernel, grid=(1,), in_specs=specs + kept, out_specs=[at_ro...  60 us
    pallas_call x1, Pallas kernels, feed(): pl.pallas_call(functools.partial(feed_kernel, own), grid=(2, chunks), in_...  52.6 us
    ppermute x12, waiting for transfers between devices, take_pair(): got = lax.ppermute(value, name, [(0, 1), (1, 0)])  41 us
    ppermute x10, waiting for transfers between devices, swap(): return lax.ppermute(value, name, [(0, 1), (1, 0)])  37.4 us
    pallas_call x1, Pallas kernels, cross_forward(): pl.pallas_call(cross_forward_kernel, grid=(blocks,), in_specs=[row_block(...  27.7 us
    ppermute x6, waiting for transfers between devices, take_turns(): lax.ppermute(value, 'z', [(i, (i + step) % 4) for i in range(4)])  21.9 us
    pallas_call x1, Pallas kernels, self_forward(): pl.pallas_call(self_forward_kernel, grid=(blocks,), in_specs=[row_block(d...  21.3 us
    pallas_call x1, Pallas kernels, cross_weight(): pl.pallas_call(functools.partial(cross_weight_kernel, staged), in_specs=[...  18 us
  transfers between devices with their start and end apart: 36, of which 17 were waited for; matrix products, arithmetic and copies ran while one was open for 10% of the time, Pallas kernels for 37%

commit v1 on v0

--- a/solution.py
+++ b/solution.py
@@ -84,20 +84,26 @@
     qmark = qmark_ref[0]
     ones = jnp.ones((16, SEQ_MAX), BF)
 
-    def one_pair(pair, carry):
-        tile = k_ref[:, pl.ds(pl.multiple_of(pair * 128, 128), 128)]
-        for side in range(2):
-            rows = head_pair(side, pair)
-            scores = dot(key_tile(tile, kmark, side), query_tile(qt_ref[rows, :], qmark, side))
-            peak = jnp.max(scores, axis=0, keepdims=True)
-            weights = jnp.exp(scores - peak).astype(BF)
-            result = dot(jnp.concatenate([vt_ref[rows, :], ones], axis=0), weights)
-            total = result[HEAD_DIM : HEAD_DIM + 1]
-            ot_ref[rows, :] = (result[:HEAD_DIM] * (1.0 / total)).astype(BF)
-            lse_ref[0, pl.ds(pair * 2 + side, 1), :] = peak + jnp.log(total)
-        return carry
-
-    lax.fori_loop(0, PAIRS, one_pair, 0)
+    def score(head):
+        pair, side = head // 2, head % 2
+        rows = slice(head * HEAD_DIM, (head + 1) * HEAD_DIM)
+        tile = k_ref[:, pair * 128 : (pair + 1) * 128]
+        return dot(key_tile(tile, kmark, side), query_tile(qt_ref[rows, :], qmark, side))
+
+    def finish(head, peak, weights):
+        rows = slice(head * HEAD_DIM, (head + 1) * HEAD_DIM)
+        result = dot(jnp.concatenate([vt_ref[rows, :], ones], axis=0), weights)
+        total = result[HEAD_DIM : HEAD_DIM + 1]
+        ot_ref[rows, :] = (result[:HEAD_DIM] * (1.0 / total)).astype(BF)
+        lse_ref[0, head : head + 1, :] = peak + jnp.log(total)
+
+    for start in range(0, HEADS, 6):
+        heads = range(start, start + 6)
+        scores = [score(head) for head in heads]
+        peaks = [jnp.max(s, axis=0, keepdims=True) for s in scores]
+        weights = [jnp.exp(s - peak).astype(BF) for s, peak in zip(scores, peaks)]
+        for head, peak, weight in zip(heads, peaks, weights):
+            finish(head, peak, weight)
 
 
 def attend_back_block(
@@ -108,26 +114,34 @@
     left = left_half((SEQ_MAX, 128))
     blank = jnp.zeros((HEAD_DIM, SEQ_MAX), BF)
 
-    def one_pair(pair, carry):
-        cols = pl.ds(pl.multiple_of(pair * 128, 128), 128)
-        k_tile, v_tile, q_tile, do_tile = k_ref[:, cols], v_ref[:, cols], q_ref[:, cols], do_ref[:, cols]
-        value_grads, key_grads = [], []
-        for side in range(2):
-            rows = head_pair(side, pair)
-            scores = dot(key_tile(k_tile, kmark, side), query_tile(qt_ref[rows, :], qmark, side))
-            probs = jnp.exp(scores - lse_ref[0, pl.ds(pair * 2 + side, 1), :])
-            value_grads.append(dot(probs.astype(BF), do_tile))
-            up = dot_ref[rows, :]
-            center = col_sum(up.astype(F32) * ot_ref[rows, :].astype(F32))
-            probs_grad = dot(v_tile, query_tile(up, blank, side))
-            score_grad = (probs * (probs_grad - center)).astype(BF)
-            key_grads.append(dot(score_grad, q_tile))
-            dqt_ref[rows, :] = (dot(kt_ref[rows, :], score_grad) * SCALE).astype(BF)
-        dv_ref[:, cols] = jnp.where(left, value_grads[0], value_grads[1]).astype(BF)
-        dk_ref[:, cols] = jnp.where(left, key_grads[0], key_grads[1]).astype(BF)
-        return carry
-
-    lax.fori_loop(0, PAIRS, one_pair, 0)
+    def begin(head):
+        pair, side = head // 2, head % 2
+        rows = slice(head * HEAD_DIM, (head + 1) * HEAD_DIM)
+        cols = slice(pair * 128, (pair + 1) * 128)
+        scores = dot(key_tile(k_ref[:, cols], kmark, side), query_tile(qt_ref[rows, :], qmark, side))
+        up = dot_ref[rows, :]
+        probs_grad = dot(v_ref[:, cols], query_tile(up, blank, side))
+        return scores, probs_grad, col_sum(up.astype(F32) * ot_ref[rows, :].astype(F32))
+
+    def middle(head, scores, probs_grad, center):
+        probs = jnp.exp(scores - lse_ref[0, head : head + 1, :])
+        return probs.astype(BF), (probs * (probs_grad - center)).astype(BF)
+
+    def finish(head, probs, score_grad):
+        rows = slice(head * HEAD_DIM, (head + 1) * HEAD_DIM)
+        cols = slice(head // 2 * 128, (head // 2 + 1) * 128)
+        dqt_ref[rows, :] = (dot(kt_ref[rows, :], score_grad) * SCALE).astype(BF)
+        return dot(probs, do_ref[:, cols]), dot(score_grad, q_ref[:, cols])
+
+    for start in range(0, HEADS, 4):
+        heads = range(start, start + 4)
+        begun = [begin(head) for head in heads]
+        mid = [middle(head, *b) for head, b in zip(heads, begun)]
+        done = [finish(head, *m) for head, m in zip(heads, mid)]
+        for i in range(0, 4, 2):
+            cols = slice((start + i) // 2 * 128, ((start + i) // 2 + 1) * 128)
+            dv_ref[:, cols] = jnp.where(left, done[i][0], done[i + 1][0]).astype(BF)
+            dk_ref[:, cols] = jnp.where(left, done[i][1], done[i + 1][1]).astype(BF)
 
 
 def self_forward_kernel(
@@ -211,12 +225,15 @@
 
     @pl.when(phase == 0)
     def _():
-        pre = dot(low_s[...], win_ref[0]) + bin_ref[...]
-        hidden, slope = gelu_parts(pre)
-        hidden = hidden.astype(BF)
-        hid_s[chunk] = hidden
-        slope_s[chunk] = slope
-        acc_s[...] += dot(hidden, wout())
+        weights_in, weights_out, count = win_ref[0], wout(), low_s.shape[0] // 4
+        blocks = [slice(i * count, (i + 1) * count) for i in range(4)]
+        pres = [dot(low_s[block, :], weights_in) + bin_ref[...] for block in blocks]
+        both = [gelu_parts(pre) for pre in pres]
+        for block, (hidden, slope) in zip(blocks, both):
+            hidden = hidden.astype(BF)
+            hid_s[chunk, block] = hidden
+            slope_s[chunk, block] = slope
+            acc_s[block, :] += dot(hidden, weights_out)
 
     @pl.when((phase == 1) & (chunk == 0))
     def _():
@@ -331,7 +348,8 @@
 
 
 def cross_weight_kernel(staged, me_ref, *refs):
-    sources, (keep_ref, send_ref, mg_ref), slots = refs[:10], refs[10:13], refs[13:23]
+    sources, (keep_ref, send_ref, mg_ref), slots = list(refs[:10]), refs[10:13], refs[13:23]
+    sources[3] = sources[3].at[pl.ds(0, 3)]
     dw_s, mg_s, sems, out_sem = refs[23:]
     get = bring(sources, slots, sems)
     memt = get(0).T
@@ -477,8 +495,10 @@
     return pl.BlockSpec(array.shape, lambda *_: zeros, pipeline_mode=pl.Buffered(1))
 
 
-def plane(array, index):
-    return pl.BlockSpec((1, *array.shape[1:]), lambda *_: (index, 0, 0), pipeline_mode=pl.Buffered(1))
+def planes(array, start, count):
+    return pl.BlockSpec(
+        (count, *array.shape[1:]), lambda *_: (start // count, 0, 0), pipeline_mode=pl.Buffered(1)
+    )
 
 
 def params(semantics):
@@ -510,7 +530,7 @@
     )(x, wqk, wv, bias, kmark, qmark)
 
 
-def cross_forward(x, mem, sot, wo, w, bias, gain, shift, kmark, qmark):
+def cross_forward(x, mem, sot, wo, wo_at, w, bias, gain, shift, kmark, qmark):
     rows, d = x.shape
     blocks = rows // SEQ_MAX
     act, wide = shape((rows, d), BF), shape((rows, d), F32)
@@ -518,7 +538,8 @@
         cross_forward_kernel,
         grid=(blocks,),
         in_specs=[
-            row_block(d), row_block(d), col_block(d), whole(wo), whole(w), whole(bias), whole(gain), whole(shift),
+            row_block(d), row_block(d), col_block(d), planes(wo, wo_at, 2), planes(w, 0, 3), whole(bias), whole(gain),
+            whole(shift),
             row_block(128), lead_block(HEAD_DIM),
         ],
         out_specs=[row_block(d)] * 5 + [col_block(d), lead_block(16), row_block(d)],
@@ -547,7 +568,7 @@
         grid=(2, chunks),
         in_specs=[
             whole(second_sum), whole(cot),
-            pl.BlockSpec((1, d, width), lambda p, j: (j, 0, 0)),
+            pl.BlockSpec((1, d, width), lambda p, j: (jnp.where(j == 0, 3, 9 + j) if own else j, 0, 0)),
             pl.BlockSpec((1, width), lambda p, j: (0, j)),
             wout_spec, whole(bout), whole(gain), whole(shift),
         ],
@@ -610,11 +631,11 @@
     )(*args, *before)
 
 
-def cross_back(block, before, ssg, first_sum, q, k, v, ot, lse, wo, w, gain, kmark, qmark):
+def cross_back(block, before, wo_at, ssg, first_sum, q, k, v, ot, lse, wo, w, gain, kmark, qmark):
     rows, d = first_sum.shape
     act = shape((rows, d), BF)
     specs = [at_row(block, d)] * 5 + [
-        at_col(block, d), at_lead(block, 16), plane(wo, 1), plane(w, 0), whole(gain), at_row(block, 128), at_lead(block, HEAD_DIM),
+        at_col(block, d), at_lead(block, 16), planes(wo, wo_at + 1, 1), planes(w, 0, 1), whole(gain), at_row(block, 128), at_lead(block, HEAD_DIM),
     ]
     args = (ssg, first_sum, q, k, v, ot, lse, wo, w, gain, kmark, qmark)
     return one_back(
@@ -622,11 +643,11 @@
     )
 
 
-def self_back(block, before, fsg, q, k, v, ot, lse, wo, kmark, qmark):
+def self_back(block, before, wo_at, fsg, q, k, v, ot, lse, wo, kmark, qmark):
     rows, d = fsg.shape
     act = shape((rows, d), BF)
     specs = [at_row(block, d)] * 4 + [
-        at_col(block, d), at_lead(block, 16), plane(wo, 0), at_row(block, 128), at_lead(block, HEAD_DIM),
+        at_col(block, d), at_lead(block, 16), planes(wo, wo_at, 1), at_row(block, 128), at_lead(block, HEAD_DIM),
     ]
     args = (fsg, q, k, v, ot, lse, wo, kmark, qmark)
     return one_back(self_back_kernel, block, before, args, specs, [act, act, act], f"self_back_{block}")
@@ -648,7 +669,7 @@
         in_specs=[pl.BlockSpec(memory_space=pltpu.SMEM)] + [anywhere] * 10,
         out_specs=[here, here, anywhere],
         out_shape=weight_outs(staged, 5, 0, devices, d) + [shape((rows, d), F32)],
-        scratch_shapes=[pltpu.VMEM(a.shape, a.dtype) for a in args] + [
+        scratch_shapes=[pltpu.VMEM((min(a.shape[0], 3), *a.shape[1:]) if a is w else a.shape, a.dtype) for a in args] + [
             pltpu.VMEM((5, d, d), F32), pltpu.VMEM((rows, d), F32), pltpu.SemaphoreType.DMA((10,)),
             pltpu.SemaphoreType.DMA,
         ],
@@ -831,49 +852,36 @@
     return {"bias": rows[0:6], "gain": rows[6:9], "shift": rows[9:12], "bout": rows[12:13], "bin": bin_}
 
 
-def behind(later, earlier):
-    later.out = lax.optimization_barrier((later.out, earlier.out))[0]
-
-
 class Stages:
+    out_at = 8
+
     def __init__(self, proj, out, small, win, wout):
         _, own, d = proj.shape
-        self.chunks = win.shape[1] // d
-        feed_local = jnp.concatenate([win.reshape(own, self.chunks, d).swapaxes(0, 1), wout.reshape(self.chunks, own, d)])
-        self.feed_all = lax.all_gather(feed_local, ("x", "c", "z", "y"), axis=1)
+        panels = win.reshape(own, -1, d).swapaxes(0, 1)
+        rest = jnp.concatenate([proj[3:6], panels[:1], wout.reshape(-1, own, d), out, panels[1:]])
+        self.rest = lax.all_gather(rest, ("x", "c", "z", "y"), axis=1)
         extra = jnp.pad(small[None, None], ((0, 0), (0, 7), (0, d - small.shape[0])))
         self.one = Doubling(proj[:2], jnp.concatenate([proj[2:3], extra], axis=1))
-        self.two = Doubling(proj[3:6], out)
         self.own, self.cut, self.d = own, small.shape[0], d
 
-    def begin(self, value):
-        one, two, own, d = self.one, self.two, self.own, self.d
+    def begin(self):
+        one, own, d = self.one, self.own, self.d
         one.line()
-        behind(two, one)
         one.first()
-        two.line()
         one.second()
-        behind(two, one)
-        two.first()
         left, right = one.core()
         full = {"qk": left.reshape(2, -1, d), "v": right[..., :own, :].reshape(1, -1, d)}
         full.update(spread_small(right[..., own, : self.cut].reshape(-1, self.cut), own))
-        value = after(value, two)
-        two.second()
-        return full, value
-
-    def finish(self, value):
-        two, d = self.two, self.d
-        value = after(value, two)
-        left, right = two.core()
-        shape_f = (2 * self.chunks, -1, d)
-        return {
-            "cross_proj": left.reshape(3, -1, d), "out": right.reshape(2, -1, d),
-            "win": self.feed_all.reshape(shape_f), "wout": self.feed_all,
-        }, value
+        return full
+
+    def finish(self):
+        planes = self.rest.reshape(self.rest.shape[0], -1, self.d)
+        return {"cross_proj": planes, "out": planes, "win": planes, "wout": self.rest}
 
 
 class Plain:
+    out_at = 0
+
     def __init__(self, proj, out, small, win, wout):
         take = functools.partial(lax.all_gather, axis_name=("dp", "fsdp"), tiled=True)
         _, own, d = proj.shape
@@ -883,11 +891,11 @@
         win = take(win, axis=0).reshape(d, -1, d).swapaxes(0, 1)
         self.rest = {"cross_proj": proj[3:], "out": take(out, axis=1), "win": win, "wout": take(wout, axis=0)}
 
-    def begin(self, value):
-        return self.full, value
-
-    def finish(self, value):
-        return self.rest, value
+    def begin(self):
+        return self.full
+
+    def finish(self):
+        return self.rest
 
 
 def body(
@@ -904,15 +912,15 @@
         pair = lax.axis_index("c").reshape(1)
     small = local_small(attn_bias, norm_gain, norm_bias, ffn_in_bias, ffn_out_bias)
     weights = gather(attn_proj, attn_out, small, ffn_in, ffn_out)
-    full, rows_in = weights.begin(query)
+    full = weights.begin()
     bias, gain, shift = full["bias"], full["gain"], full["shift"]
     qmark = query_marks(query_seg)
     smark, cmark = key_marks(query_seg), key_marks(memory_seg)
-    sq, sk, sv, sot, slse = self_forward(rows_in, full["qk"], full["v"], bias, smark, qmark)
-    rest, sot = weights.finish(sot)
+    sq, sk, sv, sot, slse = self_forward(query, full["qk"], full["v"], bias, smark, qmark)
+    rest, out_at = weights.finish(), weights.out_at
     out, cross_proj = rest["out"], rest["cross_proj"]
     first_sum, low, cq, ck, cv, cot_, clse, second_sum = cross_forward(
-        query, memory, sot, out, cross_proj, bias, gain, shift, cmark, qmark
+        query, memory, sot, out, out_at, cross_proj, bias, gain, shift, cmark, qmark
     )
     mixed, ssg, fdw, dbin, small3 = feed(
         second_sum, cotangent, rest["win"], full["bin"], rest["wout"], full["bout"], gain, shift
@@ -921,7 +929,7 @@
     grads, small2 = [], 0
     for block in blocks:
         *grads, part = cross_back(
-            block, grads, ssg, first_sum, cq, ck, cv, cot_, clse, out, cross_proj, gain, cmark, qmark
+            block, grads, out_at, ssg, first_sum, cq, ck, cv, cot_, clse, out, cross_proj, gain, cmark, qmark
         )
         small2 = small2 + part
     fsg, dq, dk, dv = grads
@@ -932,7 +940,7 @@
     upstream = after(fsg, cross_sum)
     grads, small1 = [], 0
     for block in blocks:
-        *grads, part = self_back(block, grads, upstream, sq, sk, sv, sot, slse, out, smark, qmark)
+        *grads, part = self_back(block, grads, out_at, upstream, sq, sk, sv, sot, slse, out, smark, qmark)
         small1 = small1 + part
         if block == 0:
             cross_sum.core()

time: 450 us -> 407 us (0.904)
  Pallas kernels: 219 us -> 200 us
  starting transfers between devices: 45.8 us -> 29.2 us
  other arithmetic: 26.7 us -> 18.6 us
  waiting for transfers between devices: 109 us -> 117 us
  local copies, waits for them, and re-layouts: 28.7 us -> 21.8 us
    all_gather x1, waiting for transfers between devices: 0.02 us -> 48.1 us  [__init__(): self.rest = lax.all_gather(rest, ('x', 'c', 'z', 'y'), axis=1)]
    ppermute x12 -> x6, waiting for transfers between devices: 41 us -> 20.8 us  [take_pair(): got = lax.ppermute(value, name, [(0, 1), (1, 0)])]
    ppermute x6 -> x3, waiting for transfers between devices: 21.9 us -> 6.74 us  [take_turns(): lax.ppermute(value, 'z', [(i, (i + step) % 4) for i in range(4)])]
    ppermute x6 -> x3, starting transfers between devices: 16.6 us -> 7.93 us  [take_turns(): lax.ppermute(value, 'z', [(i, (i + step) % 4) for i in range(4)])]
    pallas_call x1, Pallas kernels: 27.7 us -> 20.3 us  [cross_forward(): pl.pallas_call(cross_forward_kernel, grid=(blocks,), in_specs=[row_block(...]
    pallas_call x1, Pallas kernels: 21.3 us -> 14.5 us  [self_forward(): pl.pallas_call(self_forward_kernel, grid=(blocks,), in_specs=[row_block(d...]
    another operation x24 -> x12, other arithmetic: 15.6 us -> 9.13 us  [take_pair(): jnp.stack([jnp.where(me == 0, value, got), jnp.where(me == 0, got, value)...]
    ppermute x6, starting transfers between devices: 13.2 us -> 7.7 us  [last(): lax.ppermute(out, 'z', [(i, (i + step) % 4) for i in range(4)]).astype(F32)]
  transfers between devices with their start and end apart: 36 -> 27, of which waited for: 17 -> 15; matrix products, arithmetic and copies ran while one was open for 10% -> 7% of each run, Pallas kernels for 37% -> 32%
where the time goes in v1:
time: 407 us; the launch traced here: 401 us
  Pallas kernels  200 us (49%)
  waiting for transfers between devices  117 us (29%)
  starting transfers between devices  29.2 us (7%)
  local copies, waits for them, and re-layouts  21.8 us (5%)
  other arithmetic  18.6 us (5%)
  between operations  15 us (4%)
    pallas_call x4, Pallas kernels, one_back(): pl.pallas_call(kernel, grid=(1,), in_specs=specs + kept, out_specs=[at_ro...  56.5 us
    pallas_call x1, Pallas kernels, feed(): pl.pallas_call(functools.partial(feed_kernel, own), grid=(2, chunks), in_...  50.3 us
    all_gather x1, waiting for transfers between devices, __init__(): self.rest = lax.all_gather(rest, ('x', 'c', 'z', 'y'), axis=1)  48.1 us
    ppermute x10, waiting for transfers between devices, swap(): return lax.ppermute(value, name, [(0, 1), (1, 0)])  32.9 us
    ppermute x6, waiting for transfers between devices, take_pair(): got = lax.ppermute(value, name, [(0, 1), (1, 0)])  20.8 us
    pallas_call x1, Pallas kernels, cross_forward(): pl.pallas_call(cross_forward_kernel, grid=(blocks,), in_specs=[row_block(...  20.3 us
    pallas_call x1, Pallas kernels, cross_weight(): pl.pallas_call(functools.partial(cross_weight_kernel, staged), in_specs=[...  18.2 us
    pallas_call x1, Pallas kernels, self_forward(): pl.pallas_call(self_forward_kernel, grid=(blocks,), in_specs=[row_block(d...  14.5 us
  transfers between devices with their start and end apart: 27, of which 15 were waited for; matrix products, arithmetic and copies ran while one was open for 7% of the time, Pallas kernels for 32%

profile of v1, /device:TPU:0, one launch (start us, length us, event | category | flops | bytes accessed | tf_op | source)
XLA Modules:
  0.0 401.4 jit_solution(12831071993149046161)
XLA Ops:
  12.4 4.1 %collective-permute-start.1 = (bf16[1,80,768]{2,1,0:T(8,128)(2,1)S(1)}, bf16[1,80,768]{2,1,0:T(8,128)(2,1)S(1)}, u32[]{:S(2)}, u32[]{:S(2)}) collective-permute-start(bf16[1,80,768]{2,1,0:T(8,128)(2,1)S(1)} %fusion.9), channel_id=1, source_target_pairs={{0,4},{2,6},{4,0},{6,2},{1,5},{3,7},{5,1},{7,3},{8,12},{10,14},{12... | collective-permute-start | bytes 368648 | tf_op jit(solution)/shard_map/ppermute | solution.py:802
  20.3 5.6 %collective-permute-done.1 = bf16[1,80,768]{2,1,0:T(8,128)(2,1)S(1)} collective-permute-done((bf16[1,80,768]{2,1,0:T(8,128)(2,1)S(1)}, bf16[1,80,768]{2,1,0:T(8,128)(2,1)S(1)}, u32[]{:S(2)}, u32[]{:S(2)}) %collective-permute-start.1) | collective-permute-done | bytes 122912 | tf_op jit(solution)/shard_map/ppermute | solution.py:802
  36.9 4.5 %collective-permute-done.3 = bf16[2,4,24,768]{3,2,1,0:T(8,128)(2,1)S(1)} collective-permute-done((bf16[2,4,24,768]{3,2,1,0:T(8,128)(2,1)S(1)}, bf16[2,4,24,768]{3,2,1,0:T(8,128)(2,1)S(1)}, u32[]{:S(2)}, u32[]{:S(2)}) %collective-permute-start.3) | collective-permute-done | bytes 294944 | tf_op jit(solution)/shard_map/ppermute | solution.py:808
  42.5 4.4 %collective-permute-done.7 = bf16[1,2,4,32,768]{4,2,3,1,0:T(4,128)(2,1)S(1)} collective-permute-done((bf16[1,2,4,32,768]{4,2,3,1,0:T(4,128)(2,1)S(1)}, bf16[1,2,4,32,768]{4,2,3,1,0:T(4,128)(2,1)S(1)}, u32[]{:S(2)}, u32[]{:S(2)}) %collective-permute-start.7) | collective-permute-done | bytes 393248 | tf_op jit(solution)/shard_map/ppermute | solution.py:808
  47.9 10.9 %collective-permute-done.4 = bf16[2,4,2,24,768]{4,3,2,1,0:T(8,128)(2,1)S(1)} collective-permute-done((bf16[2,4,2,24,768]{4,3,2,1,0:T(8,128)(2,1)S(1)}, bf16[2,4,2,24,768]{4,3,2,1,0:T(8,128)(2,1)S(1)}, u32[]{:S(2)}, u32[]{:S(2)}) %collective-permute-start.4) | collective-permute-done | bytes 589856 | tf_op jit(solution)/shard_map/ppermute | solution.py:808
  73.4 14.5 %self_forward.1 = (bf16[1024,768]{1,0:T(8,128)(2,1)}, bf16[1024,768]{1,0:T(8,128)(2,1)}, bf16[1024,768]{1,0:T(8,128)(2,1)}, bf16[768,1024]{1,0:T(8,128)(2,1)}, f32[2,16,512]{2,1,0:T(8,128)}) custom-call(bf16[1024,768]{1,0:T(8,128)(2,1)} %x_ref.5, bf16[2,768,768]{2,1,0:T(8,128)(2,1)} %bitcast.82, bf16[1,768,768]{2,1,0:T(8,128)(2,1)} %bitcast.84, ...), custom_call_target="tpu_custom_call" | custom-call | flops 20000000000 | bytes 12000000 | tf_op jit(solution)/shard_map/self_forward/pallas_call | solution.py:520
  88.0 48.1 %all-gather.3.cloned.1.call-done.wo_ref.w_ref.win_ref.refs_3_ = bf16[13,768,768]{2,1,0:T(8,128)(2,1)} async-done(((bf16[13,24,768]{2,1,0:T(8,128)(2,1)}), bf16[13,768,768]{2,1,0:T(8,128)(2,1)}) %all-gather.3.cloned.1.call-update) | async-done | bytes 15335440 | tf_op jit(solution)/shard_map/all_gather | solution.py:862
  136.0 20.3 %cross_forward.1 = (f32[1024,768]{1,0:T(8,128)}, bf16[1024,768]{1,0:T(8,128)(2,1)}, bf16[1024,768]{1,0:T(8,128)(2,1)}, bf16[1024,768]{1,0:T(8,128)(2,1)}, bf16[1...) custom-call(bf16[1024,768]{1,0:T(8,128)(2,1)} %x_ref.5, ...), custom_call_target="tpu_custom_call" | custom-call | flops 24000000000 | bytes 20000000 | tf_op jit(solution)/shard_map/cross_forward/pallas_call | solution.py:537
  156.4 50.3 %feed.1 = (bf16[1024,768]{1,0:T(8,128)(2,1)}, f32[1024,768]{1,0:T(8,128)}, bf16[768,6144]{1,0:T(8,128)(2,1)}, f32[1,3072]{1,0:T(1,128)}, f32[8,768]{1,0:T(8,128)}) custom-call(f32[1024,768]{1,0:T(8,128)} %get-tuple-element.92.ss_ref, bf16[1024,768]{1,0:T(8,128)(2,1)} %cot_ref.1, ...), custom_call_target="tpu_custom_call" | custom-call | flops 40000000000 | bytes 40000000 | tf_op jit(solution)/shard_map/feed/pallas_call | solution.py:566
  206.7 14.6 %cross_back_0.1 = (f32[1024,768]{1,0:T(8,128)}, bf16[1024,768]{1,0:T(8,128)(2,1)}, bf16[1024,768]{1,0:T(8,128)(2,1)}, bf16[1024,768]{1,0:T(8,128)(2,1)}, f32[8,768]{1,0:T(8,128)}) custom-call(f32[1024,768]{1,0:T(8,128)} %get-tuple-element.94.ssg_ref.refs_5_, f32[1024,768]{1,0:T(8,128)} %get-tuple-element.95.fs_ref, ...), custom_call_target="tpu_custom_call" | custom-call | flops 24999999488 | bytes 15000000 | tf_op jit(solution)/shard_map/cross_back_0/pallas_call | solution.py:620
  221.3 15.4 %cross_back_1.1 = (f32[1024,768]{1,0:T(8,128)}, bf16[1024,768]{1,0:T(8,128)(2,1)}, bf16[1024,768]{1,0:T(8,128)(2,1)}, bf16[1024,768]{1,0:T(8,128)(2,1)}, f32[8,768]{1,0:T(8,128)}) custom-call(f32[1024,768]{1,0:T(8,128)} %get-tuple-element.94.ssg_ref.refs_5_, ...), custom_call_target="tpu_custom_call", output_to_operand_aliasing={{0}: (12, {}), {1}: (13, {}), {2}: (14, {}), {3}: (15, {})} | custom-call | flops 24999999488 | bytes 15000000 | tf_op jit(solution)/shard_map/cross_back_1/pallas_call | solution.py:620
  236.6 18.2 %cross_weight.1 = (bf16[2,4,2,120,768]{4,3,2,1,0:T(8,128)(2,1)}, bf16[2,4,2,120,768]{4,3,2,1,0:T(8,128)(2,1)}, f32[1024,768]{1,0:T(8,128)}) custom-call(s32[1]{0:T(128)} %bitcast.34.me_ref, bf16[1024,768]{1,0:T(8,128)(2,1)} %refs_0_.1, bf16[1024,768]{1,0:T(8,128)(2,1)} %get-tuple-element.106.refs_1_, bf16[1024,768]{1,0:T(8,128)(2,1)} %get-tuple-element.107.refs_2_, ...), custom_call_target="tpu_custom_call" | custom-call | flops 8999999488 | bytes 20000000 | tf_op jit(solution)/shard_map/cross_weight/pallas_call | solution.py:667
  255.8 13.7 %self_back_0.1 = (bf16[1024,768]{1,0:T(8,128)(2,1)}, bf16[1024,768]{1,0:T(8,128)(2,1)}, bf16[1024,768]{1,0:T(8,128)(2,1)}, f32[8,768]{1,0:T(8,128)}) custom-call(f32[1024,768]{1,0:T(8,128)} %get-tuple-element.151.refs_7_.fsg_ref, bf16[1024,768]{1,0:T(8,128)(2,1)} %get-tuple-element.112.q_ref, bf16[1024,768]{1,0:T(8,128)(2,1)} %get-tuple-element.113.k_ref, ...), custom_call_target="tpu_custom_call" | custom-call | flops 24999999488 | bytes 15000000 | tf_op jit(solution)/shard_map/self_back_0/pallas_call | solution.py:620
  271.0 5.2 %first_stage.2 = (bf16[4,2,120,384]{3,2,1,0:T(8,128)(2,1)}, bf16[4,2,120,384]{3,2,1,0:T(8,128)(2,1)}, bf16[2,4,120,384]{3,2,1,0:T(8,128)(2,1)}, bf16[2,4,120,384]{3,2,1,0:T(8,128)(2,1)}) custom-call(s32[3]{0:T(128)} %pad_add_fusion.me_ref, bf16[2,4,2,120,768]{4,3,2,1,0:T(8,128)(2,1)} %get-tuple-element.117.keep_ref, bf16[2,4,2,120,768]{4,3,2,1,0:T(8,128)(2,1)} %copy-done), custom_call_target="tpu_custom_call" | custom-call | flops 1474560 | bytes 8847360 | tf_op jit(solution)/shard_map/first_stage/pallas_call | solution.py:469
  277.8 12.9 %self_back_1.1 = (bf16[1024,768]{1,0:T(8,128)(2,1)}, bf16[1024,768]{1,0:T(8,128)(2,1)}, bf16[1024,768]{1,0:T(8,128)(2,1)}, f32[8,768]{1,0:T(8,128)}) custom-call(f32[1024,768]{1,0:T(8,128)} %get-tuple-element.151.refs_7_.fsg_ref, bf16[1024,768]{1,0:T(8,128)(2,1)} %get-tuple-element.112.q_ref, ...), custom_call_target="tpu_custom_call", output_to_operand_aliasing={{0}: (9, {}), {1}: (10, {}), {2}: (11, {})} | custom-call | flops 24999999488 | bytes 15000000 | tf_op jit(solution)/shard_map/self_back_1/pallas_call | solution.py:620
  292.1 11.4 %collective-permute-done.10.gl_ref = bf16[4,2,120,384]{3,2,1,0:T(8,128)(2,1)S(1)} collective-permute-done((bf16[4,2,120,384]{3,2,1,0:T(8,128)(2,1)}, bf16[4,2,120,384]{3,2,1,0:T(8,128)(2,1)S(1)}, u32[]{:S(2)}, u32[]{:S(2)}) %collective-permute-start.10) | collective-permute-done | bytes 737312 | tf_op jit(solution)/shard_map/ppermute | solution.py:727
  305.5 3.1 second_stage.2
  308.6 11.0 %self_weight.1 = (bf16[2,4,2,104,768]{4,3,2,1,0:T(8,128)(2,1)}, bf16[2,4,2,104,768]{4,3,2,1,0:T(8,128)(2,1)}) custom-call(s32[1]{0:T(128)} %bitcast.34.me_ref, f32[24,768]{1,0:T(8,128)} %pad_maximum_fusion.8.small_ref, f32[1,3072]{1,0:T(1,128)} %get-tuple-element.129.dbin_ref, bf16[1024,768]{1,0:T(8,128)(2,1)} %x_ref.5, ...), custom_call_target="tpu_custom_call" | custom-call | flops 4000000000 | bytes 10000000 | tf_op jit(solution)/shard_map/self_weight/pallas_call | solution.py:686
  321.4 9.3 %collective-permute-done.13.gl_ref = bf16[4,120,384]{2,1,0:T(8,128)(2,1)S(1)} collective-permute-done((bf16[4,120,384]{2,1,0:T(8,128)(2,1)S(1)}, bf16[4,120,384]{2,1,0:T(8,128)(2,1)S(1)}, u32[]{:S(2)}, u32[]{:S(2)}) %collective-permute-start.13) | collective-permute-done | bytes 368672 | tf_op jit(solution)/shard_map/ppermute | solution.py:727
  335.5 4.6 %first_stage.3 = (bf16[4,2,104,384]{3,2,1,0:T(8,128)(2,1)}, bf16[4,2,104,384]{3,2,1,0:T(8,128)(2,1)}, bf16[2,4,104,384]{3,2,1,0:T(8,128)(2,1)}, bf16[2,4,104,384]{3,2,1,0:T(8,128)(2,1)}) custom-call(s32[3]{0:T(128)} %pad_add_fusion.me_ref, bf16[2,4,2,104,768]{4,3,2,1,0:T(8,128)(2,1)} %get-tuple-element.140.keep_ref, bf16[2,4,2,104,768]{4,3,2,1,0:T(8,128)(2,1)} %copy-done.1), custom_call_target="tpu_custom_call" | custom-call | flops 1277952 | bytes 7667712 | tf_op jit(solution)/shard_map/first_stage/pallas_call | solution.py:469
  346.0 10.4 %collective-permute-done.15.gl_ref = bf16[4,2,104,384]{3,2,1,0:T(8,128)(2,1)S(1)} collective-permute-done((bf16[4,2,104,384]{3,2,1,0:T(8,128)(2,1)}, bf16[4,2,104,384]{3,2,1,0:T(8,128)(2,1)S(1)}, u32[]{:S(2)}, u32[]{:S(2)}) %collective-permute-start.15) | collective-permute-done | bytes 639008 | tf_op jit(solution)/shard_map/ppermute | solution.py:727
  363.1 8.7 %self_input.1 = f32[1024,768]{1,0:T(8,128)} custom-call(f32[1024,768]{1,0:T(8,128)} %get-tuple-element.151.refs_7_.fsg_ref, bf16[1024,768]{1,0:T(8,128)(2,1)} %get-tuple-element.137.dq_ref, bf16[1024,768]{1,0:T(8,128)(2,1)} %get-tuple-element.138.dk_ref, bf16[1024,768]{1,0:T(8,128)(2,1)} %get-tuple-element.139.dv_ref, bf16[2,768,768]{2,1,0:T(8,128)(2,1)} %bitcast.83, ...), custom_call_target="tpu_custom_call" | custom-call | flops 4000000000 | bytes 14000000 | tf_op jit(solution)/shard_map/self_input/pallas_call | solution.py:702
  379.6 4.5 %collective-permute-done.19 = bf16[104,768]{1,0:T(8,128)(2,1)S(1)} collective-permute-done((bf16[104,768]{1,0:T(8,128)(2,1)}, bf16[104,768]{1,0:T(8,128)(2,1)S(1)}, u32[]{:S(2)}, u32[]{:S(2)}) %collective-permute-start.19) | collective-permute-done | bytes 159776 | tf_op jit(solution)/shard_map/ppermute | solution.py:759
  384.1 3.7 collective-permute-done.20
  (191 shorter events, 77.2 us)
Async XLA Ops:
  7.3 128.8 %all-gather.3.cloned.1.call-start = ((), (), s32[]{:S(2)}) async-start(), calls=%async_computation.2 | async-start | bytes 15814656 | tf_op jit(solution)/shard_map/all_gather | solution.py:862
  11.9 379.6 %reduce-scatter.2.cloned.1.call-start = ((), (), s32[]{:S(2)}) async-start(), calls=%async_computation.1 | async-start | bytes 9732096 | tf_op jit(solution)/shard_map/reduce_scatter | solution.py:764
  12.4 13.6 %collective-permute-start.1 = (bf16[1,80,768]{2,1,0:T(8,128)(2,1)S(1)}, bf16[1,80,768]{2,1,0:T(8,128)(2,1)S(1)}, u32[]{:S(2)}, u32[]{:S(2)}) collective-permute-start(bf16[1,80,768]{2,1,0:T(8,128)(2,1)S(1)} %fusion.9), channel_id=1, source_target_pairs={{0,4},{2,6},{4,0},{6,2},{1,5},{3,7},{5,1},{7,3},{8,12},{10,14},{12... | collective-permute-start | bytes 368648 | tf_op jit(solution)/shard_map/ppermute | solution.py:802
  16.5 9.5 %collective-permute-start.2 = (bf16[1,80,768]{2,1,0:T(8,128)(2,1)S(1)}, bf16[1,80,768]{2,1,0:T(8,128)(2,1)S(1)}, u32[]{:S(2)}, u32[]{:S(2)}) collective-permute-start(bf16[1,80,768]{2,1,0:T(8,128)(2,1)S(1)} %fusion.9), channel_id=1, source_target_pairs={{0,2},{2,4},{4,6},{6,0},{1,3},{3,5},{5,7},{7,1},{8,10},{10,12},{12... | collective-permute-start | bytes 368648 | tf_op jit(solution)/shard_map/ppermute | solution.py:802
  31.6 9.9 %collective-permute-start.3 = (bf16[2,4,24,768]{3,2,1,0:T(8,128)(2,1)S(1)}, bf16[2,4,24,768]{3,2,1,0:T(8,128)(2,1)S(1)}, u32[]{:S(2)}, u32[]{:S(2)}) collective-permute-start(bf16[2,4,24,768]{3,2,1,0:T(8,128)(2,1)S(1)} %bitcast.99), channel_id=1, source_target_pairs={{0,1},{1,0},{2,3},{3,2},{4,5},{5,4},{6,7},{7,6},{8,9},{9,8},{10,11... | collective-permute-start | bytes 884744 | tf_op jit(solution)/shard_map/ppermute | solution.py:808
  35.1 11.7 %collective-permute-start.7 = (bf16[1,2,4,32,768]{4,2,3,1,0:T(4,128)(2,1)S(1)}, bf16[1,2,4,32,768]{4,2,3,1,0:T(4,128)(2,1)S(1)}, u32[]{:S(2)}, u32[]{:S(2)}) collective-permute-start(bf16[1,2,4,32,768]{4,2,3,1,0:T(4,128)(2,1)S(1)} %pad_maximum_fusion.6), channel_id=1, source_target_pairs={{0,1},{1,0},{2,3},{3,2},{4,5},{5,4},{6,7},{7,6},{8,9},{9,8},{10,11... | collective-permute-start | bytes 1179656 | tf_op jit(solution)/shard_map/ppermute | solution.py:808
  41.6 17.2 %collective-permute-start.4 = (bf16[2,4,2,24,768]{4,3,2,1,0:T(8,128)(2,1)S(1)}, bf16[2,4,2,24,768]{4,3,2,1,0:T(8,128)(2,1)S(1)}, u32[]{:S(2)}, u32[]{:S(2)}) collective-permute-start(bf16[2,4,2,24,768]{4,3,2,1,0:T(8,128)(2,1)S(1)} %pad_maximum_fusion.3), channel_id=1, source_target_pairs={{0,16},{16,0},{1,17},{17,1},{2,18},{18,2},{3,19},{19,3},{4,20},{20... | collective-permute-start | bytes 1769480 | tf_op jit(solution)/shard_map/ppermute | solution.py:808
  47.8 14.3 %collective-permute-start.8 = (bf16[1,2,4,2,32,768]{5,2,4,3,1,0:T(4,128)(2,1)S(1)}, bf16[1,2,4,2,32,768]{5,2,4,3,1,0:T(4,128)(2,1)}, u32[]{:S(2)}, u32[]{:S(2)}) collective-permute-start(bf16[1,2,4,2,32,768]{5,2,4,3,1,0:T(4,128)(2,1)S(1)} %pad_maximum_fusion.2), channel_id=1, source_target_pairs={{0,8},{8,0},{1,9},{9,1},{2,10},{10,2},{3,11},{11,3},{4,12},{12,4},... | collective-permute-start | bytes 2359304 | tf_op jit(solution)/shard_map/ppermute | solution.py:808
  60.0 10.3 %collective-permute-start.5 = (bf16[2,2,4,2,24,768]{5,4,3,2,1,0:T(8,128)(2,1)}, bf16[2,2,4,2,24,768]{5,4,3,2,1,0:T(8,128)(2,1)}, u32[]{:S(2)}, u32[]{:S(2)}) collective-permute-start(bf16[2,2,4,2,24,768]{5,4,3,2,1,0:T(8,128)(2,1)} %pad_maximum_fusion.1), channel_id=1, source_target_pairs={{0,8},{8,0},{1,9},{9,1},{2,10},{10,2},{3,11},{11,3},{4,12},{12,4},... | collective-permute-start | bytes 3538952 | tf_op jit(solution)/shard_map/ppermute | solution.py:808
  254.8 14.6 %collective-permute-start.9 = (bf16[2,4,2,120,768]{4,3,2,1,0:T(8,128)(2,1)}, bf16[2,4,2,120,768]{4,3,2,1,0:T(8,128)(2,1)S(1)}, u32[]{:S(2)}, u32[]{:S(2)}) collective-permute-start(bf16[2,4,2,120,768]{4,3,2,1,0:T(8,128)(2,1)} %get-tuple-element.118), channel_id=1, source_target_pairs={{0,8},{8,0},{1,9},{9,1},{2,10},{10,2},{3,11},{11,3},{4,12},{12,4},... | collective-permute-start | bytes 8847368 | tf_op jit(solution)/shard_map/ppermute | solution.py:727
  276.2 27.2 %collective-permute-start.10 = (bf16[4,2,120,384]{3,2,1,0:T(8,128)(2,1)}, bf16[4,2,120,384]{3,2,1,0:T(8,128)(2,1)S(1)}, u32[]{:S(2)}, u32[]{:S(2)}) collective-permute-start(bf16[4,2,120,384]{3,2,1,0:T(8,128)(2,1)} %get-tuple-element.132), channel_id=1, source_target_pairs={{0,16},{16,0},{1,17},{17,1},{2,18},{18,2},{3,19},{19,3},{4,20},{20... | collective-permute-start | bytes 2211848 | tf_op jit(solution)/shard_map/ppermute | solution.py:727
  277.7 26.9 %collective-permute-start.11 = (bf16[2,4,120,384]{3,2,1,0:T(8,128)(2,1)}, bf16[2,4,120,384]{3,2,1,0:T(8,128)(2,1)S(1)}, u32[]{:S(2)}, u32[]{:S(2)}) collective-permute-start(bf16[2,4,120,384]{3,2,1,0:T(8,128)(2,1)} %get-tuple-element.134), channel_id=1, source_target_pairs={{0,1},{1,0},{2,3},{3,2},{4,5},{5,4},{6,7},{7,6},{8,9},{9,8},{10,11... | collective-permute-start | bytes 2211848 | tf_op jit(solution)/shard_map/ppermute | solution.py:727
  319.6 14.4 %collective-permute-start.12 = (bf16[2,4,2,104,768]{4,3,2,1,0:T(8,128)(2,1)}, bf16[2,4,2,104,768]{4,3,2,1,0:T(8,128)(2,1)S(1)}, u32[]{:S(2)}, u32[]{:S(2)}) collective-permute-start(bf16[2,4,2,104,768]{4,3,2,1,0:T(8,128)(2,1)} %get-tuple-element.141), channel_id=1, source_target_pairs={{0,8},{8,0},{1,9},{9,1},{2,10},{10,2},{3,11},{11,3},{4,12},{12,4},... | collective-permute-start | bytes 7667720 | tf_op jit(solution)/shard_map/ppermute | solution.py:727
  319.7 11.0 %collective-permute-start.13 = (bf16[4,120,384]{2,1,0:T(8,128)(2,1)S(1)}, bf16[4,120,384]{2,1,0:T(8,128)(2,1)S(1)}, u32[]{:S(2)}, u32[]{:S(2)}) collective-permute-start(bf16[4,120,384]{2,1,0:T(8,128)(2,1)S(1)} %copy-done.24), channel_id=1, source_target_pairs={{0,1},{1,0},{2,3},{3,2},{4,5},{5,4},{6,7},{7,6},{8,9},{9,8},{10,11... | collective-permute-start | bytes 1105928 | tf_op jit(solution)/shard_map/ppermute | solution.py:727
  319.9 10.9 %collective-permute-start.14 = (bf16[4,120,384]{2,1,0:T(8,128)(2,1)S(1)}, bf16[4,120,384]{2,1,0:T(8,128)(2,1)S(1)}, u32[]{:S(2)}, u32[]{:S(2)}) collective-permute-start(bf16[4,120,384]{2,1,0:T(8,128)(2,1)S(1)} %copy-done.23), channel_id=1, source_target_pairs={{0,16},{16,0},{1,17},{17,1},{2,18},{18,2},{3,19},{19,3},{4,20},{20... | collective-permute-start | bytes 1105928 | tf_op jit(solution)/shard_map/ppermute | solution.py:727
  340.1 16.3 %collective-permute-start.15 = (bf16[4,2,104,384]{3,2,1,0:T(8,128)(2,1)}, bf16[4,2,104,384]{3,2,1,0:T(8,128)(2,1)S(1)}, u32[]{:S(2)}, u32[]{:S(2)}) collective-permute-start(bf16[4,2,104,384]{3,2,1,0:T(8,128)(2,1)} %get-tuple-element.154), channel_id=1, source_target_pairs={{0,16},{16,0},{1,17},{17,1},{2,18},{18,2},{3,19},{19,3},{4,20},{20... | collective-permute-start | bytes 1916936 | tf_op jit(solution)/shard_map/ppermute | solution.py:727
  341.4 15.6 %collective-permute-start.16 = (bf16[2,4,104,384]{3,2,1,0:T(8,128)(2,1)}, bf16[2,4,104,384]{3,2,1,0:T(8,128)(2,1)S(1)}, u32[]{:S(2)}, u32[]{:S(2)}) collective-permute-start(bf16[2,4,104,384]{3,2,1,0:T(8,128)(2,1)} %get-tuple-element.156), channel_id=1, source_target_pairs={{0,1},{1,0},{2,3},{3,2},{4,5},{5,4},{6,7},{7,6},{8,9},{9,8},{10,11... | collective-permute-start | bytes 1916936 | tf_op jit(solution)/shard_map/ppermute | solution.py:727
  342.2 34.2 %collective-permute-start.22 = (bf16[120,768]{1,0:T(8,128)(2,1)S(1)}, bf16[120,768]{1,0:T(8,128)(2,1)S(1)}, u32[]{:S(2)}, u32[]{:S(2)}) collective-permute-start(bf16[120,768]{1,0:T(8,128)(2,1)S(1)} %copy-done.27), channel_id=1, source_target_pairs={{0,2},{2,4},{4,6},{6,0},{1,3},{3,5},{5,7},{7,1},{8,10},{10,12},{12... | collective-permute-start | bytes 552968 | tf_op jit(solution)/shard_map/ppermute | solution.py:759
  342.2 36.6 %collective-permute-start.23 = (bf16[120,768]{1,0:T(8,128)(2,1)S(1)}, bf16[120,768]{1,0:T(8,128)(2,1)S(1)}, u32[]{:S(2)}, u32[]{:S(2)}) collective-permute-start(bf16[120,768]{1,0:T(8,128)(2,1)S(1)} %copy-done.26), channel_id=1, source_target_pairs={{0,4},{2,6},{4,0},{6,2},{1,5},{3,7},{5,1},{7,3},{8,12},{10,14},{12... | collective-permute-start | bytes 552968 | tf_op jit(solution)/shard_map/ppermute | solution.py:759
  343.9 34.8 %collective-permute-start.24 = (bf16[120,768]{1,0:T(8,128)(2,1)S(1)}, bf16[120,768]{1,0:T(8,128)(2,1)S(1)}, u32[]{:S(2)}, u32[]{:S(2)}) collective-permute-start(bf16[120,768]{1,0:T(8,128)(2,1)S(1)} %copy-done.25), channel_id=1, source_target_pairs={{0,6},{2,0},{4,2},{6,4},{1,7},{3,1},{5,3},{7,5},{8,14},{10,8},{12,... | collective-permute-start | bytes 552968 | tf_op jit(solution)/shard_map/ppermute | solution.py:759
  360.8 11.1 %collective-permute-start.17 = (bf16[4,104,384]{2,1,0:T(8,128)(2,1)}, bf16[4,104,384]{2,1,0:T(8,128)(2,1)S(1)}, u32[]{:S(2)}, u32[]{:S(2)}) collective-permute-start(bf16[4,104,384]{2,1,0:T(8,128)(2,1)} %get-tuple-element.158), channel_id=1, source_target_pairs={{0,1},{1,0},{2,3},{3,2},{4,5},{5,4},{6,7},{7,6},{8,9},{9,8},{10,11... | collective-permute-start | bytes 958472 | tf_op jit(solution)/shard_map/ppermute | solution.py:727
  361.6 10.2 %collective-permute-start.18 = (bf16[4,104,384]{2,1,0:T(8,128)(2,1)}, bf16[4,104,384]{2,1,0:T(8,128)(2,1)S(1)}, u32[]{:S(2)}, u32[]{:S(2)}) collective-permute-start(bf16[4,104,384]{2,1,0:T(8,128)(2,1)} %get-tuple-element.160), channel_id=1, source_target_pairs={{0,16},{16,0},{1,17},{17,1},{2,18},{18,2},{3,19},{19,3},{4,20},{20... | collective-permute-start | bytes 958472 | tf_op jit(solution)/shard_map/ppermute | solution.py:727
  374.9 12.8 %collective-permute-start.20 = (bf16[104,768]{1,0:T(8,128)(2,1)}, bf16[104,768]{1,0:T(8,128)(2,1)S(1)}, u32[]{:S(2)}, u32[]{:S(2)}) collective-permute-start(bf16[104,768]{1,0:T(8,128)(2,1)} %get-tuple-element.163), channel_id=1, source_target_pairs={{0,4},{2,6},{4,0},{6,2},{1,5},{3,7},{5,1},{7,3},{8,12},{10,14},{12... | collective-permute-start | bytes 479240 | tf_op jit(solution)/shard_map/ppermute | solution.py:759
  376.4 11.4 %collective-permute-start.21 = (bf16[104,768]{1,0:T(8,128)(2,1)}, bf16[104,768]{1,0:T(8,128)(2,1)S(1)}, u32[]{:S(2)}, u32[]{:S(2)}) collective-permute-start(bf16[104,768]{1,0:T(8,128)(2,1)} %get-tuple-element.164), channel_id=1, source_target_pairs={{0,6},{2,0},{4,2},{6,4},{1,7},{3,1},{5,3},{7,5},{8,14},{10,8},{12,... | collective-permute-start | bytes 479240 | tf_op jit(solution)/shard_map/ppermute | solution.py:759
  (33 other events, 228.9 us)
Sparse Core Ops, SparseCore 0:
  12.0 123.9 all-gather.2
  206.8 151.9 reduce-scatter.1

commit v2 on v1

--- a/solution.py
+++ b/solution.py
@@ -330,78 +330,127 @@
     return get
 
 
-def split_out(grads, me, keep_ref, send_ref, small=None):
-    places = keep_ref.shape[1] * keep_ref.shape[2]
-    own = grads[0].shape[0] // (4 * places)
+def lay_out(out_s, at, grads, more=None):
+    places = out_s.shape[2] * out_s.shape[3]
+    d = out_s.shape[5]
+    own = d // (4 * places)
+    for quarter in range(4):
+        first = quarter * places
+        parts = [g[first * own : (first + places) * own].reshape(places, own, d) for g in grads]
+        if more is not None:
+            parts.append(jnp.stack([more(first + i) for i in range(places)]))
+        rows = jnp.concatenate(parts, axis=1).astype(BF)
+        count = rows.shape[1]
+        out_s[quarter // 2, quarter % 2, :, :, at : at + count] = rows.reshape(*out_s.shape[2:4], count, d)
+
+
+def hand_out(out_s, me, keep_ref, send_ref, sems):
+    moves = []
     for x in range(2):
-        cores = []
-        for core in range(2):
-            rows = pl.ds((2 * x + core) * places * own, places * own)
-            parts = [g[rows, :].reshape(places, own, g.shape[1]) for g in grads]
-            if small is not None:
-                parts.append(small(x, core))
-            cores.append(jnp.concatenate(parts, axis=1))
-        mine = me == 0
-        block = keep_ref.shape[1:]
-        keep_ref[x] = jnp.where(mine, cores[0], cores[1]).astype(BF).reshape(block)
-        send_ref[x] = jnp.where(mine, cores[1], cores[0]).astype(BF).reshape(block)
+        moves.append(pltpu.make_async_copy(out_s.at[x, me], keep_ref.at[x], sems.at[2 * x]))
+        moves.append(pltpu.make_async_copy(out_s.at[x, 1 - me], send_ref.at[x], sems.at[2 * x + 1]))
+    for move in moves:
+        move.start()
+    return moves
 
 
 def cross_weight_kernel(staged, me_ref, *refs):
-    sources, (keep_ref, send_ref, mg_ref), slots = list(refs[:10]), refs[10:13], refs[13:23]
-    sources[3] = sources[3].at[pl.ds(0, 3)]
-    dw_s, mg_s, sems, out_sem = refs[23:]
+    sources, (keep_ref, send_ref), slots = refs[:9], refs[9:11], refs[11:20]
+    out_s, sems, out_sems = refs[20:]
     get = bring(sources, slots, sems)
     memt = get(0).T
     dk = get(1)
-    dw_s[3] = dot(memt, dk)
+    keys = dot(memt, dk)
     dv = get(2)
-    dw_s[4] = dot(memt, dv)
-    get(3)
-    w_s = slots[3]
-    mg_s[...] = dot_nt(dk, w_s[1]) + dot_nt(dv, w_s[2])
-    move = pltpu.make_async_copy(mg_s, mg_ref, out_sem)
-    move.start()
-    dw_s[0] = dot(get(4), get(5).astype(BF))
-    dw_s[1] = dot(get(6), get(7).astype(BF))
-    dw_s[2] = dot(get(8).T, get(9))
+    values = dot(memt, dv)
     if staged:
-        split_out([dw_s.at[i] for i in range(5)], me_ref[0], keep_ref, send_ref)
+        lay_out(out_s, 0, [keys, values])
     else:
-        keep_ref[...] = dw_s[...].astype(BF)
-        send_ref[...] = jnp.zeros(send_ref.shape, BF)
-    move.wait()
-
-
-def self_weight_kernel(staged, me_ref, small_ref, dbin_ref, x_ref, dq_ref, dk_ref, dv_ref, keep_ref, send_ref, *scratch):
-    dw_s, sems = scratch[4:]
-    get = bring((x_ref, dq_ref, dk_ref, dv_ref), scratch[:4], sems)
-    xt = get(0).T
-    for i in range(3):
-        dw_s[i] = dot(xt, get(i + 1))
+        out_s[0], out_s[1] = keys.astype(BF), values.astype(BF)
+    outs = [dot(get(3), get(4).astype(BF)), dot(get(5), get(6).astype(BF))]
+    if staged:
+        lay_out(out_s, 2 * outs[0].shape[0] // 32, outs)
+    else:
+        out_s[2], out_s[3] = outs[0].astype(BF), outs[1].astype(BF)
+    queries = dot(get(7).T, get(8))
+    if staged:
+        lay_out(out_s, 4 * outs[0].shape[0] // 32, [queries])
+        moves = hand_out(out_s, me_ref[0], keep_ref, send_ref, out_sems)
+    else:
+        out_s[4] = queries.astype(BF)
+        send_ref[0] = 0
+        moves = [pltpu.make_async_copy(out_s, keep_ref, out_sems.at[0])]
+        moves[0].start()
+    for move in moves:
+        move.wait()
+
+
+def self_last_kernel(
+    staged, me_ref, fsg_ref, q_ref, k_ref, v_ref, ot_ref, lse_ref, wo_ref, kmark_ref, qmark_ref, sums_ref, dbin_ref, x_ref,
+    *refs,
+):
+    (keep_ref, send_ref), outs = refs[3:5], refs[5:8]
+    qt_s, kt_s, do_s, dot_s, dqt_s, dq_s, dk_s, dv_s, x_s, out_s, sems, out_sems = refs[8:]
+    grads = (dq_s, dk_s, dv_s)
+    before = x_s.shape[0] - SEQ_MAX
+    mine = pl.ds(before, SEQ_MAX)
+    loads = [pltpu.make_async_copy(x_ref, x_s, sems.at[0])]
+    if before:
+        early = pl.ds(0, before)
+        loads += [
+            pltpu.make_async_copy(o.at[early], g.at[early], sems.at[1 + i]) for i, (o, g) in enumerate(zip(outs, grads))
+        ]
+    for load in loads:
+        load.start()
+    branch = fsg_ref[...].astype(BF)
+    mixed_grad = dot_nt(branch, wo_ref[0]).astype(BF)
+    do_s[...] = mixed_grad
+    dot_s[...] = mixed_grad.T
+    qt_s[...] = q_ref[...].T
+    kt_s[...] = k_ref[...].T
+    attend_back_block(
+        q_ref, k_ref, v_ref, qt_s, kt_s, ot_ref, do_s, dot_s, kmark_ref, qmark_ref, lse_ref, dqt_s,
+        dk_s.at[mine], dv_s.at[mine],
+    )
+    dq_s[mine] = dqt_s[...].T
+    moves = [
+        pltpu.make_async_copy(g.at[mine], o.at[mine], sems.at[4 + i]) for i, (g, o) in enumerate(zip(grads, outs))
+    ]
+    for load in loads:
+        load.wait()
+    for move in moves:
+        move.start()
+    last = [col_sum(dq_s[mine].astype(F32)), col_sum(dv_s[mine].astype(F32)), col_sum(branch.astype(F32))]
+    sums = sums_ref[...] + place_rows(last, 16)
+    xt = x_s[...].T
     if not staged:
-        keep_ref[...] = dw_s[...].astype(BF)
-        send_ref[...] = jnp.zeros(send_ref.shape, BF)
-        return
-    d = small_ref.shape[1]
-    places = keep_ref.shape[1] * keep_ref.shape[2]
-    own = d // (4 * places)
-    wide = dbin_ref.shape[1]
-
-    lines = jnp.broadcast_to(dbin_ref[...], (8, wide))
-
-    def small(x, core):
-        out = []
-        for place in range(places):
-            device = (2 * x + core) * places + place
-            rows, line = small_ref[...], lines
+        for i in range(3):
+            out_s[i] = dot(xt, grads[i][...]).astype(BF)
+        send_ref[...] = sums
+        moves.append(pltpu.make_async_copy(out_s, keep_ref, out_sems.at[0]))
+        moves[-1].start()
+    else:
+        d, wide = sums_ref.shape[1], dbin_ref.shape[1]
+        lines = jnp.broadcast_to(dbin_ref[...], (8, wide))
+        last_row = lax.broadcasted_iota(jnp.int32, (16, d), 0) == 15
+
+        def small(device):
+            rows, line = sums, lines
             if device:
-                rows = pltpu.roll(rows, d - own * device, 1)
-                line = pltpu.roll(lines, wide - wide // (4 * places) * device, 1)
-            out.append(jnp.concatenate([rows, line[:, :d]], axis=0))
-        return jnp.stack(out)
-
-    split_out([dw_s.at[i] for i in range(3)], me_ref[0], keep_ref, send_ref, small)
+                rows = pltpu.roll(rows, d - d // 32 * device, 1)
+                line = pltpu.roll(lines, wide - wide // 32 * device, 1)
+            line = line[:, :d]
+            return jnp.where(last_row, jnp.concatenate([line, line], axis=0), rows)
+
+        lay_out(out_s, 0, [dot(xt, dq_s[...]), dot(xt, dk_s[...])])
+        lay_out(out_s, 2 * d // 32, [dot(xt, dv_s[...])], small)
+        moves += hand_out(out_s, me_ref[0], keep_ref, send_ref, out_sems)
+    for move in moves:
+        move.wait()
+
+
+def memory_input_kernel(dk_ref, dv_ref, wk_ref, wv_ref, mg_ref):
+    mg_ref[...] = dot_nt(dk_ref[...], wk_ref[0]) + dot_nt(dv_ref[...], wv_ref[0])
 
 
 def self_input_kernel(fsg_ref, dq_ref, dk_ref, dv_ref, wqk_ref, wv_ref, qg_ref):
@@ -445,6 +494,24 @@
             index < 2, jnp.where(index == 0, total[0], total[1]), jnp.where(index == 2, total[2], total[3])
         )
         ref[...] = value.astype(ref.dtype)
+
+
+def final_stage_kernel(own, *refs):
+    cross_refs, self_refs, outs = refs[:4], refs[4:8], refs[8:]
+    proj_ref, out_ref, bias_ref, gain_ref, shift_ref, hidden_ref, last_ref = outs
+    cross = functools.reduce(jnp.add, [r[...].astype(F32) for r in cross_refs])
+    selfs = functools.reduce(jnp.add, [r[...].astype(F32) for r in self_refs])
+    for i in range(3):
+        proj_ref[i] = selfs[i * own : (i + 1) * own]
+    for ref, index, at in ((proj_ref, 4, 0), (proj_ref, 5, 1), (out_ref, 1, 2), (out_ref, 0, 3), (proj_ref, 3, 4)):
+        ref[index] = cross[at * own : (at + 1) * own]
+    sums = selfs[3 * own : 3 * own + 16, :128]
+    bias_ref[...] = sums[0:6, :own]
+    for ref, lines in ((gain_ref, (6, 11, 8)), (shift_ref, (7, 12, 9))):
+        for i, line in enumerate(lines):
+            ref[i : i + 1] = sums[line : line + 1, :own]
+    hidden_ref[...] = sums[15:16, : hidden_ref.shape[1]]
+    last_ref[...] = sums[10:11, :own]
 
 
 def stage_call(kernel, me, args, outs, name):
@@ -655,23 +722,25 @@
 
 def weight_outs(staged, count, extra, devices, d):
     if not staged:
-        return [shape((count, d, d), BF), shape((8, 128), BF)]
-    half = shape((2, 4, 2, count * d // devices + extra, d), BF)
-    return [half, half]
-
-
-def cross_weight(staged, me, devices, dq, dk, dv, low, mem, ot, ssg, sot, fsg, w):
+        return [shape((count, d, d), BF), shape((1,), jnp.int32)], pltpu.VMEM((count, d, d), BF)
+    rows = count * d // devices + extra
+    half = shape((2, 4, 2, rows, d), BF)
+    return [half, half], pltpu.VMEM((2, 2, 4, 2, rows, d), BF)
+
+
+def cross_weight(staged, me, devices, dq, dk, dv, low, mem, ot, ssg, sot, fsg):
     rows, d = dq.shape
-    args = (mem, dk, dv, w, ot, ssg, sot, fsg, low, dq)
-    anywhere, here = pl.BlockSpec(memory_space=pl.ANY), pl.BlockSpec(memory_space=pltpu.VMEM)
+    args = (mem, dk, dv, ot, ssg, sot, fsg, low, dq)
+    anywhere = pl.BlockSpec(memory_space=pl.ANY)
+    outs, scratch = weight_outs(staged, 5, 0, devices, d)
+    last = anywhere if staged else pl.BlockSpec(memory_space=pltpu.SMEM)
     return pl.pallas_call(
         functools.partial(cross_weight_kernel, staged),
-        in_specs=[pl.BlockSpec(memory_space=pltpu.SMEM)] + [anywhere] * 10,
-        out_specs=[here, here, anywhere],
-        out_shape=weight_outs(staged, 5, 0, devices, d) + [shape((rows, d), F32)],
-        scratch_shapes=[pltpu.VMEM((min(a.shape[0], 3), *a.shape[1:]) if a is w else a.shape, a.dtype) for a in args] + [
-            pltpu.VMEM((5, d, d), F32), pltpu.VMEM((rows, d), F32), pltpu.SemaphoreType.DMA((10,)),
-            pltpu.SemaphoreType.DMA,
+        in_specs=[pl.BlockSpec(memory_space=pltpu.SMEM)] + [anywhere] * 9,
+        out_specs=[anywhere, last],
+        out_shape=outs,
+        scratch_shapes=[pltpu.VMEM(a.shape, a.dtype) for a in args] + [
+            scratch, pltpu.SemaphoreType.DMA((9,)), pltpu.SemaphoreType.DMA((4,)),
         ],
         compiler_params=pltpu.CompilerParams(vmem_limit_bytes=VMEM_LIMIT),
         cost_estimate=cost(9e9, 20e6),
@@ -679,22 +748,48 @@
     )(me, *args)
 
 
-def self_weight(staged, me, devices, small, dbin, dq, dk, dv, x):
-    rows, d = dq.shape
-    args = (x, dq, dk, dv)
+def self_last(staged, me, devices, block, before, wo_at, fsg, q, k, v, ot, lse, wo, kmark, qmark, sums, dbin, x):
+    rows, d = x.shape
     anywhere, here = pl.BlockSpec(memory_space=pl.ANY), pl.BlockSpec(memory_space=pltpu.VMEM)
+    outs, scratch = weight_outs(staged, 3, 16, devices, d)
+    act = shape((rows, d), BF)
+    args = (me, fsg, q, k, v, ot, lse, wo, kmark, qmark, sums, dbin, x)
+    if not before:
+        before = [jnp.zeros((rows, d), BF)] * 3
+    fixed = lambda array: pl.BlockSpec(array.shape, lambda b: (0,) * array.ndim)
+    if not staged:
+        outs[1] = shape((16, d), F32)
     return pl.pallas_call(
-        functools.partial(self_weight_kernel, staged),
-        in_specs=[pl.BlockSpec(memory_space=pltpu.SMEM), here, here] + [anywhere] * 4,
-        out_specs=[here, here],
-        out_shape=weight_outs(staged, 3, 32, devices, d),
-        scratch_shapes=[pltpu.VMEM(a.shape, a.dtype) for a in args] + [
-            pltpu.VMEM((3, d, d), F32), pltpu.SemaphoreType.DMA((4,)),
+        functools.partial(self_last_kernel, staged),
+        grid=(1,),
+        in_specs=[pl.BlockSpec(memory_space=pltpu.SMEM)] + [at_row(block, d)] * 4 + [
+            at_col(block, d), at_lead(block, 16), planes(wo, wo_at, 1), at_row(block, 128), at_lead(block, HEAD_DIM),
+            fixed(sums), fixed(dbin), anywhere,
+        ] + [anywhere] * 3,
+        out_specs=[anywhere, anywhere if staged else fixed(outs[1])] + [anywhere] * 3,
+        out_shape=outs + [act] * 3,
+        scratch_shapes=back_scratch(d) + [pltpu.VMEM((rows, d), BF)] * 4 + [
+            scratch, pltpu.SemaphoreType.DMA((7,)), pltpu.SemaphoreType.DMA((4,)),
         ],
-        compiler_params=pltpu.CompilerParams(vmem_limit_bytes=VMEM_LIMIT),
-        cost_estimate=cost(4e9, 10e6),
-        name="self_weight",
-    )(me, small, dbin, *args)
+        input_output_aliases={len(args) + i: 2 + i for i in range(3)},
+        compiler_params=params(("arbitrary",)),
+        cost_estimate=cost(25e9, 20e6),
+        name="self_last",
+    )(*args, *before)
+
+
+def memory_input(dk, dv, w):
+    rows, d = dk.shape
+    return pl.pallas_call(
+        memory_input_kernel,
+        grid=(rows // SEQ_MAX,),
+        in_specs=[row_block(d)] * 2 + [planes(w, 1, 1), planes(w, 2, 1)],
+        out_specs=row_block(d),
+        out_shape=shape((rows, d), F32),
+        compiler_params=params(("arbitrary",)),
+        cost_estimate=cost(3e9, 9e6),
+        name="memory_input",
+    )(dk, dv, w, w)
 
 
 def self_input(fsg, dq, dk, dv, wqk, wv):
@@ -754,10 +849,28 @@
         self.keep = [own]
 
     def last(self):
-        total = self.keep[0]
-        for step, out in zip(range(1, 4), self.out):
-            total = total + lax.ppermute(out, "z", [(i, (i + step) % 4) for i in range(4)]).astype(F32)
-        return total
+        steps = zip(range(1, 4), self.out)
+        return self.keep + [lax.ppermute(out, "z", [(i, (i + step) % 4) for i in range(4)]) for step, out in steps]
+
+    @staticmethod
+    def finish(cross, selfs, small, dbin, own, devices):
+        d = cross[0].shape[1]
+        wide = dbin.shape[1] // devices
+        outs = [
+            shape(dims, F32)
+            for dims in ((6, own, d), (2, own, d), (6, own), (3, own), (3, own), (1, wide), (1, own))
+        ]
+        args = cross + selfs
+        proj, out, bias, gain, shift, hidden, last = pl.pallas_call(
+            functools.partial(final_stage_kernel, own),
+            in_specs=[pl.BlockSpec(memory_space=pltpu.VMEM)] * 8,
+            out_specs=[pl.BlockSpec(memory_space=pltpu.VMEM)] * 7,
+            out_shape=outs,
+            compiler_params=pltpu.CompilerParams(vmem_limit_bytes=VMEM_LIMIT),
+            cost_estimate=cost(2e6, 3e6),
+            name="final_stage",
+        )(*args)
+        return proj, out, bias, gain, shift, hidden.reshape(-1), last.reshape(-1)
 
     @staticmethod
     def feed(grads, own):
@@ -769,7 +882,7 @@
 
 class Whole:
     def __init__(self, me, grads, _):
-        self.grads, self.out = grads, ()
+        self.grads, self.out, self.keep = grads, (), ()
 
     def core(self):
         pass
@@ -779,6 +892,15 @@
     def last(self):
         sums = lax.psum_scatter(self.grads, ("dp", "fsdp"), scatter_dimension=1, tiled=True).astype(F32)
         return sums.reshape(-1, sums.shape[2])
+
+    @staticmethod
+    def finish(cross, selfs, small, dbin, own, devices):
+        sum_up = functools.partial(lax.psum_scatter, axis_name=("dp", "fsdp"), scatter_dimension=1, tiled=True)
+        small, dbin = sum_up(small), sum_up(dbin)[0]
+        cross, selfs = cross.reshape(5, own, -1), selfs.reshape(3, own, -1)
+        proj = jnp.concatenate([selfs, cross[4:], cross[:2]])
+        gain, shift = jnp.stack([small[6], small[11], small[8]]), jnp.stack([small[7], small[12], small[9]])
+        return proj, cross[3:1:-1], small[0:6], gain, shift, dbin, small[10]
 
     @staticmethod
     def feed(grads, own):
@@ -793,6 +915,10 @@
     for s, s.out in zip(sums, outs):
         pass
     return value
+
+
+def hold(sums, value):
+    sums.keep = lax.optimization_barrier((sums.keep, value))[0]
 
 
 def take_turns(value):
@@ -933,45 +1059,37 @@
         )
         small2 = small2 + part
     fsg, dq, dk, dv = grads
-    keep, send, memory_grad = cross_weight(
-        staged, pair, devices, dq, dk, dv, low, memory, cot_, ssg, sot, fsg, cross_proj
-    )
+    keep, send = cross_weight(staged, pair, devices, dq, dk, dv, low, memory, cot_, ssg, sot, fsg)
     cross_sum = scatter(me, keep, send)
-    upstream = after(fsg, cross_sum)
-    grads, small1 = [], 0
-    for block in blocks:
+    dk = after(dk, cross_sum)
+    memory_grad = memory_input(dk, dv, cross_proj)
+    cross_sum.core()
+    upstream, memory_grad = after((fsg, memory_grad), cross_sum)
+    grads = []
+    small1 = jnp.zeros((8, d), F32)
+    for block in blocks[:-1]:
         *grads, part = self_back(block, grads, out_at, upstream, sq, sk, sv, sot, slse, out, smark, qmark)
         small1 = small1 + part
-        if block == 0:
-            cross_sum.core()
-            upstream = after(upstream, cross_sum)
-    dq, dk, dv = grads
     cross_sum.first()
-    dq = after(dq, cross_sum)
-    sums = jnp.concatenate([small1, small2, small3])
-    keep, send = self_weight(staged, pair, devices, sums, dbin, dq, dk, dv, query)
+    upstream = after(upstream, cross_sum)
+    sums = jnp.concatenate([small1[:3], small2[:5], small3[:5], jnp.zeros((3, d), F32)])
+    keep, send, dq, dk, dv = self_last(
+        staged, pair, devices, blocks[-1], grads, out_at, upstream, sq, sk, sv, sot, slse, out, smark, qmark, sums, dbin,
+        query,
+    )
     self_sum = scatter(me, keep, send)
     cross_sum.second()
+    self_sum.out = after(self_sum.out, cross_sum)
     self_sum.core()
     upstream = after(fsg, self_sum, cross_sum)
     query_grad = self_input(upstream, dq, dk, dv, full["qk"], full["v"])
+    cross = cross_sum.last()
+    hold(self_sum, (query_grad, cross))
     self_sum.first()
-    cross = cross_sum.last()
     self_sum.second()
-    rows = self_sum.last()
-    cross = cross.reshape(5, own, d)
-    proj_grad = jnp.concatenate([rows[: 3 * own].reshape(3, own, d), cross[2:]])
-    if staged:
-        sums = rows[3 * own : 3 * own + 24, :own]
-        dbin = rows[3 * own + 24, : dbin.shape[1] // devices]
-    else:
-        sum_up = functools.partial(lax.psum_scatter, axis_name=("dp", "fsdp"), scatter_dimension=1, tiled=True)
-        sums, dbin = sum_up(sums), sum_up(dbin)[0]
-    bias_g = jnp.concatenate([sums[0:3], sums[8:11]])
-    gain_g = jnp.stack([sums[11], sums[19], sums[16]])
-    shift_g = jnp.stack([sums[12], sums[20], sums[17]])
+    proj_g, out_g, bias_g, gain_g, shift_g, dbin_g, dbout_g = scatter.finish(cross, self_sum.last(), send, dbin, own, devices)
     return (
-        mixed, query_grad, memory_grad, proj_grad, cross[1::-1], bias_g, gain_g, shift_g, dwin, dbin, dwout, sums[18],
+        mixed, query_grad, memory_grad, proj_g, out_g, bias_g, gain_g, shift_g, dwin, dbin_g, dwout, dbout_g,
     )
 
 

time: 407 us -> 397 us (0.975)
  waiting for transfers between devices: 117 us -> 108 us
  starting transfers between devices: 29.2 us -> 33.6 us
    ppermute x10, waiting for transfers between devices: 32.9 us -> 16.8 us  [swap(): return lax.ppermute(value, name, [(0, 1), (1, 0)])]
    pallas_call x1 -> x3, Pallas kernels: 11 us -> 26.3 us  [the longest x1 17.9 us: self_last(): pl.pallas_call(functools.partial(self_last_kernel, staged), grid=(1,), in...]
    pallas_call x4 -> x3, Pallas kernels: 56.5 us -> 42.9 us  [one_back(): pl.pallas_call(kernel, grid=(1,), in_specs=specs + kept, out_specs=[at_ro...]
    ppermute x6, waiting for transfers between devices: 8.17 us -> 15.8 us  [last(): lax.ppermute(out, 'z', [(i, (i + step) % 4) for i in range(4)])]
    ppermute x6, starting transfers between devices: 7.7 us -> 11.9 us  [last(): lax.ppermute(out, 'z', [(i, (i + step) % 4) for i in range(4)])]
    unnamed x64 -> x66, local copies, waits for them, and re-layouts: 9.9 us -> 11.2 us
  transfers between devices with their start and end apart: 27 -> 27, of which waited for: 15 -> 16; matrix products, arithmetic and copies ran while one was open for 7% -> 6% of each run, Pallas kernels for 32% -> 32%
where the time goes in v2:
time: 397 us; the launch traced here: 391 us
  Pallas kernels  197 us (50%)
  waiting for transfers between devices  108 us (27%)
  starting transfers between devices  33.6 us (8%)
  local copies, waits for them, and re-layouts  22.1 us (6%)
  other arithmetic  15.2 us (4%)
  between operations  14.8 us (4%)
    pallas_call x1, Pallas kernels, feed(): pl.pallas_call(functools.partial(feed_kernel, own), grid=(2, chunks), in_...  50.2 us
    all_gather x1, waiting for transfers between devices, __init__(): self.rest = lax.all_gather(rest, ('x', 'c', 'z', 'y'), axis=1)  48.1 us
    pallas_call x3, Pallas kernels, one_back(): pl.pallas_call(kernel, grid=(1,), in_specs=specs + kept, out_specs=[at_ro...  42.9 us
    ppermute x6, waiting for transfers between devices, take_pair(): got = lax.ppermute(value, name, [(0, 1), (1, 0)])  20.8 us
    pallas_call x1, Pallas kernels, cross_forward(): pl.pallas_call(cross_forward_kernel, grid=(blocks,), in_specs=[row_block(...  20.3 us
    pallas_call x1, Pallas kernels, self_last(): pl.pallas_call(functools.partial(self_last_kernel, staged), grid=(1,), in...  17.9 us
    ppermute x10, waiting for transfers between devices, swap(): return lax.ppermute(value, name, [(0, 1), (1, 0)])  16.8 us
    ppermute x6, waiting for transfers between devices, last(): lax.ppermute(out, 'z', [(i, (i + step) % 4) for i in range(4)])  15.8 us
  transfers between devices with their start and end apart: 27, of which 16 were waited for; matrix products, arithmetic and copies ran while one was open for 6% of the time, Pallas kernels for 32%

profile of v2, /device:TPU:0, one launch (start us, length us, event | category | flops | bytes accessed | tf_op | source)
XLA Modules:
  0.0 390.8 jit_solution(9768536381508292861)
XLA Ops:
  12.4 4.1 %collective-permute-start.1 = (bf16[1,80,768]{2,1,0:T(8,128)(2,1)S(1)}, bf16[1,80,768]{2,1,0:T(8,128)(2,1)S(1)}, u32[]{:S(2)}, u32[]{:S(2)}) collective-permute-start(bf16[1,80,768]{2,1,0:T(8,128)(2,1)S(1)} %fusion.9), channel_id=1, source_target_pairs={{0,4},{2,6},{4,0},{6,2},{1,5},{3,7},{5,1},{7,3},{8,12},{10,14},{12... | collective-permute-start | bytes 368648 | tf_op jit(solution)/shard_map/ppermute | solution.py:928
  20.3 5.6 %collective-permute-done.1 = bf16[1,80,768]{2,1,0:T(8,128)(2,1)S(1)} collective-permute-done((bf16[1,80,768]{2,1,0:T(8,128)(2,1)S(1)}, bf16[1,80,768]{2,1,0:T(8,128)(2,1)S(1)}, u32[]{:S(2)}, u32[]{:S(2)}) %collective-permute-start.1) | collective-permute-done | bytes 122912 | tf_op jit(solution)/shard_map/ppermute | solution.py:928
  36.9 4.5 %collective-permute-done.3 = bf16[2,4,24,768]{3,2,1,0:T(8,128)(2,1)S(1)} collective-permute-done((bf16[2,4,24,768]{3,2,1,0:T(8,128)(2,1)S(1)}, bf16[2,4,24,768]{3,2,1,0:T(8,128)(2,1)S(1)}, u32[]{:S(2)}, u32[]{:S(2)}) %collective-permute-start.3) | collective-permute-done | bytes 294944 | tf_op jit(solution)/shard_map/ppermute | solution.py:934
  42.5 4.4 %collective-permute-done.7 = bf16[1,2,4,32,768]{4,2,3,1,0:T(4,128)(2,1)S(1)} collective-permute-done((bf16[1,2,4,32,768]{4,2,3,1,0:T(4,128)(2,1)S(1)}, bf16[1,2,4,32,768]{4,2,3,1,0:T(4,128)(2,1)S(1)}, u32[]{:S(2)}, u32[]{:S(2)}) %collective-permute-start.7) | collective-permute-done | bytes 393248 | tf_op jit(solution)/shard_map/ppermute | solution.py:934
  47.9 10.9 %collective-permute-done.4 = bf16[2,4,2,24,768]{4,3,2,1,0:T(8,128)(2,1)S(1)} collective-permute-done((bf16[2,4,2,24,768]{4,3,2,1,0:T(8,128)(2,1)S(1)}, bf16[2,4,2,24,768]{4,3,2,1,0:T(8,128)(2,1)S(1)}, u32[]{:S(2)}, u32[]{:S(2)}) %collective-permute-start.4) | collective-permute-done | bytes 589856 | tf_op jit(solution)/shard_map/ppermute | solution.py:934
  73.4 14.5 %self_forward.1 = (bf16[1024,768]{1,0:T(8,128)(2,1)}, bf16[1024,768]{1,0:T(8,128)(2,1)}, bf16[1024,768]{1,0:T(8,128)(2,1)}, bf16[768,1024]{1,0:T(8,128)(2,1)}, f32[2,16,512]{2,1,0:T(8,128)}) custom-call(bf16[1024,768]{1,0:T(8,128)(2,1)} %x_ref.5, bf16[2,768,768]{2,1,0:T(8,128)(2,1)} %bitcast.79, bf16[1,768,768]{2,1,0:T(8,128)(2,1)} %bitcast.81, ...), custom_call_target="tpu_custom_call" | custom-call | flops 20000000000 | bytes 12000000 | tf_op jit(solution)/shard_map/self_forward/pallas_call | solution.py:587
  87.9 48.1 %all-gather.3.cloned.1.call-done.wo_ref.w_ref.win_ref.wk_ref.wv_ref = bf16[13,768,768]{2,1,0:T(8,128)(2,1)} async-done(((bf16[13,24,768]{2,1,0:T(8,128)(2,1)}), bf16[13,768,768]{2,1,0:T(8,128)(2,1)}) %all-gather.3.cloned.1.call-update) | async-done | bytes 15335440 | tf_op jit(solution)/shard_map/all_gather | solution.py:988
  136.0 20.3 %cross_forward.1 = (f32[1024,768]{1,0:T(8,128)}, bf16[1024,768]{1,0:T(8,128)(2,1)}, bf16[1024,768]{1,0:T(8,128)(2,1)}, bf16[1024,768]{1,0:T(8,128)(2,1)}, bf16[1...) custom-call(bf16[1024,768]{1,0:T(8,128)(2,1)} %x_ref.5, ...), custom_call_target="tpu_custom_call" | custom-call | flops 24000000000 | bytes 20000000 | tf_op jit(solution)/shard_map/cross_forward/pallas_call | solution.py:604
  156.3 50.2 %feed.1 = (bf16[1024,768]{1,0:T(8,128)(2,1)}, f32[1024,768]{1,0:T(8,128)}, bf16[768,6144]{1,0:T(8,128)(2,1)}, f32[1,3072]{1,0:T(1,128)}, f32[8,768]{1,0:T(8,128)}) custom-call(f32[1024,768]{1,0:T(8,128)} %get-tuple-element.104.ss_ref, bf16[1024,768]{1,0:T(8,128)(2,1)} %cot_ref.1, ...), custom_call_target="tpu_custom_call" | custom-call | flops 40000000000 | bytes 40000000 | tf_op jit(solution)/shard_map/feed/pallas_call | solution.py:633
  206.6 14.6 %cross_back_0.1 = (f32[1024,768]{1,0:T(8,128)}, bf16[1024,768]{1,0:T(8,128)(2,1)}, bf16[1024,768]{1,0:T(8,128)(2,1)}, bf16[1024,768]{1,0:T(8,128)(2,1)}, f32[8,768]{1,0:T(8,128)}) custom-call(f32[1024,768]{1,0:T(8,128)} %get-tuple-element.106.ssg_ref.refs_4_, f32[1024,768]{1,0:T(8,128)} %get-tuple-element.107.fs_ref, ...), custom_call_target="tpu_custom_call" | custom-call | flops 24999999488 | bytes 15000000 | tf_op jit(solution)/shard_map/cross_back_0/pallas_call | solution.py:687
  221.2 15.4 %cross_back_1.1 = (f32[1024,768]{1,0:T(8,128)}, bf16[1024,768]{1,0:T(8,128)(2,1)}, bf16[1024,768]{1,0:T(8,128)(2,1)}, bf16[1024,768]{1,0:T(8,128)(2,1)}, f32[8,768]{1,0:T(8,128)}) custom-call(f32[1024,768]{1,0:T(8,128)} %get-tuple-element.106.ssg_ref.refs_4_, ...), custom_call_target="tpu_custom_call", output_to_operand_aliasing={{0}: (12, {}), {1}: (13, {}), {2}: (14, {}), {3}: (15, {})} | custom-call | flops 24999999488 | bytes 15000000 | tf_op jit(solution)/shard_map/cross_back_1/pallas_call | solution.py:687
  236.6 14.2 %cross_weight.1 = (bf16[2,4,2,120,768]{4,3,2,1,0:T(8,128)(2,1)}, bf16[2,4,2,120,768]{4,3,2,1,0:T(8,128)(2,1)}) custom-call(s32[1]{0:T(128)} %bitcast.34.me_ref, bf16[1024,768]{1,0:T(8,128)(2,1)} %refs_0_.1, bf16[1024,768]{1,0:T(8,128)(2,1)} %get-tuple-element.123.refs_1_.dk_ref, bf16[1024,768]{1,0:T(8,128)(2,1)} %get-tuple-element.119.refs_2_.dv_ref, ...), custom_call_target="tpu_custom_call" | custom-call | flops 8999999488 | bytes 20000000 | tf_op jit(solution)/shard_map/cross_weight/pallas_call | solution.py:737
  251.8 6.1 %memory_input.1 = f32[1024,768]{1,0:T(8,128)} custom-call(bf16[1024,768]{1,0:T(8,128)(2,1)} %get-tuple-element.123.refs_1_.dk_ref, bf16[1024,768]{1,0:T(8,128)(2,1)} %get-tuple-element.119.refs_2_.dv_ref, bf16[13,768,768]{2,1,0:T(8,128)(2,1)} %all-gather.3.cloned.1.call-done.wo_ref.w_ref.win_ref.wk_ref.wv_ref, ...), custom_call_target="tpu_custom_call" | custom-call | flops 3000000000 | bytes 9000000 | tf_op jit(solution)/shard_map/memory_input/pallas_call | solution.py:783
  259.5 4.9 %first_stage.2 = (bf16[4,2,120,384]{3,2,1,0:T(8,128)(2,1)}, bf16[4,2,120,384]{3,2,1,0:T(8,128)(2,1)}, bf16[2,4,120,384]{3,2,1,0:T(8,128)(2,1)}, bf16[2,4,120,384]{3,2,1,0:T(8,128)(2,1)}) custom-call(s32[3]{0:T(128)} %pad_add_fusion.me_ref, bf16[2,4,2,120,768]{4,3,2,1,0:T(8,128)(2,1)} %get-tuple-element.124.keep_ref, bf16[2,4,2,120,768]{4,3,2,1,0:T(8,128)(2,1)} %copy-done), custom_call_target="tpu_custom_call" | custom-call | flops 1474560 | bytes 8847360 | tf_op jit(solution)/shard_map/first_stage/pallas_call | solution.py:536
  266.4 12.9 %self_back_0.1 = (bf16[1024,768]{1,0:T(8,128)(2,1)}, bf16[1024,768]{1,0:T(8,128)(2,1)}, bf16[1024,768]{1,0:T(8,128)(2,1)}, f32[8,768]{1,0:T(8,128)}) custom-call(f32[1024,768]{1,0:T(8,128)} %get-tuple-element.163.refs_6_.fsg_ref, bf16[1024,768]{1,0:T(8,128)(2,1)} %get-tuple-element.136.q_ref, bf16[1024,768]{1,0:T(8,128)(2,1)} %get-tuple-element.137.k_ref, ...), custom_call_target="tpu_custom_call" | custom-call | flops 24999999488 | bytes 15000000 | tf_op jit(solution)/shard_map/self_back_0/pallas_call | solution.py:687
  280.8 4.7 %collective-permute-done.10.gl_ref = bf16[4,2,120,384]{3,2,1,0:T(8,128)(2,1)S(1)} collective-permute-done((bf16[4,2,120,384]{3,2,1,0:T(8,128)(2,1)}, bf16[4,2,120,384]{3,2,1,0:T(8,128)(2,1)S(1)}, u32[]{:S(2)}, u32[]{:S(2)}) %collective-permute-start.10) | collective-permute-done | bytes 737312 | tf_op jit(solution)/shard_map/ppermute | solution.py:822
  294.1 17.9 %self_last.1 = (bf16[2,4,2,88,768]{4,3,2,1,0:T(8,128)(2,1)}, bf16[2,4,2,88,768]{4,3,2,1,0:T(8,128)(2,1)}, bf16[1024,768]{1,0:T(8,128)(2,1)}, bf16[1024,768]{1,0:T(8,128)(2,1)}, bf16[1024,768]{1,0:T(8,128)(2,1)}) custom-call(s32[1]{0:T(128)} %bitcast.34.me_ref, ...), custom_call_target="tpu_custom_call", output_to_operand_aliasing={{2}: (13, {}), {3}: (14, {}), {4}: (15, {})} | custom-call | flops 24999999488 | bytes 20000000 | tf_op jit(solution)/shard_map/self_last/pallas_call | solution.py:762
  315.3 4.5 %collective-permute-done.14.got_ref = bf16[2,4,2,88,768]{4,3,2,1,0:T(8,128)(2,1)S(1)} collective-permute-done((bf16[2,4,2,88,768]{4,3,2,1,0:T(8,128)(2,1)}, bf16[2,4,2,88,768]{4,3,2,1,0:T(8,128)(2,1)S(1)}, u32[]{:S(2)}, u32[]{:S(2)}) %collective-permute-start.14) | collective-permute-done | bytes 2162720 | tf_op jit(solution)/shard_map/ppermute | solution.py:822
  321.1 4.4 %first_stage.3 = (bf16[4,2,88,384]{3,2,1,0:T(8,128)(2,1)}, bf16[4,2,88,384]{3,2,1,0:T(8,128)(2,1)}, bf16[2,4,88,384]{3,2,1,0:T(8,128)(2,1)}, bf16[2,4,88,384]{3,2,1,0:T(8,128)(2,1)}) custom-call(s32[3]{0:T(128)} %pad_add_fusion.me_ref, bf16[2,4,2,88,768]{4,3,2,1,0:T(8,128)(2,1)} %get-tuple-element.148.keep_ref, bf16[2,4,2,88,768]{4,3,2,1,0:T(8,128)(2,1)} %copy-done.1), custom_call_target="tpu_custom_call" | custom-call | flops 1081344 | bytes 6488064 | tf_op jit(solution)/shard_map/first_stage/pallas_call | solution.py:536
  331.4 8.7 %self_input.1 = f32[1024,768]{1,0:T(8,128)} custom-call(f32[1024,768]{1,0:T(8,128)} %get-tuple-element.163.refs_6_.fsg_ref, bf16[1024,768]{1,0:T(8,128)(2,1)} %get-tuple-element.164.dq_ref, bf16[1024,768]{1,0:T(8,128)(2,1)} %get-tuple-element.165.dk_ref, bf16[1024,768]{1,0:T(8,128)(2,1)} %get-tuple-element.166.dv_ref, bf16[2,768,768]{2,1,0:T(8,128)(2,1)} %bitcast.80, ...), custom_call_target="tpu_custom_call" | custom-call | flops 4000000000 | bytes 14000000 | tf_op jit(solution)/shard_map/self_input/pallas_call | solution.py:797
  340.5 8.7 %collective-permute-done.16.refs_2_ = bf16[120,768]{1,0:T(8,128)(2,1)S(1)} collective-permute-done((bf16[120,768]{1,0:T(8,128)(2,1)S(1)}, bf16[120,768]{1,0:T(8,128)(2,1)S(1)}, u32[]{:S(2)}, u32[]{:S(2)}) %collective-permute-start.16) | collective-permute-done | bytes 184352 | tf_op jit(solution)/shard_map/ppermute | solution.py:853
  355.5 4.7 %collective-permute-done.20.gl_ref = bf16[4,88,384]{2,1,0:T(8,128)(2,1)S(1)} collective-permute-done((bf16[4,88,384]{2,1,0:T(8,128)(2,1)}, bf16[4,88,384]{2,1,0:T(8,128)(2,1)S(1)}, u32[]{:S(2)}, u32[]{:S(2)}) %collective-permute-start.20) | collective-permute-done | bytes 270368 | tf_op jit(solution)/shard_map/ppermute | solution.py:822
  363.5 5.5 %collective-permute-start.22 = (bf16[88,768]{1,0:T(8,128)(2,1)}, bf16[88,768]{1,0:T(8,128)(2,1)S(1)}, u32[]{:S(2)}, u32[]{:S(2)}) collective-permute-start(bf16[88,768]{1,0:T(8,128)(2,1)} %get-tuple-element.183), channel_id=1, source_target_pairs={{0,2},{2,4},{4,6},{6,0},{1,3},{3,5},{5,7},{7,1},{8,10},{10,12},{12... | collective-permute-start | bytes 405512 | tf_op jit(solution)/shard_map/ppermute | solution.py:853
  373.6 4.4 %collective-permute-done.23.refs_6_ = bf16[88,768]{1,0:T(8,128)(2,1)S(1)} collective-permute-done((bf16[88,768]{1,0:T(8,128)(2,1)}, bf16[88,768]{1,0:T(8,128)(2,1)S(1)}, u32[]{:S(2)}, u32[]{:S(2)}) %collective-permute-start.23) | collective-permute-done | bytes 135200 | tf_op jit(solution)/shard_map/ppermute | solution.py:853
  (183 shorter events, 81.8 us)
Async XLA Ops:
  7.3 128.8 %all-gather.3.cloned.1.call-start = ((), (), s32[]{:S(2)}) async-start(), calls=%async_computation.2 | async-start | bytes 15814656 | tf_op jit(solution)/shard_map/all_gather | solution.py:988
  11.9 369.2 %reduce-scatter.2.cloned.1.call-start = ((), (), s32[]{:S(2)}) async-start(), calls=%async_computation.1 | async-start | bytes 9732096 | tf_op jit(solution)/shard_map/reduce_scatter | solution.py:877
  12.4 13.6 %collective-permute-start.1 = (bf16[1,80,768]{2,1,0:T(8,128)(2,1)S(1)}, bf16[1,80,768]{2,1,0:T(8,128)(2,1)S(1)}, u32[]{:S(2)}, u32[]{:S(2)}) collective-permute-start(bf16[1,80,768]{2,1,0:T(8,128)(2,1)S(1)} %fusion.9), channel_id=1, source_target_pairs={{0,4},{2,6},{4,0},{6,2},{1,5},{3,7},{5,1},{7,3},{8,12},{10,14},{12... | collective-permute-start | bytes 368648 | tf_op jit(solution)/shard_map/ppermute | solution.py:928
  16.5 9.5 %collective-permute-start.2 = (bf16[1,80,768]{2,1,0:T(8,128)(2,1)S(1)}, bf16[1,80,768]{2,1,0:T(8,128)(2,1)S(1)}, u32[]{:S(2)}, u32[]{:S(2)}) collective-permute-start(bf16[1,80,768]{2,1,0:T(8,128)(2,1)S(1)} %fusion.9), channel_id=1, source_target_pairs={{0,2},{2,4},{4,6},{6,0},{1,3},{3,5},{5,7},{7,1},{8,10},{10,12},{12... | collective-permute-start | bytes 368648 | tf_op jit(solution)/shard_map/ppermute | solution.py:928
  18.0 9.0 %collective-permute-start = (bf16[1,80,768]{2,1,0:T(8,128)(2,1)S(1)}, bf16[1,80,768]{2,1,0:T(8,128)(2,1)S(1)}, u32[]{:S(2)}, u32[]{:S(2)}) collective-permute-start(bf16[1,80,768]{2,1,0:T(8,128)(2,1)S(1)} %fusion.9), channel_id=1, source_target_pairs={{0,6},{2,0},{4,2},{6,4},{1,7},{3,1},{5,3},{7,5},{8,14},{10,8},{12,... | collective-permute-start | bytes 368648 | tf_op jit(solution)/shard_map/ppermute | solution.py:928
  31.6 9.9 %collective-permute-start.3 = (bf16[2,4,24,768]{3,2,1,0:T(8,128)(2,1)S(1)}, bf16[2,4,24,768]{3,2,1,0:T(8,128)(2,1)S(1)}, u32[]{:S(2)}, u32[]{:S(2)}) collective-permute-start(bf16[2,4,24,768]{3,2,1,0:T(8,128)(2,1)S(1)} %bitcast.93), channel_id=1, source_target_pairs={{0,1},{1,0},{2,3},{3,2},{4,5},{5,4},{6,7},{7,6},{8,9},{9,8},{10,11... | collective-permute-start | bytes 884744 | tf_op jit(solution)/shard_map/ppermute | solution.py:934
  35.1 11.7 %collective-permute-start.7 = (bf16[1,2,4,32,768]{4,2,3,1,0:T(4,128)(2,1)S(1)}, bf16[1,2,4,32,768]{4,2,3,1,0:T(4,128)(2,1)S(1)}, u32[]{:S(2)}, u32[]{:S(2)}) collective-permute-start(bf16[1,2,4,32,768]{4,2,3,1,0:T(4,128)(2,1)S(1)} %pad_maximum_fusion.5), channel_id=1, source_target_pairs={{0,1},{1,0},{2,3},{3,2},{4,5},{5,4},{6,7},{7,6},{8,9},{9,8},{10,11... | collective-permute-start | bytes 1179656 | tf_op jit(solution)/shard_map/ppermute | solution.py:934
  41.6 17.2 %collective-permute-start.4 = (bf16[2,4,2,24,768]{4,3,2,1,0:T(8,128)(2,1)S(1)}, bf16[2,4,2,24,768]{4,3,2,1,0:T(8,128)(2,1)S(1)}, u32[]{:S(2)}, u32[]{:S(2)}) collective-permute-start(bf16[2,4,2,24,768]{4,3,2,1,0:T(8,128)(2,1)S(1)} %pad_maximum_fusion.3), channel_id=1, source_target_pairs={{0,16},{16,0},{1,17},{17,1},{2,18},{18,2},{3,19},{19,3},{4,20},{20... | collective-permute-start | bytes 1769480 | tf_op jit(solution)/shard_map/ppermute | solution.py:934
  47.8 14.3 %collective-permute-start.8 = (bf16[1,2,4,2,32,768]{5,2,4,3,1,0:T(4,128)(2,1)S(1)}, bf16[1,2,4,2,32,768]{5,2,4,3,1,0:T(4,128)(2,1)}, u32[]{:S(2)}, u32[]{:S(2)}) collective-permute-start(bf16[1,2,4,2,32,768]{5,2,4,3,1,0:T(4,128)(2,1)S(1)} %pad_maximum_fusion.2), channel_id=1, source_target_pairs={{0,8},{8,0},{1,9},{9,1},{2,10},{10,2},{3,11},{11,3},{4,12},{12,4},... | collective-permute-start | bytes 2359304 | tf_op jit(solution)/shard_map/ppermute | solution.py:934
  60.0 10.3 %collective-permute-start.5 = (bf16[2,2,4,2,24,768]{5,4,3,2,1,0:T(8,128)(2,1)}, bf16[2,2,4,2,24,768]{5,4,3,2,1,0:T(8,128)(2,1)}, u32[]{:S(2)}, u32[]{:S(2)}) collective-permute-start(bf16[2,2,4,2,24,768]{5,4,3,2,1,0:T(8,128)(2,1)} %pad_maximum_fusion.1), channel_id=1, source_target_pairs={{0,8},{8,0},{1,9},{9,1},{2,10},{10,2},{3,11},{11,3},{4,12},{12,4},... | collective-permute-start | bytes 3538952 | tf_op jit(solution)/shard_map/ppermute | solution.py:934
  250.8 7.1 %collective-permute-start.9 = (bf16[2,4,2,120,768]{4,3,2,1,0:T(8,128)(2,1)}, bf16[2,4,2,120,768]{4,3,2,1,0:T(8,128)(2,1)S(1)}, u32[]{:S(2)}, u32[]{:S(2)}) collective-permute-start(bf16[2,4,2,120,768]{4,3,2,1,0:T(8,128)(2,1)} %get-tuple-element.125), channel_id=1, source_target_pairs={{0,8},{8,0},{1,9},{9,1},{2,10},{10,2},{3,11},{11,3},{4,12},{12,4},... | collective-permute-start | bytes 8847368 | tf_op jit(solution)/shard_map/ppermute | solution.py:822
  264.4 21.1 %collective-permute-start.10 = (bf16[4,2,120,384]{3,2,1,0:T(8,128)(2,1)}, bf16[4,2,120,384]{3,2,1,0:T(8,128)(2,1)S(1)}, u32[]{:S(2)}, u32[]{:S(2)}) collective-permute-start(bf16[4,2,120,384]{3,2,1,0:T(8,128)(2,1)} %get-tuple-element.130), channel_id=1, source_target_pairs={{0,16},{16,0},{1,17},{17,1},{2,18},{18,2},{3,19},{19,3},{4,20},{20... | collective-permute-start | bytes 2211848 | tf_op jit(solution)/shard_map/ppermute | solution.py:822
  265.8 22.2 %collective-permute-start.11 = (bf16[2,4,120,384]{3,2,1,0:T(8,128)(2,1)}, bf16[2,4,120,384]{3,2,1,0:T(8,128)(2,1)S(1)}, u32[]{:S(2)}, u32[]{:S(2)}) collective-permute-start(bf16[2,4,120,384]{3,2,1,0:T(8,128)(2,1)} %get-tuple-element.132), channel_id=1, source_target_pairs={{0,1},{1,0},{2,3},{3,2},{4,5},{5,4},{6,7},{7,6},{8,9},{9,8},{10,11... | collective-permute-start | bytes 2211848 | tf_op jit(solution)/shard_map/ppermute | solution.py:822
  292.0 20.0 %collective-permute-start.12 = (bf16[4,120,384]{2,1,0:T(8,128)(2,1)}, bf16[4,120,384]{2,1,0:T(8,128)(2,1)S(1)}, u32[]{:S(2)}, u32[]{:S(2)}) collective-permute-start(bf16[4,120,384]{2,1,0:T(8,128)(2,1)} %get-tuple-element.151), channel_id=1, source_target_pairs={{0,1},{1,0},{2,3},{3,2},{4,5},{5,4},{6,7},{7,6},{8,9},{9,8},{10,11... | collective-permute-start | bytes 1105928 | tf_op jit(solution)/shard_map/ppermute | solution.py:822
  292.6 19.4 %collective-permute-start.13 = (bf16[4,120,384]{2,1,0:T(8,128)(2,1)}, bf16[4,120,384]{2,1,0:T(8,128)(2,1)S(1)}, u32[]{:S(2)}, u32[]{:S(2)}) collective-permute-start(bf16[4,120,384]{2,1,0:T(8,128)(2,1)} %get-tuple-element.153), channel_id=1, source_target_pairs={{0,16},{16,0},{1,17},{17,1},{2,18},{18,2},{3,19},{19,3},{4,20},{20... | collective-permute-start | bytes 1105928 | tf_op jit(solution)/shard_map/ppermute | solution.py:822
  325.5 23.8 %collective-permute-start.18 = (bf16[4,2,88,384]{3,2,1,0:T(8,128)(2,1)}, bf16[4,2,88,384]{3,2,1,0:T(8,128)(2,1)S(1)}, u32[]{:S(2)}, u32[]{:S(2)}) collective-permute-start(bf16[4,2,88,384]{3,2,1,0:T(8,128)(2,1)} %get-tuple-element.175), channel_id=1, source_target_pairs={{0,16},{16,0},{1,17},{17,1},{2,18},{18,2},{3,19},{19,3},{4,20},{20... | collective-permute-start | bytes 1622024 | tf_op jit(solution)/shard_map/ppermute | solution.py:822
  326.1 23.2 %collective-permute-start.19 = (bf16[2,4,88,384]{3,2,1,0:T(8,128)(2,1)}, bf16[2,4,88,384]{3,2,1,0:T(8,128)(2,1)S(1)}, u32[]{:S(2)}, u32[]{:S(2)}) collective-permute-start(bf16[2,4,88,384]{3,2,1,0:T(8,128)(2,1)} %get-tuple-element.177), channel_id=1, source_target_pairs={{0,1},{1,0},{2,3},{3,2},{4,5},{5,4},{6,7},{7,6},{8,9},{9,8},{10,11... | collective-permute-start | bytes 1622024 | tf_op jit(solution)/shard_map/ppermute | solution.py:822
  327.4 13.1 %collective-permute-start.15 = (bf16[120,768]{1,0:T(8,128)(2,1)S(1)}, bf16[120,768]{1,0:T(8,128)(2,1)S(1)}, u32[]{:S(2)}, u32[]{:S(2)}) collective-permute-start(bf16[120,768]{1,0:T(8,128)(2,1)S(1)} %copy-done.28), channel_id=1, source_target_pairs={{0,2},{2,4},{4,6},{6,0},{1,3},{3,5},{5,7},{7,1},{8,10},{10,12},{12... | collective-permute-start | bytes 552968 | tf_op jit(solution)/shard_map/ppermute | solution.py:853
  327.5 21.7 %collective-permute-start.16 = (bf16[120,768]{1,0:T(8,128)(2,1)S(1)}, bf16[120,768]{1,0:T(8,128)(2,1)S(1)}, u32[]{:S(2)}, u32[]{:S(2)}) collective-permute-start(bf16[120,768]{1,0:T(8,128)(2,1)S(1)} %copy-done.27), channel_id=1, source_target_pairs={{0,4},{2,6},{4,0},{6,2},{1,5},{3,7},{5,1},{7,3},{8,12},{10,14},{12... | collective-permute-start | bytes 552968 | tf_op jit(solution)/shard_map/ppermute | solution.py:853
  329.5 19.7 %collective-permute-start.17 = (bf16[120,768]{1,0:T(8,128)(2,1)S(1)}, bf16[120,768]{1,0:T(8,128)(2,1)S(1)}, u32[]{:S(2)}, u32[]{:S(2)}) collective-permute-start(bf16[120,768]{1,0:T(8,128)(2,1)S(1)} %copy-done.26), channel_id=1, source_target_pairs={{0,6},{2,0},{4,2},{6,4},{1,7},{3,1},{5,3},{7,5},{8,14},{10,8},{12,... | collective-permute-start | bytes 552968 | tf_op jit(solution)/shard_map/ppermute | solution.py:853
  353.6 6.7 %collective-permute-start.20 = (bf16[4,88,384]{2,1,0:T(8,128)(2,1)}, bf16[4,88,384]{2,1,0:T(8,128)(2,1)S(1)}, u32[]{:S(2)}, u32[]{:S(2)}) collective-permute-start(bf16[4,88,384]{2,1,0:T(8,128)(2,1)} %get-tuple-element.179), channel_id=1, source_target_pairs={{0,1},{1,0},{2,3},{3,2},{4,5},{5,4},{6,7},{7,6},{8,9},{9,8},{10,11... | collective-permute-start | bytes 811016 | tf_op jit(solution)/shard_map/ppermute | solution.py:822
  363.5 10.0 %collective-permute-start.22 = (bf16[88,768]{1,0:T(8,128)(2,1)}, bf16[88,768]{1,0:T(8,128)(2,1)S(1)}, u32[]{:S(2)}, u32[]{:S(2)}) collective-permute-start(bf16[88,768]{1,0:T(8,128)(2,1)} %get-tuple-element.183), channel_id=1, source_target_pairs={{0,2},{2,4},{4,6},{6,0},{1,3},{3,5},{5,7},{7,1},{8,10},{10,12},{12... | collective-permute-start | bytes 405512 | tf_op jit(solution)/shard_map/ppermute | solution.py:853
  369.0 9.0 %collective-permute-start.23 = (bf16[88,768]{1,0:T(8,128)(2,1)}, bf16[88,768]{1,0:T(8,128)(2,1)S(1)}, u32[]{:S(2)}, u32[]{:S(2)}) collective-permute-start(bf16[88,768]{1,0:T(8,128)(2,1)} %get-tuple-element.184), channel_id=1, source_target_pairs={{0,4},{2,6},{4,0},{6,2},{1,5},{3,7},{5,1},{7,3},{8,12},{10,14},{12... | collective-permute-start | bytes 405512 | tf_op jit(solution)/shard_map/ppermute | solution.py:853
  369.5 8.5 %collective-permute-start.24 = (bf16[88,768]{1,0:T(8,128)(2,1)}, bf16[88,768]{1,0:T(8,128)(2,1)S(1)}, u32[]{:S(2)}, u32[]{:S(2)}) collective-permute-start(bf16[88,768]{1,0:T(8,128)(2,1)} %get-tuple-element.185), channel_id=1, source_target_pairs={{0,6},{2,0},{4,2},{6,4},{1,7},{3,1},{5,3},{7,5},{8,14},{10,8},{12,... | collective-permute-start | bytes 405512 | tf_op jit(solution)/shard_map/ppermute | solution.py:853
  (34 other events, 250.3 us)
Sparse Core Ops, SparseCore 0:
  12.0 123.9 all-gather.2
  206.7 143.9 reduce-scatter.1

commit v3 on v2

--- a/solution.py
+++ b/solution.py
@@ -12,6 +12,7 @@
 HEAD_DIM = 64
 SEQ_MAX = 512
 PAIRS = HEADS // 2
+FINE = 256
 EPSILON = 1e-05
 MASKED = 1e30
 SCALE = HEAD_DIM ** (-0.5)
@@ -549,6 +550,10 @@
     return pl.BlockSpec((SEQ_MAX, width), lambda b: (b, 0))
 
 
+def fine_block(width):
+    return pl.BlockSpec((FINE, width), lambda b: (b, 0))
+
+
 def col_block(height):
     return pl.BlockSpec((height, SEQ_MAX), lambda b: (0, b))
 
@@ -635,7 +640,7 @@
         grid=(2, chunks),
         in_specs=[
             whole(second_sum), whole(cot),
-            pl.BlockSpec((1, d, width), lambda p, j: (jnp.where(j == 0, 3, 9 + j) if own else j, 0, 0)),
+            pl.BlockSpec((1, d, width), lambda p, j: (jnp.where(j == 0, 3, 7 + j) if own else j, 0, 0)),
             pl.BlockSpec((1, width), lambda p, j: (0, j)),
             wout_spec, whole(bout), whole(gain), whole(shift),
         ],
@@ -782,9 +787,9 @@
     rows, d = dk.shape
     return pl.pallas_call(
         memory_input_kernel,
-        grid=(rows // SEQ_MAX,),
-        in_specs=[row_block(d)] * 2 + [planes(w, 1, 1), planes(w, 2, 1)],
-        out_specs=row_block(d),
+        grid=(rows // FINE,),
+        in_specs=[fine_block(d)] * 2 + [planes(w, 1, 1), planes(w, 2, 1)],
+        out_specs=fine_block(d),
         out_shape=shape((rows, d), F32),
         compiler_params=params(("arbitrary",)),
         cost_estimate=cost(3e9, 9e6),
@@ -796,9 +801,9 @@
     rows, d = fsg.shape
     return pl.pallas_call(
         self_input_kernel,
-        grid=(rows // SEQ_MAX,),
-        in_specs=[row_block(d)] * 4 + [whole(wqk), whole(wv)],
-        out_specs=row_block(d),
+        grid=(rows // FINE,),
+        in_specs=[fine_block(d)] * 4 + [whole(wqk), whole(wv)],
+        out_specs=fine_block(d),
         out_shape=shape((rows, d), F32),
         compiler_params=params(("arbitrary",)),
         cost_estimate=cost(4e9, 14e6),
@@ -979,15 +984,16 @@
 
 
 class Stages:
-    out_at = 8
+    out_at = 0
 
     def __init__(self, proj, out, small, win, wout):
         _, own, d = proj.shape
         panels = win.reshape(own, -1, d).swapaxes(0, 1)
-        rest = jnp.concatenate([proj[3:6], panels[:1], wout.reshape(-1, own, d), out, panels[1:]])
+        rest = jnp.concatenate([proj[3:6], panels[:1], wout.reshape(-1, own, d), panels[1:]])
         self.rest = lax.all_gather(rest, ("x", "c", "z", "y"), axis=1)
         extra = jnp.pad(small[None, None], ((0, 0), (0, 7), (0, d - small.shape[0])))
         self.one = Doubling(proj[:2], jnp.concatenate([proj[2:3], extra], axis=1))
+        self.two = Doubling(out[:1], out[1:])
         self.own, self.cut, self.d = own, small.shape[0], d
 
     def begin(self):
@@ -995,14 +1001,21 @@
         one.line()
         one.first()
         one.second()
+        self.two.out = after(self.two.out, one)
         left, right = one.core()
         full = {"qk": left.reshape(2, -1, d), "v": right[..., :own, :].reshape(1, -1, d)}
         full.update(spread_small(right[..., own, : self.cut].reshape(-1, self.cut), own))
         return full
 
-    def finish(self):
+    def finish(self, value):
         planes = self.rest.reshape(self.rest.shape[0], -1, self.d)
-        return {"cross_proj": planes, "out": planes, "win": planes, "wout": self.rest}
+        two = self.two
+        two.line()
+        two.out, value = lax.optimization_barrier((two.out, value))
+        two.first()
+        two.second()
+        out = jnp.concatenate(two.core()).reshape(2, -1, self.d)
+        return {"cross_proj": planes, "out": out, "win": planes, "wout": self.rest}, value
 
 
 class Plain:
@@ -1020,8 +1033,8 @@
     def begin(self):
         return self.full
 
-    def finish(self):
-        return self.rest
+    def finish(self, value):
+        return self.rest, value
 
 
 def body(
@@ -1043,7 +1056,7 @@
     qmark = query_marks(query_seg)
     smark, cmark = key_marks(query_seg), key_marks(memory_seg)
     sq, sk, sv, sot, slse = self_forward(query, full["qk"], full["v"], bias, smark, qmark)
-    rest, out_at = weights.finish(), weights.out_at
+    (rest, sot), out_at = weights.finish(sot), weights.out_at
     out, cross_proj = rest["out"], rest["cross_proj"]
     first_sum, low, cq, ck, cv, cot_, clse, second_sum = cross_forward(
         query, memory, sot, out, out_at, cross_proj, bias, gain, shift, cmark, qmark

time: 397 us -> 389 us (0.980)
  waiting for transfers between devices: 108 us -> 78.1 us
  starting transfers between devices: 33.6 us -> 53 us
    all_gather x1, waiting for transfers between devices: 48.1 us -> 1.38 us  [__init__(): self.rest = lax.all_gather(rest, ('x', 'c', 'z', 'y'), axis=1)]
    ppermute x6 -> x12, waiting for transfers between devices: 20.8 us -> 38.5 us  [take_pair(): got = lax.ppermute(value, name, [(0, 1), (1, 0)])]
    ppermute x3 -> x6, starting transfers between devices: 7.93 us -> 23 us  [take_turns(): lax.ppermute(value, 'z', [(i, (i + step) % 4) for i in range(4)])]
    ppermute x6 -> x12, starting transfers between devices: 5.4 us -> 10.2 us  [take_pair(): got = lax.ppermute(value, name, [(0, 1), (1, 0)])]
    unnamed x66 -> x62, local copies, waits for them, and re-layouts: 11.2 us -> 8.66 us
    another operation x12 -> x23, other arithmetic: 9.13 us -> 7.89 us  [take_pair(): jnp.stack([jnp.where(me == 0, value, got), jnp.where(me == 0, got, value)...]
  transfers between devices with their start and end apart: 27 -> 36, of which waited for: 16 -> 19; matrix products, arithmetic and copies ran while one was open for 6% -> 6% of each run, Pallas kernels for 32% -> 33%
where the time goes in v3:
time: 389 us; the launch traced here: 383 us
  Pallas kernels  198 us (51%)
  waiting for transfers between devices  78.1 us (20%)
  starting transfers between devices  53 us (14%)
  local copies, waits for them, and re-layouts  22.2 us (6%)
  other arithmetic  16.6 us (4%)
  between operations  14.9 us (4%)
    pallas_call x1, Pallas kernels, feed(): pl.pallas_call(functools.partial(feed_kernel, own), grid=(2, chunks), in_...  50.2 us
    pallas_call x3, Pallas kernels, one_back(): pl.pallas_call(kernel, grid=(1,), in_specs=specs + kept, out_specs=[at_ro...  42.6 us
    ppermute x12, waiting for transfers between devices, take_pair(): got = lax.ppermute(value, name, [(0, 1), (1, 0)])  38.5 us
    ppermute x6, starting transfers between devices, take_turns(): lax.ppermute(value, 'z', [(i, (i + step) % 4) for i in range(4)])  23 us
    pallas_call x1, Pallas kernels, cross_forward(): pl.pallas_call(cross_forward_kernel, grid=(blocks,), in_specs=[row_block(...  20.6 us
    ppermute x10, waiting for transfers between devices, swap(): return lax.ppermute(value, name, [(0, 1), (1, 0)])  17.9 us
    pallas_call x1, Pallas kernels, self_last(): pl.pallas_call(functools.partial(self_last_kernel, staged), grid=(1,), in...  17.9 us
    ppermute x6, waiting for transfers between devices, last(): lax.ppermute(out, 'z', [(i, (i + step) % 4) for i in range(4)])  15.2 us
  transfers between devices with their start and end apart: 36, of which 19 were waited for; matrix products, arithmetic and copies ran while one was open for 6% of the time, Pallas kernels for 33%

profile of v3, /device:TPU:0, one launch (start us, length us, event | category | flops | bytes accessed | tf_op | source)
XLA Modules:
  0.0 382.8 jit_solution(12988133212743899651)
XLA Ops:
  35.5 4.5 %collective-permute-done.3 = bf16[2,4,24,768]{3,2,1,0:T(8,128)(2,1)S(1)} collective-permute-done((bf16[2,4,24,768]{3,2,1,0:T(8,128)(2,1)S(1)}, bf16[2,4,24,768]{3,2,1,0:T(8,128)(2,1)S(1)}, u32[]{:S(2)}, u32[]{:S(2)}) %collective-permute-start.3) | collective-permute-done | bytes 294944 | tf_op jit(solution)/shard_map/ppermute | solution.py:939
  40.7 6.6 %collective-permute-done.6 = bf16[1,2,4,32,768]{4,2,3,1,0:T(4,128)(2,1)S(1)} collective-permute-done((bf16[1,2,4,32,768]{4,2,3,1,0:T(4,128)(2,1)S(1)}, bf16[1,2,4,32,768]{4,2,3,1,0:T(4,128)(2,1)S(1)}, u32[]{:S(2)}, u32[]{:S(2)}) %collective-permute-start.6) | collective-permute-done | bytes 393248 | tf_op jit(solution)/shard_map/ppermute | solution.py:939
  48.3 11.5 %collective-permute-done.4 = bf16[2,4,2,24,768]{4,3,2,1,0:T(8,128)(2,1)S(1)} collective-permute-done((bf16[2,4,2,24,768]{4,3,2,1,0:T(8,128)(2,1)S(1)}, bf16[2,4,2,24,768]{4,3,2,1,0:T(8,128)(2,1)S(1)}, u32[]{:S(2)}, u32[]{:S(2)}) %collective-permute-start.4) | collective-permute-done | bytes 589856 | tf_op jit(solution)/shard_map/ppermute | solution.py:939
  60.8 9.4 %collective-permute-start.9 = (bf16[2,24,768]{2,1,0:T(8,128)(2,1)S(1)}, bf16[2,24,768]{2,1,0:T(8,128)(2,1)S(1)}, u32[]{:S(2)}, u32[]{:S(2)}) collective-permute-start(bf16[2,24,768]{2,1,0:T(8,128)(2,1)S(1)} %copy-done.17), channel_id=1, source_target_pairs={{0,2},{2,4},{4,6},{6,0},{1,3},{3,5},{5,7},{7,1},{8,10},{10,12},{12... | collective-permute-start | bytes 221192 | tf_op jit(solution)/shard_map/ppermute | solution.py:933
  86.1 14.6 %self_forward.1 = (bf16[1024,768]{1,0:T(8,128)(2,1)}, bf16[1024,768]{1,0:T(8,128)(2,1)}, bf16[1024,768]{1,0:T(8,128)(2,1)}, bf16[768,1024]{1,0:T(8,128)(2,1)}, f32[2,16,512]{2,1,0:T(8,128)}) custom-call(bf16[1024,768]{1,0:T(8,128)(2,1)} %x_ref.5, bf16[2,768,768]{2,1,0:T(8,128)(2,1)} %bitcast.124, bf16[1,768,768]{2,1,0:T(8,128)(2,1)} %bitcast.132, ...), custom_call_target="tpu_custom_call" | custom-call | flops 20000000000 | bytes 12000000 | tf_op jit(solution)/shard_map/self_forward/pallas_call | solution.py:592
  102.7 6.4 %collective-permute-done.15 = bf16[1,4,24,768]{3,2,1,0:T(8,128)(2,1)S(1)} collective-permute-done((bf16[1,4,24,768]{3,2,1,0:T(8,128)(2,1)S(1)}, bf16[1,4,24,768]{3,2,1,0:T(8,128)(2,1)S(1)}, u32[]{:S(2)}, u32[]{:S(2)}) %collective-permute-start.15) | collective-permute-done | bytes 147488 | tf_op jit(solution)/shard_map/ppermute | solution.py:939
  111.4 6.6 %collective-permute-done.16 = bf16[1,2,4,24,768]{4,3,2,1,0:T(8,128)(2,1)S(1)} collective-permute-done((bf16[1,2,4,24,768]{4,3,2,1,0:T(8,128)(2,1)S(1)}, bf16[1,2,4,24,768]{4,3,2,1,0:T(8,128)(2,1)S(1)}, u32[]{:S(2)}, u32[]{:S(2)}) %collective-permute-start.16) | collective-permute-done | bytes 294944 | tf_op jit(solution)/shard_map/ppermute | solution.py:939
  126.7 20.6 %cross_forward.1 = (f32[1024,768]{1,0:T(8,128)}, bf16[1024,768]{1,0:T(8,128)(2,1)}, bf16[1024,768]{1,0:T(8,128)(2,1)}, bf16[1024,768]{1,0:T(8,128)(2,1)}, bf16[1...) custom-call(bf16[1024,768]{1,0:T(8,128)(2,1)} %x_ref.5, ...), custom_call_target="tpu_custom_call" | custom-call | flops 24000000000 | bytes 20000000 | tf_op jit(solution)/shard_map/cross_forward/pallas_call | solution.py:609
  147.3 50.2 %feed.1 = (bf16[1024,768]{1,0:T(8,128)(2,1)}, f32[1024,768]{1,0:T(8,128)}, bf16[768,6144]{1,0:T(8,128)(2,1)}, f32[1,3072]{1,0:T(1,128)}, f32[8,768]{1,0:T(8,128)}) custom-call(f32[1024,768]{1,0:T(8,128)} %get-tuple-element.116.ss_ref, bf16[1024,768]{1,0:T(8,128)(2,1)} %cot_ref.1, ...), custom_call_target="tpu_custom_call" | custom-call | flops 40000000000 | bytes 40000000 | tf_op jit(solution)/shard_map/feed/pallas_call | solution.py:638
  197.6 14.6 %cross_back_0.1 = (f32[1024,768]{1,0:T(8,128)}, bf16[1024,768]{1,0:T(8,128)(2,1)}, bf16[1024,768]{1,0:T(8,128)(2,1)}, bf16[1024,768]{1,0:T(8,128)(2,1)}, f32[8,768]{1,0:T(8,128)}) custom-call(f32[1024,768]{1,0:T(8,128)} %get-tuple-element.118.ssg_ref.refs_4_, f32[1024,768]{1,0:T(8,128)} %get-tuple-element.119.fs_ref, ...), custom_call_target="tpu_custom_call" | custom-call | flops 24999999488 | bytes 15000000 | tf_op jit(solution)/shard_map/cross_back_0/pallas_call | solution.py:692
  212.1 15.2 %cross_back_1.1 = (f32[1024,768]{1,0:T(8,128)}, bf16[1024,768]{1,0:T(8,128)(2,1)}, bf16[1024,768]{1,0:T(8,128)(2,1)}, bf16[1024,768]{1,0:T(8,128)(2,1)}, f32[8,768]{1,0:T(8,128)}) custom-call(f32[1024,768]{1,0:T(8,128)} %get-tuple-element.118.ssg_ref.refs_4_, ...), custom_call_target="tpu_custom_call", output_to_operand_aliasing={{0}: (12, {}), {1}: (13, {}), {2}: (14, {}), {3}: (15, {})} | custom-call | flops 24999999488 | bytes 15000000 | tf_op jit(solution)/shard_map/cross_back_1/pallas_call | solution.py:692
  227.3 14.4 %cross_weight.1 = (bf16[2,4,2,120,768]{4,3,2,1,0:T(8,128)(2,1)}, bf16[2,4,2,120,768]{4,3,2,1,0:T(8,128)(2,1)}) custom-call(s32[1]{0:T(128)} %bitcast.55.me_ref, bf16[1024,768]{1,0:T(8,128)(2,1)} %refs_0_.1, bf16[1024,768]{1,0:T(8,128)(2,1)} %get-tuple-element.135.refs_1_.dk_ref, bf16[1024,768]{1,0:T(8,128)(2,1)} %get-tuple-element.131.refs_2_.dv_ref, ...), custom_call_target="tpu_custom_call" | custom-call | flops 8999999488 | bytes 20000000 | tf_op jit(solution)/shard_map/cross_weight/pallas_call | solution.py:742
  242.7 6.7 %memory_input.1 = f32[1024,768]{1,0:T(8,128)} custom-call(bf16[1024,768]{1,0:T(8,128)(2,1)} %get-tuple-element.135.refs_1_.dk_ref, bf16[1024,768]{1,0:T(8,128)(2,1)} %get-tuple-element.131.refs_2_.dv_ref, bf16[11,768,768]{2,1,0:T(8,128)(2,1)} %all-gather.3.cloned.1.call-done.w_ref.win_ref.wk_ref.wv_ref, ...), custom_call_target="tpu_custom_call" | custom-call | flops 3000000000 | bytes 9000000 | tf_op jit(solution)/shard_map/memory_input/pallas_call | solution.py:788
  251.0 4.9 %first_stage.2 = (bf16[4,2,120,384]{3,2,1,0:T(8,128)(2,1)}, bf16[4,2,120,384]{3,2,1,0:T(8,128)(2,1)}, bf16[2,4,120,384]{3,2,1,0:T(8,128)(2,1)}, bf16[2,4,120,384]{3,2,1,0:T(8,128)(2,1)}) custom-call(s32[3]{0:T(128)} %pad_add_fusion.me_ref, bf16[2,4,2,120,768]{4,3,2,1,0:T(8,128)(2,1)} %get-tuple-element.136.keep_ref, bf16[2,4,2,120,768]{4,3,2,1,0:T(8,128)(2,1)} %copy-done), custom_call_target="tpu_custom_call" | custom-call | flops 1474560 | bytes 8847360 | tf_op jit(solution)/shard_map/first_stage/pallas_call | solution.py:537
  257.9 12.9 %self_back_0.1 = (bf16[1024,768]{1,0:T(8,128)(2,1)}, bf16[1024,768]{1,0:T(8,128)(2,1)}, bf16[1024,768]{1,0:T(8,128)(2,1)}, f32[8,768]{1,0:T(8,128)}) custom-call(f32[1024,768]{1,0:T(8,128)} %get-tuple-element.175.refs_6_.fsg_ref, bf16[1024,768]{1,0:T(8,128)(2,1)} %get-tuple-element.148.q_ref, bf16[1024,768]{1,0:T(8,128)(2,1)} %get-tuple-element.149.k_ref, ...), custom_call_target="tpu_custom_call" | custom-call | flops 24999999488 | bytes 15000000 | tf_op jit(solution)/shard_map/self_back_0/pallas_call | solution.py:692
  272.3 5.1 %collective-permute-done.19.gl_ref = bf16[4,2,120,384]{3,2,1,0:T(8,128)(2,1)S(1)} collective-permute-done((bf16[4,2,120,384]{3,2,1,0:T(8,128)(2,1)}, bf16[4,2,120,384]{3,2,1,0:T(8,128)(2,1)S(1)}, u32[]{:S(2)}, u32[]{:S(2)}) %collective-permute-start.19) | collective-permute-done | bytes 737312 | tf_op jit(solution)/shard_map/ppermute | solution.py:827
  286.0 17.9 %self_last.1 = (bf16[2,4,2,88,768]{4,3,2,1,0:T(8,128)(2,1)}, bf16[2,4,2,88,768]{4,3,2,1,0:T(8,128)(2,1)}, bf16[1024,768]{1,0:T(8,128)(2,1)}, bf16[1024,768]{1,0:T(8,128)(2,1)}, bf16[1024,768]{1,0:T(8,128)(2,1)}) custom-call(s32[1]{0:T(128)} %bitcast.55.me_ref, ...), custom_call_target="tpu_custom_call", output_to_operand_aliasing={{2}: (13, {}), {3}: (14, {}), {4}: (15, {})} | custom-call | flops 24999999488 | bytes 20000000 | tf_op jit(solution)/shard_map/self_last/pallas_call | solution.py:767
  307.3 4.5 %collective-permute-done.23.got_ref = bf16[2,4,2,88,768]{4,3,2,1,0:T(8,128)(2,1)S(1)} collective-permute-done((bf16[2,4,2,88,768]{4,3,2,1,0:T(8,128)(2,1)}, bf16[2,4,2,88,768]{4,3,2,1,0:T(8,128)(2,1)S(1)}, u32[]{:S(2)}, u32[]{:S(2)}) %collective-permute-start.23) | collective-permute-done | bytes 2162720 | tf_op jit(solution)/shard_map/ppermute | solution.py:827
  313.1 4.4 %first_stage.3 = (bf16[4,2,88,384]{3,2,1,0:T(8,128)(2,1)}, bf16[4,2,88,384]{3,2,1,0:T(8,128)(2,1)}, bf16[2,4,88,384]{3,2,1,0:T(8,128)(2,1)}, bf16[2,4,88,384]{3,2,1,0:T(8,128)(2,1)}) custom-call(s32[3]{0:T(128)} %pad_add_fusion.me_ref, bf16[2,4,2,88,768]{4,3,2,1,0:T(8,128)(2,1)} %get-tuple-element.160.keep_ref, bf16[2,4,2,88,768]{4,3,2,1,0:T(8,128)(2,1)} %copy-done.1), custom_call_target="tpu_custom_call" | custom-call | flops 1081344 | bytes 6488064 | tf_op jit(solution)/shard_map/first_stage/pallas_call | solution.py:537
  323.5 9.0 %self_input.1 = f32[1024,768]{1,0:T(8,128)} custom-call(f32[1024,768]{1,0:T(8,128)} %get-tuple-element.175.refs_6_.fsg_ref, bf16[1024,768]{1,0:T(8,128)(2,1)} %get-tuple-element.176.dq_ref, bf16[1024,768]{1,0:T(8,128)(2,1)} %get-tuple-element.177.dk_ref, bf16[1024,768]{1,0:T(8,128)(2,1)} %get-tuple-element.178.dv_ref, bf16[2,768,768]{2,1,0:T(8,128)(2,1)} %bitcast.125, ...), custom_call_target="tpu_custom_call" | custom-call | flops 4000000000 | bytes 14000000 | tf_op jit(solution)/shard_map/self_input/pallas_call | solution.py:802
  332.5 8.7 %collective-permute-done.25.refs_2_ = bf16[120,768]{1,0:T(8,128)(2,1)S(1)} collective-permute-done((bf16[120,768]{1,0:T(8,128)(2,1)S(1)}, bf16[120,768]{1,0:T(8,128)(2,1)S(1)}, u32[]{:S(2)}, u32[]{:S(2)}) %collective-permute-start.25) | collective-permute-done | bytes 184352 | tf_op jit(solution)/shard_map/ppermute | solution.py:858
  348.0 5.6 %collective-permute-done.29.gl_ref = bf16[4,88,384]{2,1,0:T(8,128)(2,1)S(1)} collective-permute-done((bf16[4,88,384]{2,1,0:T(8,128)(2,1)}, bf16[4,88,384]{2,1,0:T(8,128)(2,1)S(1)}, u32[]{:S(2)}, u32[]{:S(2)}) %collective-permute-start.29) | collective-permute-done | bytes 270368 | tf_op jit(solution)/shard_map/ppermute | solution.py:827
  356.6 4.6 %collective-permute-start.31 = (bf16[88,768]{1,0:T(8,128)(2,1)}, bf16[88,768]{1,0:T(8,128)(2,1)S(1)}, u32[]{:S(2)}, u32[]{:S(2)}) collective-permute-start(bf16[88,768]{1,0:T(8,128)(2,1)} %get-tuple-element.195), channel_id=1, source_target_pairs={{0,2},{2,4},{4,6},{6,0},{1,3},{3,5},{5,7},{7,1},{8,10},{10,12},{12... | collective-permute-start | bytes 405512 | tf_op jit(solution)/shard_map/ppermute | solution.py:858
  365.6 4.5 %collective-permute-done.32.refs_6_ = bf16[88,768]{1,0:T(8,128)(2,1)S(1)} collective-permute-done((bf16[88,768]{1,0:T(8,128)(2,1)}, bf16[88,768]{1,0:T(8,128)(2,1)S(1)}, u32[]{:S(2)}, u32[]{:S(2)}) %collective-permute-start.32) | collective-permute-done | bytes 135200 | tf_op jit(solution)/shard_map/ppermute | solution.py:858
  (216 shorter events, 104.7 us)
Async XLA Ops:
  7.3 119.4 %all-gather.3.cloned.1.call-start = ((), (), s32[]{:S(2)}) async-start(), calls=%async_computation.2 | async-start | bytes 13381632 | tf_op jit(solution)/shard_map/all_gather | solution.py:993
  11.0 362.1 %reduce-scatter.2.cloned.1.call-start = ((), (), s32[]{:S(2)}) async-start(), calls=%async_computation.1 | async-start | bytes 9732096 | tf_op jit(solution)/shard_map/reduce_scatter | solution.py:882
  11.5 13.6 %collective-permute-start.1 = (bf16[1,80,768]{2,1,0:T(8,128)(2,1)S(1)}, bf16[1,80,768]{2,1,0:T(8,128)(2,1)S(1)}, u32[]{:S(2)}, u32[]{:S(2)}) collective-permute-start(bf16[1,80,768]{2,1,0:T(8,128)(2,1)S(1)} %fusion.10), channel_id=1, source_target_pairs={{0,4},{2,6},{4,0},{6,2},{1,5},{3,7},{5,1},{7,3},{8,12},{10,14},{12... | collective-permute-start | bytes 368648 | tf_op jit(solution)/shard_map/ppermute | solution.py:933
  15.6 9.5 %collective-permute-start.2 = (bf16[1,80,768]{2,1,0:T(8,128)(2,1)S(1)}, bf16[1,80,768]{2,1,0:T(8,128)(2,1)S(1)}, u32[]{:S(2)}, u32[]{:S(2)}) collective-permute-start(bf16[1,80,768]{2,1,0:T(8,128)(2,1)S(1)} %fusion.10), channel_id=1, source_target_pairs={{0,2},{2,4},{4,6},{6,0},{1,3},{3,5},{5,7},{7,1},{8,10},{10,12},{12... | collective-permute-start | bytes 368648 | tf_op jit(solution)/shard_map/ppermute | solution.py:933
  17.2 8.6 %collective-permute-start = (bf16[1,80,768]{2,1,0:T(8,128)(2,1)S(1)}, bf16[1,80,768]{2,1,0:T(8,128)(2,1)S(1)}, u32[]{:S(2)}, u32[]{:S(2)}) collective-permute-start(bf16[1,80,768]{2,1,0:T(8,128)(2,1)S(1)} %fusion.10), channel_id=1, source_target_pairs={{0,6},{2,0},{4,2},{6,4},{1,7},{3,1},{5,3},{7,5},{8,14},{10,8},{12,... | collective-permute-start | bytes 368648 | tf_op jit(solution)/shard_map/ppermute | solution.py:933
  30.2 9.8 %collective-permute-start.3 = (bf16[2,4,24,768]{3,2,1,0:T(8,128)(2,1)S(1)}, bf16[2,4,24,768]{3,2,1,0:T(8,128)(2,1)S(1)}, u32[]{:S(2)}, u32[]{:S(2)}) collective-permute-start(bf16[2,4,24,768]{3,2,1,0:T(8,128)(2,1)S(1)} %bitcast.144), channel_id=1, source_target_pairs={{0,1},{1,0},{2,3},{3,2},{4,5},{5,4},{6,7},{7,6},{8,9},{9,8},{10,11... | collective-permute-start | bytes 884744 | tf_op jit(solution)/shard_map/ppermute | solution.py:939
  33.8 13.5 %collective-permute-start.6 = (bf16[1,2,4,32,768]{4,2,3,1,0:T(4,128)(2,1)S(1)}, bf16[1,2,4,32,768]{4,2,3,1,0:T(4,128)(2,1)S(1)}, u32[]{:S(2)}, u32[]{:S(2)}) collective-permute-start(bf16[1,2,4,32,768]{4,2,3,1,0:T(4,128)(2,1)S(1)} %pad_maximum_fusion.8), channel_id=1, source_target_pairs={{0,1},{1,0},{2,3},{3,2},{4,5},{5,4},{6,7},{7,6},{8,9},{9,8},{10,11... | collective-permute-start | bytes 1179656 | tf_op jit(solution)/shard_map/ppermute | solution.py:939
  40.1 19.7 %collective-permute-start.4 = (bf16[2,4,2,24,768]{4,3,2,1,0:T(8,128)(2,1)S(1)}, bf16[2,4,2,24,768]{4,3,2,1,0:T(8,128)(2,1)S(1)}, u32[]{:S(2)}, u32[]{:S(2)}) collective-permute-start(bf16[2,4,2,24,768]{4,3,2,1,0:T(8,128)(2,1)S(1)} %pad_maximum_fusion.3), channel_id=1, source_target_pairs={{0,16},{16,0},{1,17},{17,1},{2,18},{18,2},{3,19},{19,3},{4,20},{20... | collective-permute-start | bytes 1769480 | tf_op jit(solution)/shard_map/ppermute | solution.py:939
  60.8 16.4 %collective-permute-start.9 = (bf16[2,24,768]{2,1,0:T(8,128)(2,1)S(1)}, bf16[2,24,768]{2,1,0:T(8,128)(2,1)S(1)}, u32[]{:S(2)}, u32[]{:S(2)}) collective-permute-start(bf16[2,24,768]{2,1,0:T(8,128)(2,1)S(1)} %copy-done.17), channel_id=1, source_target_pairs={{0,2},{2,4},{4,6},{6,0},{1,3},{3,5},{5,7},{7,1},{8,10},{10,12},{12... | collective-permute-start | bytes 221192 | tf_op jit(solution)/shard_map/ppermute | solution.py:933
  101.2 9.5 %collective-permute-start.12 = (bf16[1,4,24,768]{3,2,1,0:T(8,128)(2,1)S(1)}, bf16[1,4,24,768]{3,2,1,0:T(8,128)(2,1)S(1)}, u32[]{:S(2)}, u32[]{:S(2)}) collective-permute-start(bf16[1,4,24,768]{3,2,1,0:T(8,128)(2,1)S(1)} %get-tuple-element.114), channel_id=1, source_target_pairs={{0,1},{1,0},{2,3},{3,2},{4,5},{5,4},{6,7},{7,6},{8,9},{9,8},{10,11... | collective-permute-start | bytes 442376 | tf_op jit(solution)/shard_map/ppermute | solution.py:939
  109.1 8.8 %collective-permute-start.16 = (bf16[1,2,4,24,768]{4,3,2,1,0:T(8,128)(2,1)S(1)}, bf16[1,2,4,24,768]{4,3,2,1,0:T(8,128)(2,1)S(1)}, u32[]{:S(2)}, u32[]{:S(2)}) collective-permute-start(bf16[1,2,4,24,768]{4,3,2,1,0:T(8,128)(2,1)S(1)} %pad_maximum_fusion.11), channel_id=1, source_target_pairs={{0,1},{1,0},{2,3},{3,2},{4,5},{5,4},{6,7},{7,6},{8,9},{9,8},{10,11... | collective-permute-start | bytes 884744 | tf_op jit(solution)/shard_map/ppermute | solution.py:939
  110.7 8.5 %collective-permute-start.13 = (bf16[1,4,2,24,768]{4,3,1,2,0:T(8,128)(2,1)S(1)}, bf16[1,4,2,24,768]{4,3,1,2,0:T(8,128)(2,1)S(1)}, u32[]{:S(2)}, u32[]{:S(2)}) collective-permute-start(bf16[1,4,2,24,768]{4,3,1,2,0:T(8,128)(2,1)S(1)} %pad_maximum_fusion.10), channel_id=1, source_target_pairs={{0,16},{16,0},{1,17},{17,1},{2,18},{18,2},{3,19},{19,3},{4,20},{20... | collective-permute-start | bytes 884744 | tf_op jit(solution)/shard_map/ppermute | solution.py:939
  255.9 21.5 %collective-permute-start.19 = (bf16[4,2,120,384]{3,2,1,0:T(8,128)(2,1)}, bf16[4,2,120,384]{3,2,1,0:T(8,128)(2,1)S(1)}, u32[]{:S(2)}, u32[]{:S(2)}) collective-permute-start(bf16[4,2,120,384]{3,2,1,0:T(8,128)(2,1)} %get-tuple-element.142), channel_id=1, source_target_pairs={{0,16},{16,0},{1,17},{17,1},{2,18},{18,2},{3,19},{19,3},{4,20},{20... | collective-permute-start | bytes 2211848 | tf_op jit(solution)/shard_map/ppermute | solution.py:827
  257.4 22.7 %collective-permute-start.20 = (bf16[2,4,120,384]{3,2,1,0:T(8,128)(2,1)}, bf16[2,4,120,384]{3,2,1,0:T(8,128)(2,1)S(1)}, u32[]{:S(2)}, u32[]{:S(2)}) collective-permute-start(bf16[2,4,120,384]{3,2,1,0:T(8,128)(2,1)} %get-tuple-element.144), channel_id=1, source_target_pairs={{0,1},{1,0},{2,3},{3,2},{4,5},{5,4},{6,7},{7,6},{8,9},{9,8},{10,11... | collective-permute-start | bytes 2211848 | tf_op jit(solution)/shard_map/ppermute | solution.py:827
  284.1 19.8 %collective-permute-start.21 = (bf16[4,120,384]{2,1,0:T(8,128)(2,1)}, bf16[4,120,384]{2,1,0:T(8,128)(2,1)S(1)}, u32[]{:S(2)}, u32[]{:S(2)}) collective-permute-start(bf16[4,120,384]{2,1,0:T(8,128)(2,1)} %get-tuple-element.163), channel_id=1, source_target_pairs={{0,1},{1,0},{2,3},{3,2},{4,5},{5,4},{6,7},{7,6},{8,9},{9,8},{10,11... | collective-permute-start | bytes 1105928 | tf_op jit(solution)/shard_map/ppermute | solution.py:827
  284.6 19.4 %collective-permute-start.22 = (bf16[4,120,384]{2,1,0:T(8,128)(2,1)}, bf16[4,120,384]{2,1,0:T(8,128)(2,1)S(1)}, u32[]{:S(2)}, u32[]{:S(2)}) collective-permute-start(bf16[4,120,384]{2,1,0:T(8,128)(2,1)} %get-tuple-element.165), channel_id=1, source_target_pairs={{0,16},{16,0},{1,17},{17,1},{2,18},{18,2},{3,19},{19,3},{4,20},{20... | collective-permute-start | bytes 1105928 | tf_op jit(solution)/shard_map/ppermute | solution.py:827
  317.5 23.7 %collective-permute-start.27 = (bf16[4,2,88,384]{3,2,1,0:T(8,128)(2,1)}, bf16[4,2,88,384]{3,2,1,0:T(8,128)(2,1)S(1)}, u32[]{:S(2)}, u32[]{:S(2)}) collective-permute-start(bf16[4,2,88,384]{3,2,1,0:T(8,128)(2,1)} %get-tuple-element.187), channel_id=1, source_target_pairs={{0,16},{16,0},{1,17},{17,1},{2,18},{18,2},{3,19},{19,3},{4,20},{20... | collective-permute-start | bytes 1622024 | tf_op jit(solution)/shard_map/ppermute | solution.py:827
  318.0 23.1 %collective-permute-start.28 = (bf16[2,4,88,384]{3,2,1,0:T(8,128)(2,1)}, bf16[2,4,88,384]{3,2,1,0:T(8,128)(2,1)S(1)}, u32[]{:S(2)}, u32[]{:S(2)}) collective-permute-start(bf16[2,4,88,384]{3,2,1,0:T(8,128)(2,1)} %get-tuple-element.189), channel_id=1, source_target_pairs={{0,1},{1,0},{2,3},{3,2},{4,5},{5,4},{6,7},{7,6},{8,9},{9,8},{10,11... | collective-permute-start | bytes 1622024 | tf_op jit(solution)/shard_map/ppermute | solution.py:827
  319.6 12.8 %collective-permute-start.24 = (bf16[120,768]{1,0:T(8,128)(2,1)S(1)}, bf16[120,768]{1,0:T(8,128)(2,1)S(1)}, u32[]{:S(2)}, u32[]{:S(2)}) collective-permute-start(bf16[120,768]{1,0:T(8,128)(2,1)S(1)} %copy-done.28), channel_id=1, source_target_pairs={{0,2},{2,4},{4,6},{6,0},{1,3},{3,5},{5,7},{7,1},{8,10},{10,12},{12... | collective-permute-start | bytes 552968 | tf_op jit(solution)/shard_map/ppermute | solution.py:858
  319.6 21.5 %collective-permute-start.25 = (bf16[120,768]{1,0:T(8,128)(2,1)S(1)}, bf16[120,768]{1,0:T(8,128)(2,1)S(1)}, u32[]{:S(2)}, u32[]{:S(2)}) collective-permute-start(bf16[120,768]{1,0:T(8,128)(2,1)S(1)} %copy-done.27), channel_id=1, source_target_pairs={{0,4},{2,6},{4,0},{6,2},{1,5},{3,7},{5,1},{7,3},{8,12},{10,14},{12... | collective-permute-start | bytes 552968 | tf_op jit(solution)/shard_map/ppermute | solution.py:858
  321.2 20.0 %collective-permute-start.26 = (bf16[120,768]{1,0:T(8,128)(2,1)S(1)}, bf16[120,768]{1,0:T(8,128)(2,1)S(1)}, u32[]{:S(2)}, u32[]{:S(2)}) collective-permute-start(bf16[120,768]{1,0:T(8,128)(2,1)S(1)} %copy-done.26), channel_id=1, source_target_pairs={{0,6},{2,0},{4,2},{6,4},{1,7},{3,1},{5,3},{7,5},{8,14},{10,8},{12,... | collective-permute-start | bytes 552968 | tf_op jit(solution)/shard_map/ppermute | solution.py:858
  356.6 9.0 %collective-permute-start.31 = (bf16[88,768]{1,0:T(8,128)(2,1)}, bf16[88,768]{1,0:T(8,128)(2,1)S(1)}, u32[]{:S(2)}, u32[]{:S(2)}) collective-permute-start(bf16[88,768]{1,0:T(8,128)(2,1)} %get-tuple-element.195), channel_id=1, source_target_pairs={{0,2},{2,4},{4,6},{6,0},{1,3},{3,5},{5,7},{7,1},{8,10},{10,12},{12... | collective-permute-start | bytes 405512 | tf_op jit(solution)/shard_map/ppermute | solution.py:858
  361.2 8.8 %collective-permute-start.32 = (bf16[88,768]{1,0:T(8,128)(2,1)}, bf16[88,768]{1,0:T(8,128)(2,1)S(1)}, u32[]{:S(2)}, u32[]{:S(2)}) collective-permute-start(bf16[88,768]{1,0:T(8,128)(2,1)} %get-tuple-element.196), channel_id=1, source_target_pairs={{0,4},{2,6},{4,0},{6,2},{1,5},{3,7},{5,1},{7,3},{8,12},{10,14},{12... | collective-permute-start | bytes 405512 | tf_op jit(solution)/shard_map/ppermute | solution.py:858
  361.2 8.8 %collective-permute-start.33 = (bf16[88,768]{1,0:T(8,128)(2,1)}, bf16[88,768]{1,0:T(8,128)(2,1)S(1)}, u32[]{:S(2)}, u32[]{:S(2)}) collective-permute-start(bf16[88,768]{1,0:T(8,128)(2,1)} %get-tuple-element.197), channel_id=1, source_target_pairs={{0,6},{2,0},{4,2},{6,4},{1,7},{3,1},{5,3},{7,5},{8,14},{10,8},{12,... | collective-permute-start | bytes 405512 | tf_op jit(solution)/shard_map/ppermute | solution.py:858
  (43 other events, 301.5 us)
Sparse Core Ops, SparseCore 0:
  11.5 115.1 all-gather.2
  197.7 143.7 reduce-scatter.1

commit v4 on v3

--- a/solution.py
+++ b/solution.py
@@ -12,7 +12,7 @@
 HEAD_DIM = 64
 SEQ_MAX = 512
 PAIRS = HEADS // 2
-FINE = 256
+FINE = 512
 EPSILON = 1e-05
 MASKED = 1e30
 SCALE = HEAD_DIM ** (-0.5)
@@ -1000,8 +1000,8 @@
         one, own, d = self.one, self.own, self.d
         one.line()
         one.first()
+        self.two.out = after(self.two.out, one)
         one.second()
-        self.two.out = after(self.two.out, one)
         left, right = one.core()
         full = {"qk": left.reshape(2, -1, d), "v": right[..., :own, :].reshape(1, -1, d)}
         full.update(spread_small(right[..., own, : self.cut].reshape(-1, self.cut), own))
@@ -1100,7 +1100,8 @@
     hold(self_sum, (query_grad, cross))
     self_sum.first()
     self_sum.second()
-    proj_g, out_g, bias_g, gain_g, shift_g, dbin_g, dbout_g = scatter.finish(cross, self_sum.last(), send, dbin, own, devices)
+    selfs, dwin, dwout = lax.optimization_barrier((self_sum.last(), dwin, dwout))
+    proj_g, out_g, bias_g, gain_g, shift_g, dbin_g, dbout_g = scatter.finish(cross, selfs, send, dbin, own, devices)
     return (
         mixed, query_grad, memory_grad, proj_g, out_g, bias_g, gain_g, shift_g, dwin, dbin_g, dwout, dbout_g,
     )

time: 389 us -> 388 us (level)
    ppermute x12, waiting for transfers between devices: 38.5 us -> 31.9 us  [take_pair(): got = lax.ppermute(value, name, [(0, 1), (1, 0)])]
    ppermute x6, waiting for transfers between devices: 15.2 us -> 10.8 us  [last(): lax.ppermute(out, 'z', [(i, (i + step) % 4) for i in range(4)])]
    ppermute x10, waiting for transfers between devices: 17.9 us -> 22.2 us  [swap(): return lax.ppermute(value, name, [(0, 1), (1, 0)])]
  transfers between devices with their start and end apart: 36 -> 36, of which waited for: 19 -> 17; matrix products, arithmetic and copies ran while one was open for 6% -> 7% of each run, Pallas kernels for 33% -> 32%
where the time goes in v4:
time: 388 us; the launch traced here: 382 us
  Pallas kernels  197 us (51%)
  waiting for transfers between devices  76.1 us (20%)
  starting transfers between devices  53.7 us (14%)
  local copies, waits for them, and re-layouts  21.3 us (5%)
  other arithmetic  18.6 us (5%)
  between operations  15 us (4%)
    pallas_call x1, Pallas kernels, feed(): pl.pallas_call(functools.partial(feed_kernel, own), grid=(2, chunks), in_...  50.2 us
    pallas_call x3, Pallas kernels, one_back(): pl.pallas_call(kernel, grid=(1,), in_specs=specs + kept, out_specs=[at_ro...  42.6 us
    ppermute x12, waiting for transfers between devices, take_pair(): got = lax.ppermute(value, name, [(0, 1), (1, 0)])  31.9 us
    ppermute x6, starting transfers between devices, take_turns(): lax.ppermute(value, 'z', [(i, (i + step) % 4) for i in range(4)])  23.6 us
    ppermute x10, waiting for transfers between devices, swap(): return lax.ppermute(value, name, [(0, 1), (1, 0)])  22.2 us
    pallas_call x1, Pallas kernels, cross_forward(): pl.pallas_call(cross_forward_kernel, grid=(blocks,), in_specs=[row_block(...  20.6 us
    pallas_call x1, Pallas kernels, self_last(): pl.pallas_call(functools.partial(self_last_kernel, staged), grid=(1,), in...  17.7 us
    pallas_call x1, Pallas kernels, self_forward(): pl.pallas_call(self_forward_kernel, grid=(blocks,), in_specs=[row_block(d...  14.5 us
  transfers between devices with their start and end apart: 36, of which 17 were waited for; matrix products, arithmetic and copies ran while one was open for 7% of the time, Pallas kernels for 32%

profile of v4, /device:TPU:0, one launch (start us, length us, event | category | flops | bytes accessed | tf_op | source)
XLA Modules:
  0.0 381.9 jit_solution(4565262967447540792)
XLA Ops:
  19.5 5.5 %collective-permute-done.1 = bf16[1,80,768]{2,1,0:T(8,128)(2,1)S(1)} collective-permute-done((bf16[1,80,768]{2,1,0:T(8,128)(2,1)S(1)}, bf16[1,80,768]{2,1,0:T(8,128)(2,1)S(1)}, u32[]{:S(2)}, u32[]{:S(2)}) %collective-permute-start.1) | collective-permute-done | bytes 122912 | tf_op jit(solution)/shard_map/ppermute | solution.py:933
  41.4 7.3 %collective-permute-start.7 = (bf16[2,24,768]{2,1,0:T(8,128)(2,1)S(1)}, bf16[2,24,768]{2,1,0:T(8,128)(2,1)S(1)}, u32[]{:S(2)}, u32[]{:S(2)}) collective-permute-start(bf16[2,24,768]{2,1,0:T(8,128)(2,1)S(1)} %copy-done.17), channel_id=1, source_target_pairs={{0,2},{2,4},{4,6},{6,0},{1,3},{3,5},{5,7},{7,1},{8,10},{10,12},{12... | collective-permute-start | bytes 221192 | tf_op jit(solution)/shard_map/ppermute | solution.py:933
  48.7 5.3 %collective-permute-start.6 = (bf16[2,24,768]{2,1,0:T(8,128)(2,1)S(1)}, bf16[2,24,768]{2,1,0:T(8,128)(2,1)S(1)}, u32[]{:S(2)}, u32[]{:S(2)}) collective-permute-start(bf16[2,24,768]{2,1,0:T(8,128)(2,1)S(1)} %copy-done.17), channel_id=1, source_target_pairs={{0,4},{2,6},{4,0},{6,2},{1,5},{3,7},{5,1},{7,3},{8,12},{10,14},{12... | collective-permute-start | bytes 221192 | tf_op jit(solution)/shard_map/ppermute | solution.py:933
  58.8 5.3 %collective-permute-done.8 = bf16[2,4,2,24,768]{4,3,2,1,0:T(8,128)(2,1)S(1)} collective-permute-done((bf16[2,4,2,24,768]{4,3,2,1,0:T(8,128)(2,1)S(1)}, bf16[2,4,2,24,768]{4,3,2,1,0:T(8,128)(2,1)S(1)}, u32[]{:S(2)}, u32[]{:S(2)}) %collective-permute-start.8) | collective-permute-done | bytes 589856 | tf_op jit(solution)/shard_map/ppermute | solution.py:939
  74.0 14.5 %self_forward.1 = (bf16[1024,768]{1,0:T(8,128)(2,1)}, bf16[1024,768]{1,0:T(8,128)(2,1)}, bf16[1024,768]{1,0:T(8,128)(2,1)}, bf16[768,1024]{1,0:T(8,128)(2,1)}, f32[2,16,512]{2,1,0:T(8,128)}) custom-call(bf16[1024,768]{1,0:T(8,128)(2,1)} %x_ref.5, bf16[2,768,768]{2,1,0:T(8,128)(2,1)} %bitcast.124, bf16[1,768,768]{2,1,0:T(8,128)(2,1)} %bitcast.132, ...), custom_call_target="tpu_custom_call" | custom-call | flops 20000000000 | bytes 12000000 | tf_op jit(solution)/shard_map/self_forward/pallas_call | solution.py:592
  89.6 8.6 %collective-permute-done.15 = bf16[1,4,24,768]{3,2,1,0:T(8,128)(2,1)S(1)} collective-permute-done((bf16[1,4,24,768]{3,2,1,0:T(8,128)(2,1)S(1)}, bf16[1,4,24,768]{3,2,1,0:T(8,128)(2,1)S(1)}, u32[]{:S(2)}, u32[]{:S(2)}) %collective-permute-start.15) | collective-permute-done | bytes 147488 | tf_op jit(solution)/shard_map/ppermute | solution.py:939
  100.3 12.9 %collective-permute-done.16 = bf16[1,2,4,24,768]{4,3,2,1,0:T(8,128)(2,1)S(1)} collective-permute-done((bf16[1,2,4,24,768]{4,3,2,1,0:T(8,128)(2,1)S(1)}, bf16[1,2,4,24,768]{4,3,2,1,0:T(8,128)(2,1)S(1)}, u32[]{:S(2)}, u32[]{:S(2)}) %collective-permute-start.16) | collective-permute-done | bytes 294944 | tf_op jit(solution)/shard_map/ppermute | solution.py:939
  120.0 4.9 %all-gather.3.cloned.1.call-done.w_ref.win_ref.wk_ref.wv_ref = bf16[11,768,768]{2,1,0:T(8,128)(2,1)} async-done(((bf16[11,24,768]{2,1,0:T(8,128)(2,1)}), bf16[11,768,768]{2,1,0:T(8,128)(2,1)}) %all-gather.3.cloned.1.call-update) | async-done | bytes 12976144 | tf_op jit(solution)/shard_map/all_gather | solution.py:993
  124.9 20.6 %cross_forward.1 = (f32[1024,768]{1,0:T(8,128)}, bf16[1024,768]{1,0:T(8,128)(2,1)}, bf16[1024,768]{1,0:T(8,128)(2,1)}, bf16[1024,768]{1,0:T(8,128)(2,1)}, bf16[1...) custom-call(bf16[1024,768]{1,0:T(8,128)(2,1)} %x_ref.5, ...), custom_call_target="tpu_custom_call" | custom-call | flops 24000000000 | bytes 20000000 | tf_op jit(solution)/shard_map/cross_forward/pallas_call | solution.py:609
  145.6 50.2 %feed.1 = (bf16[1024,768]{1,0:T(8,128)(2,1)}, f32[1024,768]{1,0:T(8,128)}, bf16[768,6144]{1,0:T(8,128)(2,1)}, f32[1,3072]{1,0:T(1,128)}, f32[8,768]{1,0:T(8,128)}) custom-call(f32[1024,768]{1,0:T(8,128)} %get-tuple-element.122.ss_ref, bf16[1024,768]{1,0:T(8,128)(2,1)} %cot_ref.1, ...), custom_call_target="tpu_custom_call" | custom-call | flops 40000000000 | bytes 40000000 | tf_op jit(solution)/shard_map/feed/pallas_call | solution.py:638
  195.8 14.6 %cross_back_0.1 = (f32[1024,768]{1,0:T(8,128)}, bf16[1024,768]{1,0:T(8,128)(2,1)}, bf16[1024,768]{1,0:T(8,128)(2,1)}, bf16[1024,768]{1,0:T(8,128)(2,1)}, f32[8,768]{1,0:T(8,128)}) custom-call(f32[1024,768]{1,0:T(8,128)} %get-tuple-element.124.ssg_ref.refs_4_, f32[1024,768]{1,0:T(8,128)} %get-tuple-element.125.fs_ref, ...), custom_call_target="tpu_custom_call" | custom-call | flops 24999999488 | bytes 15000000 | tf_op jit(solution)/shard_map/cross_back_0/pallas_call | solution.py:692
  210.4 15.1 %cross_back_1.1 = (f32[1024,768]{1,0:T(8,128)}, bf16[1024,768]{1,0:T(8,128)(2,1)}, bf16[1024,768]{1,0:T(8,128)(2,1)}, bf16[1024,768]{1,0:T(8,128)(2,1)}, f32[8,768]{1,0:T(8,128)}) custom-call(f32[1024,768]{1,0:T(8,128)} %get-tuple-element.124.ssg_ref.refs_4_, ...), custom_call_target="tpu_custom_call", output_to_operand_aliasing={{0}: (12, {}), {1}: (13, {}), {2}: (14, {}), {3}: (15, {})} | custom-call | flops 24999999488 | bytes 15000000 | tf_op jit(solution)/shard_map/cross_back_1/pallas_call | solution.py:692
  225.5 14.4 %cross_weight.1 = (bf16[2,4,2,120,768]{4,3,2,1,0:T(8,128)(2,1)}, bf16[2,4,2,120,768]{4,3,2,1,0:T(8,128)(2,1)}) custom-call(s32[1]{0:T(128)} %bitcast.55.me_ref, bf16[1024,768]{1,0:T(8,128)(2,1)} %refs_0_.1, bf16[1024,768]{1,0:T(8,128)(2,1)} %get-tuple-element.141.refs_1_.dk_ref, bf16[1024,768]{1,0:T(8,128)(2,1)} %get-tuple-element.137.refs_2_.dv_ref, ...), custom_call_target="tpu_custom_call" | custom-call | flops 8999999488 | bytes 20000000 | tf_op jit(solution)/shard_map/cross_weight/pallas_call | solution.py:742
  240.7 6.2 %memory_input.1 = f32[1024,768]{1,0:T(8,128)} custom-call(bf16[1024,768]{1,0:T(8,128)(2,1)} %get-tuple-element.141.refs_1_.dk_ref, bf16[1024,768]{1,0:T(8,128)(2,1)} %get-tuple-element.137.refs_2_.dv_ref, bf16[11,768,768]{2,1,0:T(8,128)(2,1)} %all-gather.3.cloned.1.call-done.w_ref.win_ref.wk_ref.wv_ref, ...), custom_call_target="tpu_custom_call" | custom-call | flops 3000000000 | bytes 9000000 | tf_op jit(solution)/shard_map/memory_input/pallas_call | solution.py:788
  248.6 4.9 %first_stage.2 = (bf16[4,2,120,384]{3,2,1,0:T(8,128)(2,1)}, bf16[4,2,120,384]{3,2,1,0:T(8,128)(2,1)}, bf16[2,4,120,384]{3,2,1,0:T(8,128)(2,1)}, bf16[2,4,120,384]{3,2,1,0:T(8,128)(2,1)}) custom-call(s32[3]{0:T(128)} %pad_add_fusion.me_ref, bf16[2,4,2,120,768]{4,3,2,1,0:T(8,128)(2,1)} %get-tuple-element.142.keep_ref, bf16[2,4,2,120,768]{4,3,2,1,0:T(8,128)(2,1)} %copy-done), custom_call_target="tpu_custom_call" | custom-call | flops 1474560 | bytes 8847360 | tf_op jit(solution)/shard_map/first_stage/pallas_call | solution.py:537
  256.2 12.9 %self_back_0.1 = (bf16[1024,768]{1,0:T(8,128)(2,1)}, bf16[1024,768]{1,0:T(8,128)(2,1)}, bf16[1024,768]{1,0:T(8,128)(2,1)}, f32[8,768]{1,0:T(8,128)}) custom-call(f32[1024,768]{1,0:T(8,128)} %get-tuple-element.181.refs_6_.fsg_ref, bf16[1024,768]{1,0:T(8,128)(2,1)} %get-tuple-element.154.q_ref, bf16[1024,768]{1,0:T(8,128)(2,1)} %get-tuple-element.155.k_ref, ...), custom_call_target="tpu_custom_call" | custom-call | flops 24999999488 | bytes 15000000 | tf_op jit(solution)/shard_map/self_back_0/pallas_call | solution.py:692
  270.5 10.8 %collective-permute-done.19.gl_ref = bf16[4,2,120,384]{3,2,1,0:T(8,128)(2,1)S(1)} collective-permute-done((bf16[4,2,120,384]{3,2,1,0:T(8,128)(2,1)}, bf16[4,2,120,384]{3,2,1,0:T(8,128)(2,1)S(1)}, u32[]{:S(2)}, u32[]{:S(2)}) %collective-permute-start.19) | collective-permute-done | bytes 737312 | tf_op jit(solution)/shard_map/ppermute | solution.py:827
  287.8 17.7 %self_last.1 = (bf16[2,4,2,88,768]{4,3,2,1,0:T(8,128)(2,1)}, bf16[2,4,2,88,768]{4,3,2,1,0:T(8,128)(2,1)}, bf16[1024,768]{1,0:T(8,128)(2,1)}, bf16[1024,768]{1,0:T(8,128)(2,1)}, bf16[1024,768]{1,0:T(8,128)(2,1)}) custom-call(s32[1]{0:T(128)} %bitcast.55.me_ref, ...), custom_call_target="tpu_custom_call", output_to_operand_aliasing={{2}: (13, {}), {3}: (14, {}), {4}: (15, {})} | custom-call | flops 24999999488 | bytes 20000000 | tf_op jit(solution)/shard_map/self_last/pallas_call | solution.py:767
  308.8 4.5 %collective-permute-done.23.got_ref = bf16[2,4,2,88,768]{4,3,2,1,0:T(8,128)(2,1)S(1)} collective-permute-done((bf16[2,4,2,88,768]{4,3,2,1,0:T(8,128)(2,1)}, bf16[2,4,2,88,768]{4,3,2,1,0:T(8,128)(2,1)S(1)}, u32[]{:S(2)}, u32[]{:S(2)}) %collective-permute-start.23) | collective-permute-done | bytes 2162720 | tf_op jit(solution)/shard_map/ppermute | solution.py:827
  314.7 4.4 %first_stage.3 = (bf16[4,2,88,384]{3,2,1,0:T(8,128)(2,1)}, bf16[4,2,88,384]{3,2,1,0:T(8,128)(2,1)}, bf16[2,4,88,384]{3,2,1,0:T(8,128)(2,1)}, bf16[2,4,88,384]{3,2,1,0:T(8,128)(2,1)}) custom-call(s32[3]{0:T(128)} %pad_add_fusion.me_ref, bf16[2,4,2,88,768]{4,3,2,1,0:T(8,128)(2,1)} %get-tuple-element.166.keep_ref, bf16[2,4,2,88,768]{4,3,2,1,0:T(8,128)(2,1)} %copy-done.1), custom_call_target="tpu_custom_call" | custom-call | flops 1081344 | bytes 6488064 | tf_op jit(solution)/shard_map/first_stage/pallas_call | solution.py:537
  326.7 8.7 %self_input.1 = f32[1024,768]{1,0:T(8,128)} custom-call(f32[1024,768]{1,0:T(8,128)} %get-tuple-element.181.refs_6_.fsg_ref, bf16[1024,768]{1,0:T(8,128)(2,1)} %get-tuple-element.182.dq_ref, bf16[1024,768]{1,0:T(8,128)(2,1)} %get-tuple-element.183.dk_ref, bf16[1024,768]{1,0:T(8,128)(2,1)} %get-tuple-element.184.dv_ref, bf16[2,768,768]{2,1,0:T(8,128)(2,1)} %bitcast.125, ...), custom_call_target="tpu_custom_call" | custom-call | flops 4000000000 | bytes 14000000 | tf_op jit(solution)/shard_map/self_input/pallas_call | solution.py:802
  335.4 6.4 %collective-permute-done.25.refs_2_ = bf16[120,768]{1,0:T(8,128)(2,1)S(1)} collective-permute-done((bf16[120,768]{1,0:T(8,128)(2,1)S(1)}, bf16[120,768]{1,0:T(8,128)(2,1)S(1)}, u32[]{:S(2)}, u32[]{:S(2)}) %collective-permute-start.25) | collective-permute-done | bytes 184352 | tf_op jit(solution)/shard_map/ppermute | solution.py:858
  348.3 6.5 %collective-permute-done.29.gl_ref = bf16[4,88,384]{2,1,0:T(8,128)(2,1)S(1)} collective-permute-done((bf16[4,88,384]{2,1,0:T(8,128)(2,1)}, bf16[4,88,384]{2,1,0:T(8,128)(2,1)S(1)}, u32[]{:S(2)}, u32[]{:S(2)}) %collective-permute-start.29) | collective-permute-done | bytes 270368 | tf_op jit(solution)/shard_map/ppermute | solution.py:827
  357.9 4.5 %collective-permute-start.31 = (bf16[88,768]{1,0:T(8,128)(2,1)}, bf16[88,768]{1,0:T(8,128)(2,1)S(1)}, u32[]{:S(2)}, u32[]{:S(2)}) collective-permute-start(bf16[88,768]{1,0:T(8,128)(2,1)} %get-tuple-element.201), channel_id=1, source_target_pairs={{0,2},{2,4},{4,6},{6,0},{1,3},{3,5},{5,7},{7,1},{8,10},{10,12},{12... | collective-permute-start | bytes 405512 | tf_op jit(solution)/shard_map/ppermute | solution.py:858
  (216 shorter events, 100.1 us)
Async XLA Ops:
  7.3 117.7 %all-gather.3.cloned.1.call-start = ((), (), s32[]{:S(2)}) async-start(), calls=%async_computation.2 | async-start | bytes 13381632 | tf_op jit(solution)/shard_map/all_gather | solution.py:993
  11.0 353.8 %reduce-scatter.2.cloned.1.call-start = ((), (), s32[]{:S(2)}) async-start(), calls=%async_computation.1 | async-start | bytes 9732096 | tf_op jit(solution)/shard_map/reduce_scatter | solution.py:882
  11.5 13.6 %collective-permute-start.1 = (bf16[1,80,768]{2,1,0:T(8,128)(2,1)S(1)}, bf16[1,80,768]{2,1,0:T(8,128)(2,1)S(1)}, u32[]{:S(2)}, u32[]{:S(2)}) collective-permute-start(bf16[1,80,768]{2,1,0:T(8,128)(2,1)S(1)} %fusion.10), channel_id=1, source_target_pairs={{0,4},{2,6},{4,0},{6,2},{1,5},{3,7},{5,1},{7,3},{8,12},{10,14},{12... | collective-permute-start | bytes 368648 | tf_op jit(solution)/shard_map/ppermute | solution.py:933
  15.6 9.5 %collective-permute-start.2 = (bf16[1,80,768]{2,1,0:T(8,128)(2,1)S(1)}, bf16[1,80,768]{2,1,0:T(8,128)(2,1)S(1)}, u32[]{:S(2)}, u32[]{:S(2)}) collective-permute-start(bf16[1,80,768]{2,1,0:T(8,128)(2,1)S(1)} %fusion.10), channel_id=1, source_target_pairs={{0,2},{2,4},{4,6},{6,0},{1,3},{3,5},{5,7},{7,1},{8,10},{10,12},{12... | collective-permute-start | bytes 368648 | tf_op jit(solution)/shard_map/ppermute | solution.py:933
  37.4 19.6 %collective-permute-start.10 = (bf16[1,2,4,32,768]{4,2,3,1,0:T(4,128)(2,1)S(1)}, bf16[1,2,4,32,768]{4,2,3,1,0:T(4,128)(2,1)S(1)}, u32[]{:S(2)}, u32[]{:S(2)}) collective-permute-start(bf16[1,2,4,32,768]{4,2,3,1,0:T(4,128)(2,1)S(1)} %pad_maximum_fusion.8), channel_id=1, source_target_pairs={{0,1},{1,0},{2,3},{3,2},{4,5},{5,4},{6,7},{7,6},{8,9},{9,8},{10,11... | collective-permute-start | bytes 1179656 | tf_op jit(solution)/shard_map/ppermute | solution.py:939
  40.8 23.3 %collective-permute-start.8 = (bf16[2,4,2,24,768]{4,3,2,1,0:T(8,128)(2,1)S(1)}, bf16[2,4,2,24,768]{4,3,2,1,0:T(8,128)(2,1)S(1)}, u32[]{:S(2)}, u32[]{:S(2)}) collective-permute-start(bf16[2,4,2,24,768]{4,3,2,1,0:T(8,128)(2,1)S(1)} %pad_maximum_fusion.3), channel_id=1, source_target_pairs={{0,16},{16,0},{1,17},{17,1},{2,18},{18,2},{3,19},{19,3},{4,20},{20... | collective-permute-start | bytes 1769480 | tf_op jit(solution)/shard_map/ppermute | solution.py:939
  41.4 24.7 %collective-permute-start.7 = (bf16[2,24,768]{2,1,0:T(8,128)(2,1)S(1)}, bf16[2,24,768]{2,1,0:T(8,128)(2,1)S(1)}, u32[]{:S(2)}, u32[]{:S(2)}) collective-permute-start(bf16[2,24,768]{2,1,0:T(8,128)(2,1)S(1)} %copy-done.17), channel_id=1, source_target_pairs={{0,2},{2,4},{4,6},{6,0},{1,3},{3,5},{5,7},{7,1},{8,10},{10,12},{12... | collective-permute-start | bytes 221192 | tf_op jit(solution)/shard_map/ppermute | solution.py:933
  48.7 17.4 %collective-permute-start.6 = (bf16[2,24,768]{2,1,0:T(8,128)(2,1)S(1)}, bf16[2,24,768]{2,1,0:T(8,128)(2,1)S(1)}, u32[]{:S(2)}, u32[]{:S(2)}) collective-permute-start(bf16[2,24,768]{2,1,0:T(8,128)(2,1)S(1)} %copy-done.17), channel_id=1, source_target_pairs={{0,4},{2,6},{4,0},{6,2},{1,5},{3,7},{5,1},{7,3},{8,12},{10,14},{12... | collective-permute-start | bytes 221192 | tf_op jit(solution)/shard_map/ppermute | solution.py:933
  53.9 12.2 %collective-permute-start.5 = (bf16[2,24,768]{2,1,0:T(8,128)(2,1)S(1)}, bf16[2,24,768]{2,1,0:T(8,128)(2,1)}, u32[]{:S(2)}, u32[]{:S(2)}) collective-permute-start(bf16[2,24,768]{2,1,0:T(8,128)(2,1)S(1)} %copy-done.17), channel_id=1, source_target_pairs={{0,6},{2,0},{4,2},{6,4},{1,7},{3,1},{5,3},{7,5},{8,14},{10,8},{12,... | collective-permute-start | bytes 221192 | tf_op jit(solution)/shard_map/ppermute | solution.py:933
  88.6 9.7 %collective-permute-start.15 = (bf16[1,4,24,768]{3,2,1,0:T(8,128)(2,1)S(1)}, bf16[1,4,24,768]{3,2,1,0:T(8,128)(2,1)S(1)}, u32[]{:S(2)}, u32[]{:S(2)}) collective-permute-start(bf16[1,4,24,768]{3,2,1,0:T(8,128)(2,1)S(1)} %bitcast.131), channel_id=1, source_target_pairs={{0,16},{16,0},{1,17},{17,1},{2,18},{18,2},{3,19},{19,3},{4,20},{20... | collective-permute-start | bytes 442376 | tf_op jit(solution)/shard_map/ppermute | solution.py:939
  89.1 9.6 %collective-permute-start.12 = (bf16[1,4,24,768]{3,2,1,0:T(8,128)(2,1)S(1)}, bf16[1,4,24,768]{3,2,1,0:T(8,128)(2,1)S(1)}, u32[]{:S(2)}, u32[]{:S(2)}) collective-permute-start(bf16[1,4,24,768]{3,2,1,0:T(8,128)(2,1)S(1)} %get-tuple-element.120), channel_id=1, source_target_pairs={{0,1},{1,0},{2,3},{3,2},{4,5},{5,4},{6,7},{7,6},{8,9},{9,8},{10,11... | collective-permute-start | bytes 442376 | tf_op jit(solution)/shard_map/ppermute | solution.py:939
  98.4 14.9 %collective-permute-start.16 = (bf16[1,2,4,24,768]{4,3,2,1,0:T(8,128)(2,1)S(1)}, bf16[1,2,4,24,768]{4,3,2,1,0:T(8,128)(2,1)S(1)}, u32[]{:S(2)}, u32[]{:S(2)}) collective-permute-start(bf16[1,2,4,24,768]{4,3,2,1,0:T(8,128)(2,1)S(1)} %pad_maximum_fusion.11), channel_id=1, source_target_pairs={{0,1},{1,0},{2,3},{3,2},{4,5},{5,4},{6,7},{7,6},{8,9},{9,8},{10,11... | collective-permute-start | bytes 884744 | tf_op jit(solution)/shard_map/ppermute | solution.py:939
  98.8 14.6 %collective-permute-start.13 = (bf16[1,4,2,24,768]{4,3,1,2,0:T(8,128)(2,1)S(1)}, bf16[1,4,2,24,768]{4,3,1,2,0:T(8,128)(2,1)S(1)}, u32[]{:S(2)}, u32[]{:S(2)}) collective-permute-start(bf16[1,4,2,24,768]{4,3,1,2,0:T(8,128)(2,1)S(1)} %pad_maximum_fusion.10), channel_id=1, source_target_pairs={{0,16},{16,0},{1,17},{17,1},{2,18},{18,2},{3,19},{19,3},{4,20},{20... | collective-permute-start | bytes 884744 | tf_op jit(solution)/shard_map/ppermute | solution.py:939
  253.4 27.9 %collective-permute-start.19 = (bf16[4,2,120,384]{3,2,1,0:T(8,128)(2,1)}, bf16[4,2,120,384]{3,2,1,0:T(8,128)(2,1)S(1)}, u32[]{:S(2)}, u32[]{:S(2)}) collective-permute-start(bf16[4,2,120,384]{3,2,1,0:T(8,128)(2,1)} %get-tuple-element.148), channel_id=1, source_target_pairs={{0,16},{16,0},{1,17},{17,1},{2,18},{18,2},{3,19},{19,3},{4,20},{20... | collective-permute-start | bytes 2211848 | tf_op jit(solution)/shard_map/ppermute | solution.py:827
  255.5 26.0 %collective-permute-start.20 = (bf16[2,4,120,384]{3,2,1,0:T(8,128)(2,1)}, bf16[2,4,120,384]{3,2,1,0:T(8,128)(2,1)S(1)}, u32[]{:S(2)}, u32[]{:S(2)}) collective-permute-start(bf16[2,4,120,384]{3,2,1,0:T(8,128)(2,1)} %get-tuple-element.150), channel_id=1, source_target_pairs={{0,1},{1,0},{2,3},{3,2},{4,5},{5,4},{6,7},{7,6},{8,9},{9,8},{10,11... | collective-permute-start | bytes 2211848 | tf_op jit(solution)/shard_map/ppermute | solution.py:827
  285.6 20.0 %collective-permute-start.21 = (bf16[4,120,384]{2,1,0:T(8,128)(2,1)}, bf16[4,120,384]{2,1,0:T(8,128)(2,1)S(1)}, u32[]{:S(2)}, u32[]{:S(2)}) collective-permute-start(bf16[4,120,384]{2,1,0:T(8,128)(2,1)} %get-tuple-element.169), channel_id=1, source_target_pairs={{0,1},{1,0},{2,3},{3,2},{4,5},{5,4},{6,7},{7,6},{8,9},{9,8},{10,11... | collective-permute-start | bytes 1105928 | tf_op jit(solution)/shard_map/ppermute | solution.py:827
  286.2 19.3 %collective-permute-start.22 = (bf16[4,120,384]{2,1,0:T(8,128)(2,1)}, bf16[4,120,384]{2,1,0:T(8,128)(2,1)S(1)}, u32[]{:S(2)}, u32[]{:S(2)}) collective-permute-start(bf16[4,120,384]{2,1,0:T(8,128)(2,1)} %get-tuple-element.171), channel_id=1, source_target_pairs={{0,16},{16,0},{1,17},{17,1},{2,18},{18,2},{3,19},{19,3},{4,20},{20... | collective-permute-start | bytes 1105928 | tf_op jit(solution)/shard_map/ppermute | solution.py:827
  319.1 22.7 %collective-permute-start.27 = (bf16[4,2,88,384]{3,2,1,0:T(8,128)(2,1)}, bf16[4,2,88,384]{3,2,1,0:T(8,128)(2,1)S(1)}, u32[]{:S(2)}, u32[]{:S(2)}) collective-permute-start(bf16[4,2,88,384]{3,2,1,0:T(8,128)(2,1)} %get-tuple-element.193), channel_id=1, source_target_pairs={{0,16},{16,0},{1,17},{17,1},{2,18},{18,2},{3,19},{19,3},{4,20},{20... | collective-permute-start | bytes 1622024 | tf_op jit(solution)/shard_map/ppermute | solution.py:827
  319.6 22.2 %collective-permute-start.28 = (bf16[2,4,88,384]{3,2,1,0:T(8,128)(2,1)}, bf16[2,4,88,384]{3,2,1,0:T(8,128)(2,1)S(1)}, u32[]{:S(2)}, u32[]{:S(2)}) collective-permute-start(bf16[2,4,88,384]{3,2,1,0:T(8,128)(2,1)} %get-tuple-element.195), channel_id=1, source_target_pairs={{0,1},{1,0},{2,3},{3,2},{4,5},{5,4},{6,7},{7,6},{8,9},{9,8},{10,11... | collective-permute-start | bytes 1622024 | tf_op jit(solution)/shard_map/ppermute | solution.py:827
  320.9 14.5 %collective-permute-start.24 = (bf16[120,768]{1,0:T(8,128)(2,1)S(1)}, bf16[120,768]{1,0:T(8,128)(2,1)S(1)}, u32[]{:S(2)}, u32[]{:S(2)}) collective-permute-start(bf16[120,768]{1,0:T(8,128)(2,1)S(1)} %copy-done.28), channel_id=1, source_target_pairs={{0,2},{2,4},{4,6},{6,0},{1,3},{3,5},{5,7},{7,1},{8,10},{10,12},{12... | collective-permute-start | bytes 552968 | tf_op jit(solution)/shard_map/ppermute | solution.py:858
  322.8 19.0 %collective-permute-start.25 = (bf16[120,768]{1,0:T(8,128)(2,1)S(1)}, bf16[120,768]{1,0:T(8,128)(2,1)S(1)}, u32[]{:S(2)}, u32[]{:S(2)}) collective-permute-start(bf16[120,768]{1,0:T(8,128)(2,1)S(1)} %copy-done.27), channel_id=1, source_target_pairs={{0,4},{2,6},{4,0},{6,2},{1,5},{3,7},{5,1},{7,3},{8,12},{10,14},{12... | collective-permute-start | bytes 552968 | tf_op jit(solution)/shard_map/ppermute | solution.py:858
  324.9 16.9 %collective-permute-start.26 = (bf16[120,768]{1,0:T(8,128)(2,1)S(1)}, bf16[120,768]{1,0:T(8,128)(2,1)S(1)}, u32[]{:S(2)}, u32[]{:S(2)}) collective-permute-start(bf16[120,768]{1,0:T(8,128)(2,1)S(1)} %copy-done.26), channel_id=1, source_target_pairs={{0,6},{2,0},{4,2},{6,4},{1,7},{3,1},{5,3},{7,5},{8,14},{10,8},{12,... | collective-permute-start | bytes 552968 | tf_op jit(solution)/shard_map/ppermute | solution.py:858
  357.9 9.7 %collective-permute-start.31 = (bf16[88,768]{1,0:T(8,128)(2,1)}, bf16[88,768]{1,0:T(8,128)(2,1)S(1)}, u32[]{:S(2)}, u32[]{:S(2)}) collective-permute-start(bf16[88,768]{1,0:T(8,128)(2,1)} %get-tuple-element.201), channel_id=1, source_target_pairs={{0,2},{2,4},{4,6},{6,0},{1,3},{3,5},{5,7},{7,1},{8,10},{10,12},{12... | collective-permute-start | bytes 405512 | tf_op jit(solution)/shard_map/ppermute | solution.py:858
  362.4 9.4 %collective-permute-start.32 = (bf16[88,768]{1,0:T(8,128)(2,1)}, bf16[88,768]{1,0:T(8,128)(2,1)S(1)}, u32[]{:S(2)}, u32[]{:S(2)}) collective-permute-start(bf16[88,768]{1,0:T(8,128)(2,1)} %get-tuple-element.202), channel_id=1, source_target_pairs={{0,4},{2,6},{4,0},{6,2},{1,5},{3,7},{5,1},{7,3},{8,12},{10,14},{12... | collective-permute-start | bytes 405512 | tf_op jit(solution)/shard_map/ppermute | solution.py:858
  (43 other events, 317.6 us)
Sparse Core Ops, SparseCore 0:
  11.5 113.3 all-gather.2
  195.9 162.4 reduce-scatter.1

commit v5 on v4

--- a/solution.py
+++ b/solution.py
@@ -1097,8 +1097,9 @@
     upstream = after(fsg, self_sum, cross_sum)
     query_grad = self_input(upstream, dq, dk, dv, full["qk"], full["v"])
     cross = cross_sum.last()
-    hold(self_sum, (query_grad, cross))
+    hold(self_sum, query_grad)
     self_sum.first()
+    hold(self_sum, cross)
     self_sum.second()
     selfs, dwin, dwout = lax.optimization_barrier((self_sum.last(), dwin, dwout))
     proj_g, out_g, bias_g, gain_g, shift_g, dbin_g, dbout_g = scatter.finish(cross, selfs, send, dbin, own, devices)

time: 388 us -> 392 us (1.010)
  waiting for transfers between devices: 76.1 us -> 80.5 us
    ppermute x6, waiting for transfers between devices: 10.8 us -> 17.8 us  [last(): lax.ppermute(out, 'z', [(i, (i + step) % 4) for i in range(4)])]
  transfers between devices with their start and end apart: 36 -> 36, of which waited for: 17 -> 18; matrix products, arithmetic and copies ran while one was open for 7% -> 7% of each run, Pallas kernels for 32% -> 32%
where the time goes in v5:
time: 392 us; the launch traced here: 386 us
  Pallas kernels  197 us (50%)
  waiting for transfers between devices  80.5 us (21%)
  starting transfers between devices  53.3 us (14%)
  local copies, waits for them, and re-layouts  21.8 us (6%)
  other arithmetic  18.6 us (5%)
  between operations  15 us (4%)
    pallas_call x1, Pallas kernels, feed(): pl.pallas_call(functools.partial(feed_kernel, own), grid=(2, chunks), in_...  50.2 us
    pallas_call x3, Pallas kernels, one_back(): pl.pallas_call(kernel, grid=(1,), in_specs=specs + kept, out_specs=[at_ro...  42.6 us
    ppermute x12, waiting for transfers between devices, take_pair(): got = lax.ppermute(value, name, [(0, 1), (1, 0)])  31.9 us
    ppermute x6, starting transfers between devices, take_turns(): lax.ppermute(value, 'z', [(i, (i + step) % 4) for i in range(4)])  23.6 us
    pallas_call x1, Pallas kernels, cross_forward(): pl.pallas_call(cross_forward_kernel, grid=(blocks,), in_specs=[row_block(...  20.6 us
    ppermute x10, waiting for transfers between devices, swap(): return lax.ppermute(value, name, [(0, 1), (1, 0)])  19.6 us
    ppermute x6, waiting for transfers between devices, last(): lax.ppermute(out, 'z', [(i, (i + step) % 4) for i in range(4)])  17.8 us
    pallas_call x1, Pallas kernels, self_last(): pl.pallas_call(functools.partial(self_last_kernel, staged), grid=(1,), in...  17.7 us
  transfers between devices with their start and end apart: 36, of which 18 were waited for; matrix products, arithmetic and copies ran while one was open for 7% of the time, Pallas kernels for 32%

profile of v5, /device:TPU:0, one launch (start us, length us, event | category | flops | bytes accessed | tf_op | source)
XLA Modules:
  0.0 386.4 jit_solution(10584137275240020066)
XLA Ops:
  19.5 5.5 %collective-permute-done.1 = bf16[1,80,768]{2,1,0:T(8,128)(2,1)S(1)} collective-permute-done((bf16[1,80,768]{2,1,0:T(8,128)(2,1)S(1)}, bf16[1,80,768]{2,1,0:T(8,128)(2,1)S(1)}, u32[]{:S(2)}, u32[]{:S(2)}) %collective-permute-start.1) | collective-permute-done | bytes 122912 | tf_op jit(solution)/shard_map/ppermute | solution.py:933
  41.4 7.3 %collective-permute-start.7 = (bf16[2,24,768]{2,1,0:T(8,128)(2,1)S(1)}, bf16[2,24,768]{2,1,0:T(8,128)(2,1)S(1)}, u32[]{:S(2)}, u32[]{:S(2)}) collective-permute-start(bf16[2,24,768]{2,1,0:T(8,128)(2,1)S(1)} %copy-done.17), channel_id=1, source_target_pairs={{0,2},{2,4},{4,6},{6,0},{1,3},{3,5},{5,7},{7,1},{8,10},{10,12},{12... | collective-permute-start | bytes 221192 | tf_op jit(solution)/shard_map/ppermute | solution.py:933
  48.7 5.3 %collective-permute-start.6 = (bf16[2,24,768]{2,1,0:T(8,128)(2,1)S(1)}, bf16[2,24,768]{2,1,0:T(8,128)(2,1)S(1)}, u32[]{:S(2)}, u32[]{:S(2)}) collective-permute-start(bf16[2,24,768]{2,1,0:T(8,128)(2,1)S(1)} %copy-done.17), channel_id=1, source_target_pairs={{0,4},{2,6},{4,0},{6,2},{1,5},{3,7},{5,1},{7,3},{8,12},{10,14},{12... | collective-permute-start | bytes 221192 | tf_op jit(solution)/shard_map/ppermute | solution.py:933
  58.8 5.3 %collective-permute-done.8 = bf16[2,4,2,24,768]{4,3,2,1,0:T(8,128)(2,1)S(1)} collective-permute-done((bf16[2,4,2,24,768]{4,3,2,1,0:T(8,128)(2,1)S(1)}, bf16[2,4,2,24,768]{4,3,2,1,0:T(8,128)(2,1)S(1)}, u32[]{:S(2)}, u32[]{:S(2)}) %collective-permute-start.8) | collective-permute-done | bytes 589856 | tf_op jit(solution)/shard_map/ppermute | solution.py:939
  74.0 14.5 %self_forward.1 = (bf16[1024,768]{1,0:T(8,128)(2,1)}, bf16[1024,768]{1,0:T(8,128)(2,1)}, bf16[1024,768]{1,0:T(8,128)(2,1)}, bf16[768,1024]{1,0:T(8,128)(2,1)}, f32[2,16,512]{2,1,0:T(8,128)}) custom-call(bf16[1024,768]{1,0:T(8,128)(2,1)} %x_ref.5, bf16[2,768,768]{2,1,0:T(8,128)(2,1)} %bitcast.124, bf16[1,768,768]{2,1,0:T(8,128)(2,1)} %bitcast.132, ...), custom_call_target="tpu_custom_call" | custom-call | flops 20000000000 | bytes 12000000 | tf_op jit(solution)/shard_map/self_forward/pallas_call | solution.py:592
  89.6 8.6 %collective-permute-done.15 = bf16[1,4,24,768]{3,2,1,0:T(8,128)(2,1)S(1)} collective-permute-done((bf16[1,4,24,768]{3,2,1,0:T(8,128)(2,1)S(1)}, bf16[1,4,24,768]{3,2,1,0:T(8,128)(2,1)S(1)}, u32[]{:S(2)}, u32[]{:S(2)}) %collective-permute-start.15) | collective-permute-done | bytes 147488 | tf_op jit(solution)/shard_map/ppermute | solution.py:939
  100.3 12.9 %collective-permute-done.16 = bf16[1,2,4,24,768]{4,3,2,1,0:T(8,128)(2,1)S(1)} collective-permute-done((bf16[1,2,4,24,768]{4,3,2,1,0:T(8,128)(2,1)S(1)}, bf16[1,2,4,24,768]{4,3,2,1,0:T(8,128)(2,1)S(1)}, u32[]{:S(2)}, u32[]{:S(2)}) %collective-permute-start.16) | collective-permute-done | bytes 294944 | tf_op jit(solution)/shard_map/ppermute | solution.py:939
  120.0 5.0 %all-gather.3.cloned.1.call-done.w_ref.win_ref.wk_ref.wv_ref = bf16[11,768,768]{2,1,0:T(8,128)(2,1)} async-done(((bf16[11,24,768]{2,1,0:T(8,128)(2,1)}), bf16[11,768,768]{2,1,0:T(8,128)(2,1)}) %all-gather.3.cloned.1.call-update) | async-done | bytes 12976144 | tf_op jit(solution)/shard_map/all_gather | solution.py:993
  125.0 20.6 %cross_forward.1 = (f32[1024,768]{1,0:T(8,128)}, bf16[1024,768]{1,0:T(8,128)(2,1)}, bf16[1024,768]{1,0:T(8,128)(2,1)}, bf16[1024,768]{1,0:T(8,128)(2,1)}, bf16[1...) custom-call(bf16[1024,768]{1,0:T(8,128)(2,1)} %x_ref.5, ...), custom_call_target="tpu_custom_call" | custom-call | flops 24000000000 | bytes 20000000 | tf_op jit(solution)/shard_map/cross_forward/pallas_call | solution.py:609
  145.6 50.2 %feed.1 = (bf16[1024,768]{1,0:T(8,128)(2,1)}, f32[1024,768]{1,0:T(8,128)}, bf16[768,6144]{1,0:T(8,128)(2,1)}, f32[1,3072]{1,0:T(1,128)}, f32[8,768]{1,0:T(8,128)}) custom-call(f32[1024,768]{1,0:T(8,128)} %get-tuple-element.124.ss_ref, bf16[1024,768]{1,0:T(8,128)(2,1)} %cot_ref.1, ...), custom_call_target="tpu_custom_call" | custom-call | flops 40000000000 | bytes 40000000 | tf_op jit(solution)/shard_map/feed/pallas_call | solution.py:638
  195.8 14.6 %cross_back_0.1 = (f32[1024,768]{1,0:T(8,128)}, bf16[1024,768]{1,0:T(8,128)(2,1)}, bf16[1024,768]{1,0:T(8,128)(2,1)}, bf16[1024,768]{1,0:T(8,128)(2,1)}, f32[8,768]{1,0:T(8,128)}) custom-call(f32[1024,768]{1,0:T(8,128)} %get-tuple-element.126.ssg_ref.refs_4_, f32[1024,768]{1,0:T(8,128)} %get-tuple-element.127.fs_ref, ...), custom_call_target="tpu_custom_call" | custom-call | flops 24999999488 | bytes 15000000 | tf_op jit(solution)/shard_map/cross_back_0/pallas_call | solution.py:692
  210.4 15.1 %cross_back_1.1 = (f32[1024,768]{1,0:T(8,128)}, bf16[1024,768]{1,0:T(8,128)(2,1)}, bf16[1024,768]{1,0:T(8,128)(2,1)}, bf16[1024,768]{1,0:T(8,128)(2,1)}, f32[8,768]{1,0:T(8,128)}) custom-call(f32[1024,768]{1,0:T(8,128)} %get-tuple-element.126.ssg_ref.refs_4_, ...), custom_call_target="tpu_custom_call", output_to_operand_aliasing={{0}: (12, {}), {1}: (13, {}), {2}: (14, {}), {3}: (15, {})} | custom-call | flops 24999999488 | bytes 15000000 | tf_op jit(solution)/shard_map/cross_back_1/pallas_call | solution.py:692
  225.6 14.4 %cross_weight.1 = (bf16[2,4,2,120,768]{4,3,2,1,0:T(8,128)(2,1)}, bf16[2,4,2,120,768]{4,3,2,1,0:T(8,128)(2,1)}) custom-call(s32[1]{0:T(128)} %bitcast.55.me_ref, bf16[1024,768]{1,0:T(8,128)(2,1)} %refs_0_.1, bf16[1024,768]{1,0:T(8,128)(2,1)} %get-tuple-element.143.refs_1_.dk_ref, bf16[1024,768]{1,0:T(8,128)(2,1)} %get-tuple-element.139.refs_2_.dv_ref, ...), custom_call_target="tpu_custom_call" | custom-call | flops 8999999488 | bytes 20000000 | tf_op jit(solution)/shard_map/cross_weight/pallas_call | solution.py:742
  240.8 6.2 %memory_input.1 = f32[1024,768]{1,0:T(8,128)} custom-call(bf16[1024,768]{1,0:T(8,128)(2,1)} %get-tuple-element.143.refs_1_.dk_ref, bf16[1024,768]{1,0:T(8,128)(2,1)} %get-tuple-element.139.refs_2_.dv_ref, bf16[11,768,768]{2,1,0:T(8,128)(2,1)} %all-gather.3.cloned.1.call-done.w_ref.win_ref.wk_ref.wv_ref, ...), custom_call_target="tpu_custom_call" | custom-call | flops 3000000000 | bytes 9000000 | tf_op jit(solution)/shard_map/memory_input/pallas_call | solution.py:788
  248.6 4.9 %first_stage.2 = (bf16[4,2,120,384]{3,2,1,0:T(8,128)(2,1)}, bf16[4,2,120,384]{3,2,1,0:T(8,128)(2,1)}, bf16[2,4,120,384]{3,2,1,0:T(8,128)(2,1)}, bf16[2,4,120,384]{3,2,1,0:T(8,128)(2,1)}) custom-call(s32[3]{0:T(128)} %pad_add_fusion.me_ref, bf16[2,4,2,120,768]{4,3,2,1,0:T(8,128)(2,1)} %get-tuple-element.144.keep_ref, bf16[2,4,2,120,768]{4,3,2,1,0:T(8,128)(2,1)} %copy-done), custom_call_target="tpu_custom_call" | custom-call | flops 1474560 | bytes 8847360 | tf_op jit(solution)/shard_map/first_stage/pallas_call | solution.py:537
  256.2 12.9 %self_back_0.1 = (bf16[1024,768]{1,0:T(8,128)(2,1)}, bf16[1024,768]{1,0:T(8,128)(2,1)}, bf16[1024,768]{1,0:T(8,128)(2,1)}, f32[8,768]{1,0:T(8,128)}) custom-call(f32[1024,768]{1,0:T(8,128)} %get-tuple-element.183.refs_6_.fsg_ref, bf16[1024,768]{1,0:T(8,128)(2,1)} %get-tuple-element.156.q_ref, bf16[1024,768]{1,0:T(8,128)(2,1)} %get-tuple-element.157.k_ref, ...), custom_call_target="tpu_custom_call" | custom-call | flops 24999999488 | bytes 15000000 | tf_op jit(solution)/shard_map/self_back_0/pallas_call | solution.py:692
  270.5 10.8 %collective-permute-done.19.gl_ref = bf16[4,2,120,384]{3,2,1,0:T(8,128)(2,1)S(1)} collective-permute-done((bf16[4,2,120,384]{3,2,1,0:T(8,128)(2,1)}, bf16[4,2,120,384]{3,2,1,0:T(8,128)(2,1)S(1)}, u32[]{:S(2)}, u32[]{:S(2)}) %collective-permute-start.19) | collective-permute-done | bytes 737312 | tf_op jit(solution)/shard_map/ppermute | solution.py:827
  287.8 17.7 %self_last.1 = (bf16[2,4,2,88,768]{4,3,2,1,0:T(8,128)(2,1)}, bf16[2,4,2,88,768]{4,3,2,1,0:T(8,128)(2,1)}, bf16[1024,768]{1,0:T(8,128)(2,1)}, bf16[1024,768]{1,0:T(8,128)(2,1)}, bf16[1024,768]{1,0:T(8,128)(2,1)}) custom-call(s32[1]{0:T(128)} %bitcast.55.me_ref, ...), custom_call_target="tpu_custom_call", output_to_operand_aliasing={{2}: (13, {}), {3}: (14, {}), {4}: (15, {})} | custom-call | flops 24999999488 | bytes 20000000 | tf_op jit(solution)/shard_map/self_last/pallas_call | solution.py:767
  308.9 4.5 %collective-permute-done.23.got_ref = bf16[2,4,2,88,768]{4,3,2,1,0:T(8,128)(2,1)S(1)} collective-permute-done((bf16[2,4,2,88,768]{4,3,2,1,0:T(8,128)(2,1)}, bf16[2,4,2,88,768]{4,3,2,1,0:T(8,128)(2,1)S(1)}, u32[]{:S(2)}, u32[]{:S(2)}) %collective-permute-start.23) | collective-permute-done | bytes 2162720 | tf_op jit(solution)/shard_map/ppermute | solution.py:827
  314.7 4.3 %first_stage.3 = (bf16[4,2,88,384]{3,2,1,0:T(8,128)(2,1)}, bf16[4,2,88,384]{3,2,1,0:T(8,128)(2,1)}, bf16[2,4,88,384]{3,2,1,0:T(8,128)(2,1)}, bf16[2,4,88,384]{3,2,1,0:T(8,128)(2,1)}) custom-call(s32[3]{0:T(128)} %pad_add_fusion.me_ref, bf16[2,4,2,88,768]{4,3,2,1,0:T(8,128)(2,1)} %get-tuple-element.168.keep_ref, bf16[2,4,2,88,768]{4,3,2,1,0:T(8,128)(2,1)} %copy-done.1), custom_call_target="tpu_custom_call" | custom-call | flops 1081344 | bytes 6488064 | tf_op jit(solution)/shard_map/first_stage/pallas_call | solution.py:537
  320.9 8.9 %self_input.1 = f32[1024,768]{1,0:T(8,128)} custom-call(f32[1024,768]{1,0:T(8,128)} %get-tuple-element.183.refs_6_.fsg_ref, bf16[1024,768]{1,0:T(8,128)(2,1)} %get-tuple-element.184.dq_ref, bf16[1024,768]{1,0:T(8,128)(2,1)} %get-tuple-element.185.dk_ref, bf16[1024,768]{1,0:T(8,128)(2,1)} %get-tuple-element.186.dv_ref, bf16[2,768,768]{2,1,0:T(8,128)(2,1)} %bitcast.125, ...), custom_call_target="tpu_custom_call" | custom-call | flops 4000000000 | bytes 14000000 | tf_op jit(solution)/shard_map/self_input/pallas_call | solution.py:802
  345.6 5.7 %collective-permute-done.24.refs_1_ = bf16[120,768]{1,0:T(8,128)(2,1)S(1)} collective-permute-done((bf16[120,768]{1,0:T(8,128)(2,1)S(1)}, bf16[120,768]{1,0:T(8,128)(2,1)S(1)}, u32[]{:S(2)}, u32[]{:S(2)}) %collective-permute-start.24) | collective-permute-done | bytes 184352 | tf_op jit(solution)/shard_map/ppermute | solution.py:858
  351.4 6.8 %collective-permute-done.25.refs_2_ = bf16[120,768]{1,0:T(8,128)(2,1)S(1)} collective-permute-done((bf16[120,768]{1,0:T(8,128)(2,1)S(1)}, bf16[120,768]{1,0:T(8,128)(2,1)S(1)}, u32[]{:S(2)}, u32[]{:S(2)}) %collective-permute-start.25) | collective-permute-done | bytes 184352 | tf_op jit(solution)/shard_map/ppermute | solution.py:858
  371.9 4.4 %collective-permute-done.32.refs_6_ = bf16[88,768]{1,0:T(8,128)(2,1)S(1)} collective-permute-done((bf16[88,768]{1,0:T(8,128)(2,1)}, bf16[88,768]{1,0:T(8,128)(2,1)S(1)}, u32[]{:S(2)}, u32[]{:S(2)}) %collective-permute-start.32) | collective-permute-done | bytes 135200 | tf_op jit(solution)/shard_map/ppermute | solution.py:858
  (216 shorter events, 104.9 us)
Async XLA Ops:
  7.3 117.7 %all-gather.3.cloned.1.call-start = ((), (), s32[]{:S(2)}) async-start(), calls=%async_computation.2 | async-start | bytes 13381632 | tf_op jit(solution)/shard_map/all_gather | solution.py:993
  11.0 357.5 %reduce-scatter.2.cloned.1.call-start = ((), (), s32[]{:S(2)}) async-start(), calls=%async_computation.1 | async-start | bytes 9732096 | tf_op jit(solution)/shard_map/reduce_scatter | solution.py:882
  11.5 13.6 %collective-permute-start.1 = (bf16[1,80,768]{2,1,0:T(8,128)(2,1)S(1)}, bf16[1,80,768]{2,1,0:T(8,128)(2,1)S(1)}, u32[]{:S(2)}, u32[]{:S(2)}) collective-permute-start(bf16[1,80,768]{2,1,0:T(8,128)(2,1)S(1)} %fusion.10), channel_id=1, source_target_pairs={{0,4},{2,6},{4,0},{6,2},{1,5},{3,7},{5,1},{7,3},{8,12},{10,14},{12... | collective-permute-start | bytes 368648 | tf_op jit(solution)/shard_map/ppermute | solution.py:933
  37.4 19.6 %collective-permute-start.10 = (bf16[1,2,4,32,768]{4,2,3,1,0:T(4,128)(2,1)S(1)}, bf16[1,2,4,32,768]{4,2,3,1,0:T(4,128)(2,1)S(1)}, u32[]{:S(2)}, u32[]{:S(2)}) collective-permute-start(bf16[1,2,4,32,768]{4,2,3,1,0:T(4,128)(2,1)S(1)} %pad_maximum_fusion.8), channel_id=1, source_target_pairs={{0,1},{1,0},{2,3},{3,2},{4,5},{5,4},{6,7},{7,6},{8,9},{9,8},{10,11... | collective-permute-start | bytes 1179656 | tf_op jit(solution)/shard_map/ppermute | solution.py:939
  40.8 23.3 %collective-permute-start.8 = (bf16[2,4,2,24,768]{4,3,2,1,0:T(8,128)(2,1)S(1)}, bf16[2,4,2,24,768]{4,3,2,1,0:T(8,128)(2,1)S(1)}, u32[]{:S(2)}, u32[]{:S(2)}) collective-permute-start(bf16[2,4,2,24,768]{4,3,2,1,0:T(8,128)(2,1)S(1)} %pad_maximum_fusion.3), channel_id=1, source_target_pairs={{0,16},{16,0},{1,17},{17,1},{2,18},{18,2},{3,19},{19,3},{4,20},{20... | collective-permute-start | bytes 1769480 | tf_op jit(solution)/shard_map/ppermute | solution.py:939
  41.4 24.7 %collective-permute-start.7 = (bf16[2,24,768]{2,1,0:T(8,128)(2,1)S(1)}, bf16[2,24,768]{2,1,0:T(8,128)(2,1)S(1)}, u32[]{:S(2)}, u32[]{:S(2)}) collective-permute-start(bf16[2,24,768]{2,1,0:T(8,128)(2,1)S(1)} %copy-done.17), channel_id=1, source_target_pairs={{0,2},{2,4},{4,6},{6,0},{1,3},{3,5},{5,7},{7,1},{8,10},{10,12},{12... | collective-permute-start | bytes 221192 | tf_op jit(solution)/shard_map/ppermute | solution.py:933
  48.7 17.4 %collective-permute-start.6 = (bf16[2,24,768]{2,1,0:T(8,128)(2,1)S(1)}, bf16[2,24,768]{2,1,0:T(8,128)(2,1)S(1)}, u32[]{:S(2)}, u32[]{:S(2)}) collective-permute-start(bf16[2,24,768]{2,1,0:T(8,128)(2,1)S(1)} %copy-done.17), channel_id=1, source_target_pairs={{0,4},{2,6},{4,0},{6,2},{1,5},{3,7},{5,1},{7,3},{8,12},{10,14},{12... | collective-permute-start | bytes 221192 | tf_op jit(solution)/shard_map/ppermute | solution.py:933
  53.9 12.2 %collective-permute-start.5 = (bf16[2,24,768]{2,1,0:T(8,128)(2,1)S(1)}, bf16[2,24,768]{2,1,0:T(8,128)(2,1)}, u32[]{:S(2)}, u32[]{:S(2)}) collective-permute-start(bf16[2,24,768]{2,1,0:T(8,128)(2,1)S(1)} %copy-done.17), channel_id=1, source_target_pairs={{0,6},{2,0},{4,2},{6,4},{1,7},{3,1},{5,3},{7,5},{8,14},{10,8},{12,... | collective-permute-start | bytes 221192 | tf_op jit(solution)/shard_map/ppermute | solution.py:933
  88.5 9.7 %collective-permute-start.15 = (bf16[1,4,24,768]{3,2,1,0:T(8,128)(2,1)S(1)}, bf16[1,4,24,768]{3,2,1,0:T(8,128)(2,1)S(1)}, u32[]{:S(2)}, u32[]{:S(2)}) collective-permute-start(bf16[1,4,24,768]{3,2,1,0:T(8,128)(2,1)S(1)} %bitcast.131), channel_id=1, source_target_pairs={{0,16},{16,0},{1,17},{17,1},{2,18},{18,2},{3,19},{19,3},{4,20},{20... | collective-permute-start | bytes 442376 | tf_op jit(solution)/shard_map/ppermute | solution.py:939
  98.3 14.9 %collective-permute-start.16 = (bf16[1,2,4,24,768]{4,3,2,1,0:T(8,128)(2,1)S(1)}, bf16[1,2,4,24,768]{4,3,2,1,0:T(8,128)(2,1)S(1)}, u32[]{:S(2)}, u32[]{:S(2)}) collective-permute-start(bf16[1,2,4,24,768]{4,3,2,1,0:T(8,128)(2,1)S(1)} %pad_maximum_fusion.11), channel_id=1, source_target_pairs={{0,1},{1,0},{2,3},{3,2},{4,5},{5,4},{6,7},{7,6},{8,9},{9,8},{10,11... | collective-permute-start | bytes 884744 | tf_op jit(solution)/shard_map/ppermute | solution.py:939
  98.8 14.7 %collective-permute-start.13 = (bf16[1,4,2,24,768]{4,3,1,2,0:T(8,128)(2,1)S(1)}, bf16[1,4,2,24,768]{4,3,1,2,0:T(8,128)(2,1)S(1)}, u32[]{:S(2)}, u32[]{:S(2)}) collective-permute-start(bf16[1,4,2,24,768]{4,3,1,2,0:T(8,128)(2,1)S(1)} %pad_maximum_fusion.10), channel_id=1, source_target_pairs={{0,16},{16,0},{1,17},{17,1},{2,18},{18,2},{3,19},{19,3},{4,20},{20... | collective-permute-start | bytes 884744 | tf_op jit(solution)/shard_map/ppermute | solution.py:939
  253.4 27.9 %collective-permute-start.19 = (bf16[4,2,120,384]{3,2,1,0:T(8,128)(2,1)}, bf16[4,2,120,384]{3,2,1,0:T(8,128)(2,1)S(1)}, u32[]{:S(2)}, u32[]{:S(2)}) collective-permute-start(bf16[4,2,120,384]{3,2,1,0:T(8,128)(2,1)} %get-tuple-element.150), channel_id=1, source_target_pairs={{0,16},{16,0},{1,17},{17,1},{2,18},{18,2},{3,19},{19,3},{4,20},{20... | collective-permute-start | bytes 2211848 | tf_op jit(solution)/shard_map/ppermute | solution.py:827
  255.5 25.9 %collective-permute-start.20 = (bf16[2,4,120,384]{3,2,1,0:T(8,128)(2,1)}, bf16[2,4,120,384]{3,2,1,0:T(8,128)(2,1)S(1)}, u32[]{:S(2)}, u32[]{:S(2)}) collective-permute-start(bf16[2,4,120,384]{3,2,1,0:T(8,128)(2,1)} %get-tuple-element.152), channel_id=1, source_target_pairs={{0,1},{1,0},{2,3},{3,2},{4,5},{5,4},{6,7},{7,6},{8,9},{9,8},{10,11... | collective-permute-start | bytes 2211848 | tf_op jit(solution)/shard_map/ppermute | solution.py:827
  285.6 19.9 %collective-permute-start.21 = (bf16[4,120,384]{2,1,0:T(8,128)(2,1)}, bf16[4,120,384]{2,1,0:T(8,128)(2,1)S(1)}, u32[]{:S(2)}, u32[]{:S(2)}) collective-permute-start(bf16[4,120,384]{2,1,0:T(8,128)(2,1)} %get-tuple-element.171), channel_id=1, source_target_pairs={{0,1},{1,0},{2,3},{3,2},{4,5},{5,4},{6,7},{7,6},{8,9},{9,8},{10,11... | collective-permute-start | bytes 1105928 | tf_op jit(solution)/shard_map/ppermute | solution.py:827
  286.3 19.3 %collective-permute-start.22 = (bf16[4,120,384]{2,1,0:T(8,128)(2,1)}, bf16[4,120,384]{2,1,0:T(8,128)(2,1)S(1)}, u32[]{:S(2)}, u32[]{:S(2)}) collective-permute-start(bf16[4,120,384]{2,1,0:T(8,128)(2,1)} %get-tuple-element.173), channel_id=1, source_target_pairs={{0,16},{16,0},{1,17},{17,1},{2,18},{18,2},{3,19},{19,3},{4,20},{20... | collective-permute-start | bytes 1105928 | tf_op jit(solution)/shard_map/ppermute | solution.py:827
  319.0 14.5 %collective-permute-start.27 = (bf16[4,2,88,384]{3,2,1,0:T(8,128)(2,1)}, bf16[4,2,88,384]{3,2,1,0:T(8,128)(2,1)S(1)}, u32[]{:S(2)}, u32[]{:S(2)}) collective-permute-start(bf16[4,2,88,384]{3,2,1,0:T(8,128)(2,1)} %get-tuple-element.195), channel_id=1, source_target_pairs={{0,16},{16,0},{1,17},{17,1},{2,18},{18,2},{3,19},{19,3},{4,20},{20... | collective-permute-start | bytes 1622024 | tf_op jit(solution)/shard_map/ppermute | solution.py:827
  319.6 14.2 %collective-permute-start.28 = (bf16[2,4,88,384]{3,2,1,0:T(8,128)(2,1)}, bf16[2,4,88,384]{3,2,1,0:T(8,128)(2,1)S(1)}, u32[]{:S(2)}, u32[]{:S(2)}) collective-permute-start(bf16[2,4,88,384]{3,2,1,0:T(8,128)(2,1)} %get-tuple-element.197), channel_id=1, source_target_pairs={{0,1},{1,0},{2,3},{3,2},{4,5},{5,4},{6,7},{7,6},{8,9},{9,8},{10,11... | collective-permute-start | bytes 1622024 | tf_op jit(solution)/shard_map/ppermute | solution.py:827
  337.8 20.4 %collective-permute-start.29 = (bf16[4,88,384]{2,1,0:T(8,128)(2,1)}, bf16[4,88,384]{2,1,0:T(8,128)(2,1)S(1)}, u32[]{:S(2)}, u32[]{:S(2)}) collective-permute-start(bf16[4,88,384]{2,1,0:T(8,128)(2,1)} %get-tuple-element.201), channel_id=1, source_target_pairs={{0,1},{1,0},{2,3},{3,2},{4,5},{5,4},{6,7},{7,6},{8,9},{9,8},{10,11... | collective-permute-start | bytes 811016 | tf_op jit(solution)/shard_map/ppermute | solution.py:827
  339.1 19.2 %collective-permute-start.30 = (bf16[4,88,384]{2,1,0:T(8,128)(2,1)}, bf16[4,88,384]{2,1,0:T(8,128)(2,1)S(1)}, u32[]{:S(2)}, u32[]{:S(2)}) collective-permute-start(bf16[4,88,384]{2,1,0:T(8,128)(2,1)} %get-tuple-element.203), channel_id=1, source_target_pairs={{0,16},{16,0},{1,17},{17,1},{2,18},{18,2},{3,19},{19,3},{4,20},{20... | collective-permute-start | bytes 811016 | tf_op jit(solution)/shard_map/ppermute | solution.py:827
  340.1 11.3 %collective-permute-start.24 = (bf16[120,768]{1,0:T(8,128)(2,1)S(1)}, bf16[120,768]{1,0:T(8,128)(2,1)S(1)}, u32[]{:S(2)}, u32[]{:S(2)}) collective-permute-start(bf16[120,768]{1,0:T(8,128)(2,1)S(1)} %copy-done.28), channel_id=1, source_target_pairs={{0,2},{2,4},{4,6},{6,0},{1,3},{3,5},{5,7},{7,1},{8,10},{10,12},{12... | collective-permute-start | bytes 552968 | tf_op jit(solution)/shard_map/ppermute | solution.py:858
  341.8 16.5 %collective-permute-start.25 = (bf16[120,768]{1,0:T(8,128)(2,1)S(1)}, bf16[120,768]{1,0:T(8,128)(2,1)S(1)}, u32[]{:S(2)}, u32[]{:S(2)}) collective-permute-start(bf16[120,768]{1,0:T(8,128)(2,1)S(1)} %copy-done.27), channel_id=1, source_target_pairs={{0,4},{2,6},{4,0},{6,2},{1,5},{3,7},{5,1},{7,3},{8,12},{10,14},{12... | collective-permute-start | bytes 552968 | tf_op jit(solution)/shard_map/ppermute | solution.py:858
  344.1 14.2 %collective-permute-start.26 = (bf16[120,768]{1,0:T(8,128)(2,1)S(1)}, bf16[120,768]{1,0:T(8,128)(2,1)S(1)}, u32[]{:S(2)}, u32[]{:S(2)}) collective-permute-start(bf16[120,768]{1,0:T(8,128)(2,1)S(1)} %copy-done.26), channel_id=1, source_target_pairs={{0,6},{2,0},{4,2},{6,4},{1,7},{3,1},{5,3},{7,5},{8,14},{10,8},{12,... | collective-permute-start | bytes 552968 | tf_op jit(solution)/shard_map/ppermute | solution.py:858
  361.9 10.1 %collective-permute-start.31 = (bf16[88,768]{1,0:T(8,128)(2,1)}, bf16[88,768]{1,0:T(8,128)(2,1)S(1)}, u32[]{:S(2)}, u32[]{:S(2)}) collective-permute-start(bf16[88,768]{1,0:T(8,128)(2,1)} %get-tuple-element.205), channel_id=1, source_target_pairs={{0,2},{2,4},{4,6},{6,0},{1,3},{3,5},{5,7},{7,1},{8,10},{10,12},{12... | collective-permute-start | bytes 405512 | tf_op jit(solution)/shard_map/ppermute | solution.py:858
  366.1 10.3 %collective-permute-start.32 = (bf16[88,768]{1,0:T(8,128)(2,1)}, bf16[88,768]{1,0:T(8,128)(2,1)S(1)}, u32[]{:S(2)}, u32[]{:S(2)}) collective-permute-start(bf16[88,768]{1,0:T(8,128)(2,1)} %get-tuple-element.206), channel_id=1, source_target_pairs={{0,4},{2,6},{4,0},{6,2},{1,5},{3,7},{5,1},{7,3},{8,12},{10,14},{12... | collective-permute-start | bytes 405512 | tf_op jit(solution)/shard_map/ppermute | solution.py:858
  (43 other events, 297.1 us)
Sparse Core Ops, SparseCore 0:
  11.5 113.3 all-gather.2
  196.0 160.2 reduce-scatter.1
